TPU v7x, 256 devices: a whole 4x4x8 slice. The times are simulated.
256 devices in a mesh: stream: 8 (over y_lo, x), radial: 8 (over z), span: 4 (over y_hi, core).
Axes of the slice: x: 4, y: 4 (y_hi: 2, y_lo: 2; y = y_hi * 2 + y_lo), z: 8, core: 2. Of those that a mesh axis runs over, the one named last changes fastest.
Arguments:
- log_conformation: float32 [6, 128, 64, 1024], P(None, 'radial', 'span', 'stream'), may hold values from -1 to 1
- velocity: float32 [3, 128, 64, 1024], P(None, 'radial', 'span', 'stream'), may hold values from -0.25 to 0.25
Outputs:
- next_conformation: float32 [6, 128, 64, 1024], P(None, 'radial', 'span', 'stream')
- pressure_modes: float32 [128, 64, 1024], P('radial', 'span', 'stream')
All inputs are finite; a program needn't handle non-finite values.
Results may differ from a plain program's by a relative error of at most 0.0003.
Values sent between devices are 32-bit elements; how exact they have to be, the bound alone decides.
No kernel may reach another device: no remote copies, remote signals or barrier semaphores. Data moves between devices by JAX's collectives and lax.ppermute only.
A program may use at most 64 MiB of HBM per device.

v0:
```python
import math

import jax
import jax.numpy as jnp
from jax import lax
from jax.sharding import PartitionSpec as P

NX = 1024


WEISSENBERG = 20.0
EXTENSIBILITY = 100.0
TIME_STEP = 2.0
EPSILON = 1e-06
SLOTS = ((0, 1, 2), (1, 3, 4), (2, 4, 5))
PAIRS = ((0, 0), (0, 1), (0, 2), (1, 1), (1, 2), (2, 2))
DIAGONAL = (0, 3, 5)
AXES = (2, 0, 1)
COSINES = tuple((math.cos((2 * number + 1) * math.pi / 12.0) for number in range(6)))


def padded_2(block, sides, width, periodic):
    for axis, dim in sides:
        count = lax.axis_size(axis)
        forward = [(i, i + 1) for i in range(count - 1)]
        if periodic:
            forward.append((count - 1, 0))
        backward = [(target, source) for source, target in forward]
        low = lax.ppermute(
            lax.slice_in_dim(block, block.shape[dim] - width, None, axis=dim), axis, forward
        )
        high = lax.ppermute(lax.slice_in_dim(block, 0, width, axis=dim), axis, backward)
        block = jnp.concatenate([low, block, high], axis=dim)
    return block


def weno_blend(a, b, c, d, e):
    first = a / 3.0 - 7.0 * b / 6.0 + 11.0 * c / 6.0
    second = -b / 6.0 + 5.0 * c / 6.0 + d / 3.0
    third = c / 3.0 + 5.0 * d / 6.0 - e / 6.0
    rough_left = 13.0 / 12.0 * (a - 2.0 * b + c) ** 2 + 0.25 * (a - 4.0 * b + 3.0 * c) ** 2
    rough_middle = 13.0 / 12.0 * (b - 2.0 * c + d) ** 2 + 0.25 * (b - d) ** 2
    rough_right = 13.0 / 12.0 * (c - 2.0 * d + e) ** 2 + 0.25 * (3.0 * c - 4.0 * d + e) ** 2
    weight_left = 0.1 / (EPSILON + rough_left) ** 2
    weight_middle = 0.6 / (EPSILON + rough_middle) ** 2
    weight_right = 0.3 / (EPSILON + rough_right) ** 2
    return (weight_left * first + weight_middle * second + weight_right * third) / (
        weight_left + weight_middle + weight_right
    )


def upwind(padded, speeds, spatial):
    extent = speeds.shape[spatial]
    differences = jnp.diff(padded, axis=spatial)
    pieces = [
        lax.slice_in_dim(differences, offset, offset + extent, axis=spatial) for offset in range(6)
    ]
    behind = weno_blend(pieces[0], pieces[1], pieces[2], pieces[3], pieces[4])
    forward = weno_blend(pieces[5], pieces[4], pieces[3], pieces[2], pieces[1])
    return jnp.where(speeds > 0, behind, forward)


def sym_product(left, right):
    output = []
    for upper_index, lower_index in PAIRS:
        running = left[SLOTS[upper_index][0]] * right[SLOTS[0][lower_index]]
        running = running + left[SLOTS[upper_index][1]] * right[SLOTS[1][lower_index]]
        running = running + left[SLOTS[upper_index][2]] * right[SLOTS[2][lower_index]]
        output.append(running)
    return output


def sym_exp(members, signed):
    scaled = [signed * 0.125 * member for member in members]
    identity = [
        jnp.ones_like(members[0]) if position in DIAGONAL else jnp.zeros_like(members[0])
        for position in range(6)
    ]
    series = identity
    for degree in range(6, 0, -1):
        product = sym_product(scaled, series)
        series = [identity[position] + product[position] / degree for position in range(6)]
    for repeat in range(3):
        series = sym_product(series, series)
    return series


def conform(grown):
    trace_sum = grown[0] + grown[3] + grown[5]
    peterlin = (EXTENSIBILITY - 3.0) / (EXTENSIBILITY - trace_sum)
    stress = [
        peterlin * grown[position] - 1.0 if position in DIAGONAL else peterlin * grown[position]
        for position in range(6)
    ]
    return (peterlin, stress)


def relaxation(shrunk, peterlin):
    return [
        shrunk[position] - peterlin if position in DIAGONAL else shrunk[position]
        for position in range(6)
    ]


def central(quantity, spatial):
    extent = quantity.shape[spatial]
    return 0.5 * (
        lax.slice_in_dim(quantity, 2, extent, axis=spatial)
        - lax.slice_in_dim(quantity, 0, extent - 2, axis=spatial)
    )


def shaved(quantity, spatial):
    extent = quantity.shape[spatial]
    return lax.slice_in_dim(quantity, 1, extent - 1, axis=spatial)


def flux_sum(columns):
    running = None
    for direction in range(3):
        contrib = central(columns[direction], AXES[direction])
        for another in range(3):
            if another != direction:
                contrib = shaved(contrib, AXES[another])
        running = contrib if running is None else running + contrib
    return running


def pressure_source(padded_stress):
    forcing = [
        flux_sum([padded_stress[SLOTS[row_dir][col_dir]] for col_dir in range(3)])
        for row_dir in range(3)
    ]
    return flux_sum(forcing)


def mode_weights(ordinal, period):
    midpoint = period // 2
    wavenumber = jnp.where(ordinal <= midpoint, ordinal, ordinal - midpoint)
    squared_wave = 4.0 * jnp.sin(math.pi * wavenumber.astype(jnp.float32) / period) ** 2
    diagonal = 4.0 + squared_wave
    ratio_term = 4.0 / diagonal
    upper_end = 1.0 + ratio_term
    lower_end = jnp.maximum(0.3, 1.0 - ratio_term)
    centre = 0.5 * (upper_end + lower_end)
    spread = 0.5 * (upper_end - lower_end)
    return (diagonal, [1.0 / (centre + spread * cosine) for cosine in COSINES])


def relax(padded, source, diagonal, weighting):
    middle = padded[1:-1, 1:-1]
    beside_all = padded[2:, 1:-1] + padded[:-2, 1:-1] + (padded[1:-1, 2:] + padded[1:-1, :-2])
    return middle + weighting * (source - (diagonal * middle - beside_all)) / diagonal


def fourier_table(period):
    ordinal = jnp.arange(period, dtype=jnp.int32)
    midpoint = period // 2
    wavenumber = jnp.where(ordinal <= midpoint, ordinal, ordinal - midpoint)
    phases = wavenumber[:, None] * ordinal[None, :] % period
    angles = 2.0 * math.pi / period * phases.astype(jnp.float32)
    return jnp.where((ordinal <= midpoint)[:, None], jnp.cos(angles), jnp.sin(angles)) * period ** (
        -0.5
    )


def shards(log_conformation, velocity):
    extent = log_conformation.shape[3]
    members = [log_conformation[position] for position in range(6)]
    stream_ext = padded_2(log_conformation, (("stream", 3),), 3, True)
    cross_ext = padded_2(log_conformation, (("radial", 1), ("span", 2)), 3, False)
    line_radial = cross_ext[:, :, 3:-3, :]
    line_span = cross_ext[:, 3:-3, :, :]
    peterlin, stress = conform(sym_exp(members, 1.0))
    stress_stream = padded_2(jnp.stack(stress), (("stream", 3),), 2, True)
    stress_box = padded_2(stress_stream, (("radial", 1), ("span", 2)), 2, False)
    padded_stress = [stress_box[position] for position in range(6)]
    shrunk = sym_exp(members, -1.0)
    speeds = [velocity[position][None] for position in range(3)]
    slope_stream = upwind(stream_ext, speeds[0], 3)
    slope_radial = upwind(line_radial, speeds[1], 1)
    slope_span = upwind(line_span, speeds[2], 2)
    advection = speeds[0] * slope_stream + speeds[1] * slope_radial + speeds[2] * slope_span
    next_conformation = (
        log_conformation
        - TIME_STEP * advection
        + TIME_STEP / WEISSENBERG * jnp.stack(relaxation(shrunk, peterlin))
    )
    source_field = pressure_source(padded_stress)
    fourier = fourier_table(NX)
    spectrum = jnp.einsum(
        "rsx,mx->rsm",
        lax.all_to_all(source_field, "stream", split_axis=0, concat_axis=2, tiled=True),
        fourier,
        precision=lax.Precision.HIGHEST,
        preferred_element_type=jnp.float32,
    )
    mode_slab = lax.all_to_all(spectrum, "stream", split_axis=2, concat_axis=0, tiled=True)
    source = -mode_slab
    ordinal = lax.axis_index("stream") * extent + jnp.arange(extent, dtype=jnp.int32)
    diagonal, omegas = mode_weights(ordinal, NX)
    solution = omegas[0] * source / diagonal
    for number in range(1, 6):
        padded = padded_2(solution, (("radial", 0), ("span", 1)), 1, False)
        solution = relax(padded, source, diagonal, omegas[number])
    return (next_conformation, solution)


def solution(mesh):
    return jax.shard_map(
        shards,
        mesh=mesh,
        in_specs=(P(None, "radial", "span", "stream"), P(None, "radial", "span", "stream")),
        out_specs=(P(None, "radial", "span", "stream"), P("radial", "span", "stream")),
        check_vma=False,
    )
```

profile of v0, /device:TPU:129, one launch (start us, length us, event | category | flops | bytes accessed | tf_op | source)
XLA Modules:
  0.0 233.9 jit_solution(17611630736523527142)
XLA Ops:
  6.5 3.5 %collective-permute-start.1 = (f32[6,16,16,3]{2,1,3,0:T(8,128)}, f32[6,16,16,3]{2,1,3,0:T(8,128)}, u32[]{:S(2)}, u32[]{:S(2)}) collective-permute-start(f32[6,16,16,3]{2,1,3,0:T(8,128)} %copy.65), channel_id=1, source_target_pairs={{32,0},{64,32},{96,64},{128,96},{160,128},{192,160},{224,192},{0,2... | collective-permute-start | bytes 55304 | tf_op jit(solution)/shard_map/ppermute | solution.py:32
  17.6 2.4 %copy.51 = f32[6,16,16,2]{2,1,3,0:T(8,128)} copy(f32[6,16,16,2]{3,1,2,0:T(8,128)} %get-tuple-element.70) | data formatting | bytes 24576 | tf_op jit(solution)/shard_map/slice | solution.py:32
  20.0 3.6 %collective-permute-start.7 = (f32[6,16,16,2]{2,1,3,0:T(8,128)}, f32[6,16,16,2]{2,1,3,0:T(8,128)}, u32[]{:S(2)}, u32[]{:S(2)}) collective-permute-start(f32[6,16,16,2]{2,1,3,0:T(8,128)} %copy.51), channel_id=1, source_target_pairs={{32,0},{64,32},{96,64},{128,96},{160,128},{192,160},{224,192},{0,2... | collective-permute-start | bytes 36872 | tf_op jit(solution)/shard_map/ppermute | solution.py:32
  26.0 19.1 %fusion.139 = f32[1024,1024,1]{1,0,2:T(8,128)} fusion(s32[1024]{0:T(1024)S(1)} %add_select_fusion.1, pred[1024]{0:T(1024)(128)(4,1)S(1)} %iota_compare_fusion), kind=kLoop, calls=%fused_computation.7.clone.1 | loop fusion | flops 16777216 | bytes 4199424 | tf_op jit(solution)/shard_map/rsx,mx->rsm/dot_general | solution.py:191
  47.4 2.4 %copy.52 = f32[6,16,16,2]{3,1,2,0:T(8,128)} copy(f32[6,16,16,2]{2,1,3,0:T(8,128)} %collective-permute-done.6) | data formatting | bytes 24576 | tf_op jit(solution)/shard_map/ppermute | solution.py:29
  55.0 3.4 %collective-permute-start.8 = (f32[6,2,16,132]{3,2,1,0:T(8,128)}, f32[6,2,16,132]{3,2,1,0:T(8,128)}, u32[]{:S(2)}, u32[]{:S(2)}) collective-permute-start(f32[6,2,16,132]{3,2,1,0:T(8,128)} %copy.54), channel_id=1, source_target_pairs={{0,4},{4,8},{8,12},{12,16},{16,20},{20,24},{24,28},{1,5},{5,9},{9,... | collective-permute-start | bytes 304136 | tf_op jit(solution)/shard_map/ppermute | solution.py:29
  60.2 2.8 %collective-permute-done.8 = f32[6,2,16,132]{3,2,1,0:T(8,128)} collective-permute-done((f32[6,2,16,132]{3,2,1,0:T(8,128)}, f32[6,2,16,132]{3,2,1,0:T(8,128)}, u32[]{:S(2)}, u32[]{:S(2)}) %collective-permute-start.8) | collective-permute-done | bytes 101408 | tf_op jit(solution)/shard_map/ppermute | solution.py:29
  65.3 4.8 %collective-permute-start.11 = (f32[6,20,2,132]{3,1,2,0:T(8,128)S(1)}, f32[6,20,2,132]{3,1,2,0:T(8,128)S(1)}, u32[]{:S(2)}, u32[]{:S(2)}) collective-permute-start(f32[6,20,2,132]{3,1,2,0:T(8,128)S(1)} %get-tuple-element.62), channel_id=1, source_target_pairs={{1,0},{2,1},{3,2},{5,4},{6,5},{7,6},{9,8},{10,9},{11,10},{13,12},{... | collective-permute-start | bytes 380168 | tf_op jit(solution)/shard_map/ppermute | solution.py:32
  70.1 4.4 %collective-permute-start.10 = (f32[6,20,2,132]{3,1,2,0:T(8,128)S(1)}, f32[6,20,2,132]{3,1,2,0:T(8,128)S(1)}, u32[]{:S(2)}, u32[]{:S(2)}) collective-permute-start(f32[6,20,2,132]{3,1,2,0:T(8,128)S(1)} %get-tuple-element.61), channel_id=1, source_target_pairs={{0,1},{1,2},{2,3},{4,5},{5,6},{6,7},{8,9},{9,10},{10,11},{12,13},{... | collective-permute-start | bytes 380168 | tf_op jit(solution)/shard_map/ppermute | solution.py:29
  82.9 4.5 %all-to-all-start = ((f32[16,16,128]{2,1,0:T(8,128)}), f32[16,16,128]{2,1,0:T(8,128)S(1)}, u32[]{:S(2)}, u32[]{:S(2)}) async-start(f32[16,16,128]{2,1,0:T(8,128)} %copy.58), calls=%async_computation | async-start | bytes 262144 | tf_op jit(solution)/shard_map/all_to_all | solution.py:193
  88.6 4.2 %all-to-all-done = f32[16,16,128]{2,1,0:T(8,128)S(1)} async-done(((f32[16,16,128]{2,1,0:T(8,128)}), f32[16,16,128]{2,1,0:T(8,128)S(1)}, u32[]{:S(2)}, u32[]{:S(2)}) %all-to-all-start) | async-done | bytes 131104 | tf_op jit(solution)/shard_map/all_to_all | solution.py:193
  92.9 6.0 %fusion.3 = f32[2,16,1024]{2,1,0:T(8,128)S(1)} fusion(f32[2,16,1024]{2,1,0:T(8,128)S(1)} %all_to_all.23, f32[1024,1024,1]{1,0,2:T(8,128)} %fusion.139), kind=kOutput, calls=%fused_computation.6 | convolution fusion | flops 402653184 | bytes 4456448 | tf_op jit(solution)/shard_map/rsx,mx->rsm/dot_general | solution.py:191
  101.6 3.4 %all-to-all-start.1 = ((f32[8,1,4096]{2,1,0:T(1,128)}), f32[8,1,4096]{2,1,0:T(1,128)S(1)}, u32[]{:S(2)}, u32[]{:S(2)}) async-start(f32[8,1,4096]{2,1,0:T(1,128)} %reshape.83), calls=%async_computation.1 | async-start | bytes 262144 | tf_op jit(solution)/shard_map/all_to_all | solution.py:198
  105.7 4.6 %all-to-all-done.1 = f32[8,1,4096]{2,1,0:T(1,128)S(1)} async-done(((f32[8,1,4096]{2,1,0:T(1,128)}), f32[8,1,4096]{2,1,0:T(1,128)S(1)}, u32[]{:S(2)}, u32[]{:S(2)}) %all-to-all-start.1) | async-done | bytes 131104 | tf_op jit(solution)/shard_map/all_to_all | solution.py:198
  117.9 3.4 %collective-permute-start.13 = (f32[1,16,128]{2,1,0:T(8,128)S(1)}, f32[1,16,128]{2,1,0:T(8,128)S(1)}, u32[]{:S(2)}, u32[]{:S(2)}) collective-permute-start(f32[1,16,128]{2,1,0:T(8,128)S(1)} %get-tuple-element.128), channel_id=1, source_target_pairs={{0,4},{4,8},{8,12},{12,16},{16,20},{20,24},{24,28},{1,5},{5,9},{9,... | collective-permute-start | bytes 24584 | tf_op jit(solution)/shard_map/ppermute | solution.py:29
  124.1 10.2 %collective-permute-start.15 = (f32[18,1,128]{2,1,0:T(1,128)}, f32[18,1,128]{2,1,0:T(1,128)}, u32[]{:S(2)}, u32[]{:S(2)}) collective-permute-start(f32[18,1,128]{2,1,0:T(1,128)} %get-tuple-element.119), channel_id=1, source_target_pairs={{0,1},{1,2},{2,3},{4,5},{5,6},{6,7},{8,9},{9,10},{10,11},{12,13},{... | collective-permute-start | bytes 27656 | tf_op jit(solution)/shard_map/ppermute | solution.py:29
  137.5 2.4 %collective-permute-start.2 = (f32[6,3,16,128]{3,1,2,0:T(4,128)}, f32[6,3,16,128]{3,1,2,0:T(4,128)}, u32[]{:S(2)}, u32[]{:S(2)}) collective-permute-start(f32[6,3,16,128]{3,1,2,0:T(4,128)} %get-tuple-element.73), channel_id=1, source_target_pairs={{0,4},{4,8},{8,12},{12,16},{16,20},{20,24},{24,28},{1,5},{5,9},{9,... | collective-permute-start | bytes 442376 | tf_op jit(solution)/shard_map/ppermute | solution.py:29
  144.5 4.1 %collective-permute-start.16 = (f32[1,16,128]{2,1,0:T(8,128)S(1)}, f32[1,16,128]{2,1,0:T(8,128)S(1)}, u32[]{:S(2)}, u32[]{:S(2)}) collective-permute-start(f32[1,16,128]{2,1,0:T(8,128)S(1)} %get-tuple-element.127), channel_id=1, source_target_pairs={{4,0},{8,4},{12,8},{16,12},{20,16},{24,20},{28,24},{5,1},{9,5},{13... | collective-permute-start | bytes 24584 | tf_op jit(solution)/shard_map/ppermute | solution.py:32
  151.2 3.0 %collective-permute-done.17 = f32[1,16,128]{2,1,0:T(8,128)S(1)} collective-permute-done((f32[1,16,128]{2,1,0:T(8,128)S(1)}, f32[1,16,128]{2,1,0:T(8,128)S(1)}, u32[]{:S(2)}, u32[]{:S(2)}) %collective-permute-start.17) | collective-permute-done | bytes 8224 | tf_op jit(solution)/shard_map/ppermute | solution.py:29
  154.2 6.9 %collective-permute-start.19 = (f32[18,1,128]{2,1,0:T(1,128)S(1)}, f32[18,1,128]{2,1,0:T(1,128)S(1)}, u32[]{:S(2)}, u32[]{:S(2)}) collective-permute-start(f32[18,1,128]{2,1,0:T(1,128)S(1)} %get-tuple-element.117), channel_id=1, source_target_pairs={{0,1},{1,2},{2,3},{4,5},{5,6},{6,7},{8,9},{9,10},{10,11},{12,13},{... | collective-permute-start | bytes 27656 | tf_op jit(solution)/shard_map/ppermute | solution.py:29
  163.5 4.1 %collective-permute-done.18 = f32[18,1,128]{2,1,0:T(1,128)S(1)} collective-permute-done((f32[18,1,128]{2,1,0:T(1,128)S(1)}, f32[18,1,128]{2,1,0:T(1,128)S(1)}, u32[]{:S(2)}, u32[]{:S(2)}) %collective-permute-start.18) | collective-permute-done | bytes 9248 | tf_op jit(solution)/shard_map/ppermute | solution.py:32
  169.5 3.4 %collective-permute-start.21 = (f32[1,16,128]{2,1,0:T(8,128)S(1)}, f32[1,16,128]{2,1,0:T(8,128)S(1)}, u32[]{:S(2)}, u32[]{:S(2)}) collective-permute-start(f32[1,16,128]{2,1,0:T(8,128)S(1)} %get-tuple-element.124), channel_id=1, source_target_pairs={{0,4},{4,8},{8,12},{12,16},{16,20},{20,24},{24,28},{1,5},{5,9},{9,... | collective-permute-start | bytes 24584 | tf_op jit(solution)/shard_map/ppermute | solution.py:29
  175.7 5.1 %collective-permute-start.4 = (f32[6,22,3,128]{3,1,2,0:T(8,128)S(1)}, f32[6,22,3,128]{3,1,2,0:T(8,128)S(1)}, u32[]{:S(2)}, u32[]{:S(2)}) collective-permute-start(f32[6,22,3,128]{3,1,2,0:T(8,128)S(1)} %get-tuple-element.65), channel_id=1, source_target_pairs={{0,1},{1,2},{2,3},{4,5},{5,6},{6,7},{8,9},{9,10},{10,11},{12,13},{... | collective-permute-start | bytes 608264 | tf_op jit(solution)/shard_map/ppermute | solution.py:29
  182.9 2.4 %collective-permute-start.22 = (f32[18,1,128]{2,1,0:T(1,128)S(1)}, f32[18,1,128]{2,1,0:T(1,128)S(1)}, u32[]{:S(2)}, u32[]{:S(2)}) collective-permute-start(f32[18,1,128]{2,1,0:T(1,128)S(1)} %get-tuple-element.114), channel_id=1, source_target_pairs={{1,0},{2,1},{3,2},{5,4},{6,5},{7,6},{9,8},{10,9},{11,10},{13,12},{... | collective-permute-start | bytes 27656 | tf_op jit(solution)/shard_map/ppermute | solution.py:32
  186.4 3.0 %collective-permute-done.22 = f32[18,1,128]{2,1,0:T(1,128)S(1)} collective-permute-done((f32[18,1,128]{2,1,0:T(1,128)S(1)}, f32[18,1,128]{2,1,0:T(1,128)S(1)}, u32[]{:S(2)}, u32[]{:S(2)}) %collective-permute-start.22) | collective-permute-done | bytes 9248 | tf_op jit(solution)/shard_map/ppermute | solution.py:32
  189.4 3.1 %collective-permute-start.24 = (f32[1,16,128]{2,1,0:T(8,128)S(1)}, f32[1,16,128]{2,1,0:T(8,128)S(1)}, u32[]{:S(2)}, u32[]{:S(2)}) collective-permute-start(f32[1,16,128]{2,1,0:T(8,128)S(1)} %get-tuple-element.123), channel_id=1, source_target_pairs={{4,0},{8,4},{12,8},{16,12},{20,16},{24,20},{28,24},{5,1},{9,5},{13... | collective-permute-start | bytes 24584 | tf_op jit(solution)/shard_map/ppermute | solution.py:32
  194.9 3.3 %collective-permute-done.25 = f32[1,16,128]{2,1,0:T(8,128)S(1)} collective-permute-done((f32[1,16,128]{2,1,0:T(8,128)S(1)}, f32[1,16,128]{2,1,0:T(8,128)S(1)}, u32[]{:S(2)}, u32[]{:S(2)}) %collective-permute-start.25) | collective-permute-done | bytes 8224 | tf_op jit(solution)/shard_map/ppermute | solution.py:29
  198.2 3.4 %collective-permute-start.27 = (f32[18,1,128]{2,1,0:T(1,128)S(1)}, f32[18,1,128]{2,1,0:T(1,128)S(1)}, u32[]{:S(2)}, u32[]{:S(2)}) collective-permute-start(f32[18,1,128]{2,1,0:T(1,128)S(1)} %get-tuple-element.113), channel_id=1, source_target_pairs={{0,1},{1,2},{2,3},{4,5},{5,6},{6,7},{8,9},{9,10},{10,11},{12,13},{... | collective-permute-start | bytes 27656 | tf_op jit(solution)/shard_map/ppermute | solution.py:29
  204.9 3.4 %collective-permute-done.26 = f32[18,1,128]{2,1,0:T(1,128)S(1)} collective-permute-done((f32[18,1,128]{2,1,0:T(1,128)S(1)}, f32[18,1,128]{2,1,0:T(1,128)S(1)}, u32[]{:S(2)}, u32[]{:S(2)}) %collective-permute-start.26) | collective-permute-done | bytes 9248 | tf_op jit(solution)/shard_map/ppermute | solution.py:32
  210.3 3.4 %collective-permute-start.29 = (f32[1,16,128]{2,1,0:T(8,128)S(1)}, f32[1,16,128]{2,1,0:T(8,128)S(1)}, u32[]{:S(2)}, u32[]{:S(2)}) collective-permute-start(f32[1,16,128]{2,1,0:T(8,128)S(1)} %get-tuple-element.120), channel_id=1, source_target_pairs={{0,4},{4,8},{8,12},{12,16},{16,20},{20,24},{24,28},{1,5},{5,9},{9,... | collective-permute-start | bytes 24584 | tf_op jit(solution)/shard_map/ppermute | solution.py:29
  215.9 3.1 %collective-permute-start.31 = (f32[18,1,128]{2,1,0:T(1,128)S(1)}, f32[18,1,128]{2,1,0:T(1,128)S(1)}, u32[]{:S(2)}, u32[]{:S(2)}) collective-permute-start(f32[18,1,128]{2,1,0:T(1,128)S(1)} %get-tuple-element.111), channel_id=1, source_target_pairs={{0,1},{1,2},{2,3},{4,5},{5,6},{6,7},{8,9},{9,10},{10,11},{12,13},{... | collective-permute-start | bytes 27656 | tf_op jit(solution)/shard_map/ppermute | solution.py:29
  221.0 11.0 %multiply_add_fusion = f32[6,16,16,128]{3,1,2,0:T(8,128)S(1)} fusion(f32[6,16,16,128]{3,1,2,0:T(8,128)S(1)} %copy-done.8, f32[6,16,21,128]{3,1,2,0:T(8,128)S(1)} %slice_subtract_fusion.2, f32[6,21,16,128]{3,1,2,0:T(8,128)S(1)} %slice_subtract_fusion.1, f32[6,16,16,133]{3,1,2,0:T(8,128)S(1)} %slice_subtract_fusion, f32[16,16,128]{2,0,1:T(8,128)S(1)} %copy-done.10, ...), kind=kLoop, calls=%fused_computation.29 | loop fusion | flops 75497472 | bytes 17006592 | tf_op jit(solution)/shard_map/add | solution.py:185
  (171 shorter events, 84.8 us)
Async XLA Ops:
  2.9 170.0 %collective-permute-start.3 = (f32[6,3,16,128]{3,1,2,0:T(4,128)}, f32[6,3,16,128]{3,1,2,0:T(4,128)S(1)}, u32[]{:S(2)}, u32[]{:S(2)}) collective-permute-start(f32[6,3,16,128]{3,1,2,0:T(4,128)} %get-tuple-element.74), channel_id=1, source_target_pairs={{4,0},{8,4},{12,8},{16,12},{20,16},{24,20},{28,24},{5,1},{9,5},{13... | collective-permute-start | bytes 442376 | tf_op jit(solution)/shard_map/ppermute | solution.py:32
  6.5 131.1 %collective-permute-start.1 = (f32[6,16,16,3]{2,1,3,0:T(8,128)}, f32[6,16,16,3]{2,1,3,0:T(8,128)}, u32[]{:S(2)}, u32[]{:S(2)}) collective-permute-start(f32[6,16,16,3]{2,1,3,0:T(8,128)} %copy.65), channel_id=1, source_target_pairs={{32,0},{64,32},{96,64},{128,96},{160,128},{192,160},{224,192},{0,2... | collective-permute-start | bytes 55304 | tf_op jit(solution)/shard_map/ppermute | solution.py:32
  11.3 130.2 %collective-permute-start = (f32[6,16,16,3]{2,1,3,0:T(8,128)}, f32[6,16,16,3]{2,1,3,0:T(8,128)}, u32[]{:S(2)}, u32[]{:S(2)}) collective-permute-start(f32[6,16,16,3]{2,1,3,0:T(8,128)} %copy.64), channel_id=1, source_target_pairs={{0,32},{32,64},{64,96},{96,128},{128,160},{160,192},{192,224},{224... | collective-permute-start | bytes 55304 | tf_op jit(solution)/shard_map/ppermute | solution.py:29
  20.0 25.9 %collective-permute-start.7 = (f32[6,16,16,2]{2,1,3,0:T(8,128)}, f32[6,16,16,2]{2,1,3,0:T(8,128)}, u32[]{:S(2)}, u32[]{:S(2)}) collective-permute-start(f32[6,16,16,2]{2,1,3,0:T(8,128)} %copy.51), channel_id=1, source_target_pairs={{32,0},{64,32},{96,64},{128,96},{160,128},{192,160},{224,192},{0,2... | collective-permute-start | bytes 36872 | tf_op jit(solution)/shard_map/ppermute | solution.py:32
  24.9 22.5 %collective-permute-start.6 = (f32[6,16,16,2]{2,1,3,0:T(8,128)}, f32[6,16,16,2]{2,1,3,0:T(8,128)}, u32[]{:S(2)}, u32[]{:S(2)}) collective-permute-start(f32[6,16,16,2]{2,1,3,0:T(8,128)} %copy.50), channel_id=1, source_target_pairs={{0,32},{32,64},{64,96},{96,128},{128,160},{160,192},{192,224},{224... | collective-permute-start | bytes 36872 | tf_op jit(solution)/shard_map/ppermute | solution.py:29
  52.4 6.7 %collective-permute-start.9 = (f32[6,2,16,132]{3,2,1,0:T(8,128)}, f32[6,2,16,132]{3,2,1,0:T(8,128)}, u32[]{:S(2)}, u32[]{:S(2)}) collective-permute-start(f32[6,2,16,132]{3,2,1,0:T(8,128)} %copy.55), channel_id=1, source_target_pairs={{4,0},{8,4},{12,8},{16,12},{20,16},{24,20},{28,24},{5,1},{9,5},{13... | collective-permute-start | bytes 304136 | tf_op jit(solution)/shard_map/ppermute | solution.py:32
  55.0 7.9 %collective-permute-start.8 = (f32[6,2,16,132]{3,2,1,0:T(8,128)}, f32[6,2,16,132]{3,2,1,0:T(8,128)}, u32[]{:S(2)}, u32[]{:S(2)}) collective-permute-start(f32[6,2,16,132]{3,2,1,0:T(8,128)} %copy.54), channel_id=1, source_target_pairs={{0,4},{4,8},{8,12},{12,16},{16,20},{20,24},{24,28},{1,5},{5,9},{9,... | collective-permute-start | bytes 304136 | tf_op jit(solution)/shard_map/ppermute | solution.py:29
  65.3 11.7 %collective-permute-start.11 = (f32[6,20,2,132]{3,1,2,0:T(8,128)S(1)}, f32[6,20,2,132]{3,1,2,0:T(8,128)S(1)}, u32[]{:S(2)}, u32[]{:S(2)}) collective-permute-start(f32[6,20,2,132]{3,1,2,0:T(8,128)S(1)} %get-tuple-element.62), channel_id=1, source_target_pairs={{1,0},{2,1},{3,2},{5,4},{6,5},{7,6},{9,8},{10,9},{11,10},{13,12},{... | collective-permute-start | bytes 380168 | tf_op jit(solution)/shard_map/ppermute | solution.py:32
  70.1 8.1 %collective-permute-start.10 = (f32[6,20,2,132]{3,1,2,0:T(8,128)S(1)}, f32[6,20,2,132]{3,1,2,0:T(8,128)S(1)}, u32[]{:S(2)}, u32[]{:S(2)}) collective-permute-start(f32[6,20,2,132]{3,1,2,0:T(8,128)S(1)} %get-tuple-element.61), channel_id=1, source_target_pairs={{0,1},{1,2},{2,3},{4,5},{5,6},{6,7},{8,9},{9,10},{10,11},{12,13},{... | collective-permute-start | bytes 380168 | tf_op jit(solution)/shard_map/ppermute | solution.py:29
  82.9 10.0 %all-to-all-start = ((f32[16,16,128]{2,1,0:T(8,128)}), f32[16,16,128]{2,1,0:T(8,128)S(1)}, u32[]{:S(2)}, u32[]{:S(2)}) async-start(f32[16,16,128]{2,1,0:T(8,128)} %copy.58), calls=%async_computation | async-start | bytes 262144 | tf_op jit(solution)/shard_map/all_to_all | solution.py:193
  101.6 8.7 %all-to-all-start.1 = ((f32[8,1,4096]{2,1,0:T(1,128)}), f32[8,1,4096]{2,1,0:T(1,128)S(1)}, u32[]{:S(2)}, u32[]{:S(2)}) async-start(f32[8,1,4096]{2,1,0:T(1,128)} %reshape.83), calls=%async_computation.1 | async-start | bytes 262144 | tf_op jit(solution)/shard_map/all_to_all | solution.py:198
  115.9 6.0 %collective-permute-start.12 = (f32[1,16,128]{2,1,0:T(8,128)S(1)}, f32[1,16,128]{2,1,0:T(8,128)S(1)}, u32[]{:S(2)}, u32[]{:S(2)}) collective-permute-start(f32[1,16,128]{2,1,0:T(8,128)S(1)} %get-tuple-element.129), channel_id=1, source_target_pairs={{4,0},{8,4},{12,8},{16,12},{20,16},{24,20},{28,24},{5,1},{9,5},{13... | collective-permute-start | bytes 24584 | tf_op jit(solution)/shard_map/ppermute | solution.py:32
  117.9 5.6 %collective-permute-start.13 = (f32[1,16,128]{2,1,0:T(8,128)S(1)}, f32[1,16,128]{2,1,0:T(8,128)S(1)}, u32[]{:S(2)}, u32[]{:S(2)}) collective-permute-start(f32[1,16,128]{2,1,0:T(8,128)S(1)} %get-tuple-element.128), channel_id=1, source_target_pairs={{0,4},{4,8},{8,12},{12,16},{16,20},{20,24},{24,28},{1,5},{5,9},{9,... | collective-permute-start | bytes 24584 | tf_op jit(solution)/shard_map/ppermute | solution.py:29
  124.1 19.0 %collective-permute-start.15 = (f32[18,1,128]{2,1,0:T(1,128)}, f32[18,1,128]{2,1,0:T(1,128)}, u32[]{:S(2)}, u32[]{:S(2)}) collective-permute-start(f32[18,1,128]{2,1,0:T(1,128)} %get-tuple-element.119), channel_id=1, source_target_pairs={{0,1},{1,2},{2,3},{4,5},{5,6},{6,7},{8,9},{9,10},{10,11},{12,13},{... | collective-permute-start | bytes 27656 | tf_op jit(solution)/shard_map/ppermute | solution.py:29
  134.3 8.8 %collective-permute-start.14 = (f32[18,1,128]{2,1,0:T(1,128)}, f32[18,1,128]{2,1,0:T(1,128)}, u32[]{:S(2)}, u32[]{:S(2)}) collective-permute-start(f32[18,1,128]{2,1,0:T(1,128)} %get-tuple-element.118), channel_id=1, source_target_pairs={{1,0},{2,1},{3,2},{5,4},{6,5},{7,6},{9,8},{10,9},{11,10},{13,12},{... | collective-permute-start | bytes 27656 | tf_op jit(solution)/shard_map/ppermute | solution.py:32
  137.5 35.4 %collective-permute-start.2 = (f32[6,3,16,128]{3,1,2,0:T(4,128)}, f32[6,3,16,128]{3,1,2,0:T(4,128)}, u32[]{:S(2)}, u32[]{:S(2)}) collective-permute-start(f32[6,3,16,128]{3,1,2,0:T(4,128)} %get-tuple-element.73), channel_id=1, source_target_pairs={{0,4},{4,8},{8,12},{12,16},{16,20},{20,24},{24,28},{1,5},{5,9},{9,... | collective-permute-start | bytes 442376 | tf_op jit(solution)/shard_map/ppermute | solution.py:29
  144.5 6.7 %collective-permute-start.16 = (f32[1,16,128]{2,1,0:T(8,128)S(1)}, f32[1,16,128]{2,1,0:T(8,128)S(1)}, u32[]{:S(2)}, u32[]{:S(2)}) collective-permute-start(f32[1,16,128]{2,1,0:T(8,128)S(1)} %get-tuple-element.127), channel_id=1, source_target_pairs={{4,0},{8,4},{12,8},{16,12},{20,16},{24,20},{28,24},{5,1},{9,5},{13... | collective-permute-start | bytes 24584 | tf_op jit(solution)/shard_map/ppermute | solution.py:32
  148.5 5.6 %collective-permute-start.17 = (f32[1,16,128]{2,1,0:T(8,128)S(1)}, f32[1,16,128]{2,1,0:T(8,128)S(1)}, u32[]{:S(2)}, u32[]{:S(2)}) collective-permute-start(f32[1,16,128]{2,1,0:T(8,128)S(1)} %get-tuple-element.126), channel_id=1, source_target_pairs={{0,4},{4,8},{8,12},{12,16},{16,20},{20,24},{24,28},{1,5},{5,9},{9,... | collective-permute-start | bytes 24584 | tf_op jit(solution)/shard_map/ppermute | solution.py:29
  154.2 9.3 %collective-permute-start.19 = (f32[18,1,128]{2,1,0:T(1,128)S(1)}, f32[18,1,128]{2,1,0:T(1,128)S(1)}, u32[]{:S(2)}, u32[]{:S(2)}) collective-permute-start(f32[18,1,128]{2,1,0:T(1,128)S(1)} %get-tuple-element.117), channel_id=1, source_target_pairs={{0,1},{1,2},{2,3},{4,5},{5,6},{6,7},{8,9},{9,10},{10,11},{12,13},{... | collective-permute-start | bytes 27656 | tf_op jit(solution)/shard_map/ppermute | solution.py:29
  161.0 6.5 %collective-permute-start.18 = (f32[18,1,128]{2,1,0:T(1,128)S(1)}, f32[18,1,128]{2,1,0:T(1,128)S(1)}, u32[]{:S(2)}, u32[]{:S(2)}) collective-permute-start(f32[18,1,128]{2,1,0:T(1,128)S(1)} %get-tuple-element.116), channel_id=1, source_target_pairs={{1,0},{2,1},{3,2},{5,4},{6,5},{7,6},{9,8},{10,9},{11,10},{13,12},{... | collective-permute-start | bytes 27656 | tf_op jit(solution)/shard_map/ppermute | solution.py:32
  167.6 13.3 %collective-permute-start.20 = (f32[1,16,128]{2,1,0:T(8,128)S(1)}, f32[1,16,128]{2,1,0:T(8,128)S(1)}, u32[]{:S(2)}, u32[]{:S(2)}) collective-permute-start(f32[1,16,128]{2,1,0:T(8,128)S(1)} %get-tuple-element.125), channel_id=1, source_target_pairs={{4,0},{8,4},{12,8},{16,12},{20,16},{24,20},{28,24},{5,1},{9,5},{13... | collective-permute-start | bytes 24584 | tf_op jit(solution)/shard_map/ppermute | solution.py:32
  169.5 11.3 %collective-permute-start.21 = (f32[1,16,128]{2,1,0:T(8,128)S(1)}, f32[1,16,128]{2,1,0:T(8,128)S(1)}, u32[]{:S(2)}, u32[]{:S(2)}) collective-permute-start(f32[1,16,128]{2,1,0:T(8,128)S(1)} %get-tuple-element.124), channel_id=1, source_target_pairs={{0,4},{4,8},{8,12},{12,16},{16,20},{20,24},{24,28},{1,5},{5,9},{9,... | collective-permute-start | bytes 24584 | tf_op jit(solution)/shard_map/ppermute | solution.py:29
  173.8 29.9 %collective-permute-start.5 = (f32[6,22,3,128]{3,1,2,0:T(8,128)S(1)}, f32[6,22,3,128]{3,1,2,0:T(8,128)S(1)}, u32[]{:S(2)}, u32[]{:S(2)}) collective-permute-start(f32[6,22,3,128]{3,1,2,0:T(8,128)S(1)} %get-tuple-element.66), channel_id=1, source_target_pairs={{1,0},{2,1},{3,2},{5,4},{6,5},{7,6},{9,8},{10,9},{11,10},{13,12},{... | collective-permute-start | bytes 608264 | tf_op jit(solution)/shard_map/ppermute | solution.py:32
  175.7 28.0 %collective-permute-start.4 = (f32[6,22,3,128]{3,1,2,0:T(8,128)S(1)}, f32[6,22,3,128]{3,1,2,0:T(8,128)S(1)}, u32[]{:S(2)}, u32[]{:S(2)}) collective-permute-start(f32[6,22,3,128]{3,1,2,0:T(8,128)S(1)} %get-tuple-element.65), channel_id=1, source_target_pairs={{0,1},{1,2},{2,3},{4,5},{5,6},{6,7},{8,9},{9,10},{10,11},{12,13},{... | collective-permute-start | bytes 608264 | tf_op jit(solution)/shard_map/ppermute | solution.py:29
  182.9 6.5 %collective-permute-start.22 = (f32[18,1,128]{2,1,0:T(1,128)S(1)}, f32[18,1,128]{2,1,0:T(1,128)S(1)}, u32[]{:S(2)}, u32[]{:S(2)}) collective-permute-start(f32[18,1,128]{2,1,0:T(1,128)S(1)} %get-tuple-element.114), channel_id=1, source_target_pairs={{1,0},{2,1},{3,2},{5,4},{6,5},{7,6},{9,8},{10,9},{11,10},{13,12},{... | collective-permute-start | bytes 27656 | tf_op jit(solution)/shard_map/ppermute | solution.py:32
  189.4 5.5 %collective-permute-start.24 = (f32[1,16,128]{2,1,0:T(8,128)S(1)}, f32[1,16,128]{2,1,0:T(8,128)S(1)}, u32[]{:S(2)}, u32[]{:S(2)}) collective-permute-start(f32[1,16,128]{2,1,0:T(8,128)S(1)} %get-tuple-element.123), channel_id=1, source_target_pairs={{4,0},{8,4},{12,8},{16,12},{20,16},{24,20},{28,24},{5,1},{9,5},{13... | collective-permute-start | bytes 24584 | tf_op jit(solution)/shard_map/ppermute | solution.py:32
  192.6 5.6 %collective-permute-start.25 = (f32[1,16,128]{2,1,0:T(8,128)S(1)}, f32[1,16,128]{2,1,0:T(8,128)S(1)}, u32[]{:S(2)}, u32[]{:S(2)}) collective-permute-start(f32[1,16,128]{2,1,0:T(8,128)S(1)} %get-tuple-element.122), channel_id=1, source_target_pairs={{0,4},{4,8},{8,12},{12,16},{16,20},{20,24},{24,28},{1,5},{5,9},{9,... | collective-permute-start | bytes 24584 | tf_op jit(solution)/shard_map/ppermute | solution.py:29
  198.2 6.7 %collective-permute-start.27 = (f32[18,1,128]{2,1,0:T(1,128)S(1)}, f32[18,1,128]{2,1,0:T(1,128)S(1)}, u32[]{:S(2)}, u32[]{:S(2)}) collective-permute-start(f32[18,1,128]{2,1,0:T(1,128)S(1)} %get-tuple-element.113), channel_id=1, source_target_pairs={{0,1},{1,2},{2,3},{4,5},{5,6},{6,7},{8,9},{9,10},{10,11},{12,13},{... | collective-permute-start | bytes 27656 | tf_op jit(solution)/shard_map/ppermute | solution.py:29
  201.6 6.6 %collective-permute-start.26 = (f32[18,1,128]{2,1,0:T(1,128)S(1)}, f32[18,1,128]{2,1,0:T(1,128)S(1)}, u32[]{:S(2)}, u32[]{:S(2)}) collective-permute-start(f32[18,1,128]{2,1,0:T(1,128)S(1)} %get-tuple-element.112), channel_id=1, source_target_pairs={{1,0},{2,1},{3,2},{5,4},{6,5},{7,6},{9,8},{10,9},{11,10},{13,12},{... | collective-permute-start | bytes 27656 | tf_op jit(solution)/shard_map/ppermute | solution.py:32
  210.3 5.6 %collective-permute-start.29 = (f32[1,16,128]{2,1,0:T(8,128)S(1)}, f32[1,16,128]{2,1,0:T(8,128)S(1)}, u32[]{:S(2)}, u32[]{:S(2)}) collective-permute-start(f32[1,16,128]{2,1,0:T(8,128)S(1)} %get-tuple-element.120), channel_id=1, source_target_pairs={{0,4},{4,8},{8,12},{12,16},{16,20},{20,24},{24,28},{1,5},{5,9},{9,... | collective-permute-start | bytes 24584 | tf_op jit(solution)/shard_map/ppermute | solution.py:29
  215.9 17.3 %collective-permute-start.31 = (f32[18,1,128]{2,1,0:T(1,128)S(1)}, f32[18,1,128]{2,1,0:T(1,128)S(1)}, u32[]{:S(2)}, u32[]{:S(2)}) collective-permute-start(f32[18,1,128]{2,1,0:T(1,128)S(1)} %get-tuple-element.111), channel_id=1, source_target_pairs={{0,1},{1,2},{2,3},{4,5},{5,6},{6,7},{8,9},{9,10},{10,11},{12,13},{... | collective-permute-start | bytes 27656 | tf_op jit(solution)/shard_map/ppermute | solution.py:29
  219.0 14.2 %collective-permute-start.30 = (f32[18,1,128]{2,1,0:T(1,128)S(1)}, f32[18,1,128]{2,1,0:T(1,128)S(1)}, u32[]{:S(2)}, u32[]{:S(2)}) collective-permute-start(f32[18,1,128]{2,1,0:T(1,128)S(1)} %get-tuple-element.110), channel_id=1, source_target_pairs={{1,0},{2,1},{3,2},{5,4},{6,5},{7,6},{9,8},{10,9},{11,10},{13,12},{... | collective-permute-start | bytes 27656 | tf_op jit(solution)/shard_map/ppermute | solution.py:32
  (21 other events, 333.3 us)
where the time goes:
time: 235 us; the launch traced here: 234 us
  starting transfers between devices  104 us (44%)
  other arithmetic  54 us (23%)
  waiting for transfers between devices  35.6 us (15%)
  local copies, waits for them, and re-layouts  33.1 us (14%)
  matrix products  6.02 us (3%)
    ppermute x16, starting transfers between devices, padded_2(): lax.ppermute(lax.slice_in_dim(block, block.shape[dim] - width, None, axis...  55 us
    ppermute x16, starting transfers between devices, padded_2(): lax.ppermute(lax.slice_in_dim(block, 0, width, axis=dim), axis, backward)  40.7 us
    dot_general x1, other arithmetic, shards(): jnp.einsum('rsx,mx->rsm', lax.all_to_all(source_field, 'stream', split_ax...  19.1 us
    ppermute x16, waiting for transfers between devices, padded_2(): lax.ppermute(lax.slice_in_dim(block, block.shape[dim] - width, None, axis...  13.9 us
    ppermute x16, waiting for transfers between devices, padded_2(): lax.ppermute(lax.slice_in_dim(block, 0, width, axis=dim), axis, backward)  12.8 us
    add x1, other arithmetic, shards(): log_conformation - TIME_STEP * advection  11 us
    unnamed x45, local copies, waits for them, and re-layouts  10.4 us
    dot_general x1, matrix products, shards(): jnp.einsum('rsx,mx->rsm', lax.all_to_all(source_field, 'stream', split_ax...  6.02 us
  transfers between devices with their start and end apart: 34, of which 13 were waited for; matrix products, arithmetic and copies ran while one was open for 38% of the time, Pallas kernels for 0%

commit v1 on v0

v1 whole, which is shorter than its diff:
```python
import math

import jax
import jax.numpy as jnp
import ml_dtypes
import numpy as np
from jax import lax
from jax.experimental import pallas as pl
from jax.experimental.pallas import tpu as pltpu
from jax.sharding import PartitionSpec as P

NX = 1024
LANES = 128
BLOCK = 16
PARTS = 8
LINES = 60
ROWS = 64

WEISSENBERG = 20.0
EXTENSIBILITY = 100.0
TIME_STEP = 2.0
EPSILON = 1e-06
COSINES = tuple((math.cos((2 * number + 1) * math.pi / 12.0) for number in range(6)))
VMEM_LIMIT = 48 * 1024 * 1024


def split_bf16(table):
    high = table.astype(np.float32).astype(ml_dtypes.bfloat16)
    low = (table - high.astype(np.float64)).astype(np.float32).astype(ml_dtypes.bfloat16)
    return high, low


def tables():
    ordinal = np.arange(NX)
    wave = np.where(ordinal <= NX // 2, ordinal, ordinal - NX // 2)
    angle = 2.0 * np.pi / NX * ((ordinal[:, None] * wave[None, :]) % NX)
    fourier = -np.where((ordinal <= NX // 2)[None, :], np.cos(angle), np.sin(angle)) * NX**-0.5
    places = []
    for part in range(PARTS):
        start = part * LANES
        places += [start - 2, start - 1, start + LANES, start + LANES + 1]
    edges = fourier[np.array(places) % NX]
    return split_bf16(fourier) + split_bf16(edges)


def mode_table():
    ordinal = np.arange(NX)
    wave = np.where(ordinal <= NX // 2, ordinal, ordinal - NX // 2)
    diagonal = 4.0 + 4.0 * np.sin(np.pi * wave / NX) ** 2
    ratio = 4.0 / diagonal
    upper = 1.0 + ratio
    lower = np.maximum(0.3, 1.0 - ratio)
    rows = []
    for cosine in COSINES:
        omega = 1.0 / (0.5 * (upper + lower) + 0.5 * (upper - lower) * cosine)
        rows += [omega / diagonal, 1.0 - omega]
    rows += [np.zeros(NX)] * 4
    return np.stack(rows).astype(np.float32).reshape(16, PARTS, LANES).transpose(1, 0, 2)


TABLE_HIGH, TABLE_LOW, EDGE_HIGH, EDGE_LOW = tables()
MODES = mode_table()
PICK = np.zeros((8, LANES), np.float32)
for row, lane in enumerate((126, 127, 0, 1)):
    PICK[row, lane] = 1.0
ENDS = np.zeros((8, LANES), np.float32)
for row, lane in ((0, 0), (1, 1), (2, 2), (4, 125), (5, 126), (6, 127)):
    ENDS[row, lane] = 1.0


def params():
    return pltpu.CompilerParams(vmem_limit_bytes=VMEM_LIMIT)


VMEM = pl.BlockSpec(memory_space=pltpu.VMEM)
SMEM = pl.BlockSpec(memory_space=pltpu.SMEM)


def dot_nt(left, right):
    return lax.dot_general(
        left,
        right,
        (((1,), (1,)), ((), ())),
        precision=lax.Precision.HIGHEST,
        preferred_element_type=jnp.float32,
    )


def dot_tn(left, right, precision=None):
    return lax.dot_general(
        left,
        right,
        (((0,), (0,)), ((), ())),
        precision=precision,
        preferred_element_type=jnp.float32,
    )


def sym_square(m):
    a, b, c, d, e, f = m
    bb, cc, ee = b * b, c * c, e * e
    return [
        a * a + bb + cc,
        b * (a + d) + c * e,
        c * (a + f) + b * e,
        bb + d * d + ee,
        e * (d + f) + b * c,
        cc + ee + f * f,
    ]


def sym_times(m, n):
    a, b, c, d, e, f = m
    p, q, r, s, t, u = n
    return [
        a * p + b * q + c * r,
        a * q + b * s + c * t,
        a * r + b * t + c * u,
        b * q + d * s + e * t,
        b * r + d * t + e * u,
        c * r + e * t + f * u,
    ]


DIAG = (1.0, 0.0, 0.0, 1.0, 0.0, 1.0)


def with_diag(m, value):
    return [m[i] + value if DIAG[i] else m[i] for i in range(6)]


def exp_pair(psi):
    m = [0.125 * v for v in psi]
    m2 = sym_square(m)
    m3 = sym_times(m, m2)
    tail = [m[i] * (1.0 / 24) + m2[i] * (1.0 / 120) + m3[i] * (1.0 / 720) for i in range(6)]
    tail = sym_times(m3, with_diag(tail, 1.0 / 6))
    out = with_diag([m[i] + 0.5 * m2[i] + tail[i] for i in range(6)], 1.0)
    for _ in range(3):
        out = sym_square(out)
    a, b, c, d, e, f = out
    scale = jnp.exp(-(psi[0] + psi[3] + psi[5]))
    inverse = [
        (d * f - e * e) * scale,
        (c * e - b * f) * scale,
        (b * e - c * d) * scale,
        (a * f - c * c) * scale,
        (b * c - a * e) * scale,
        (a * d - b * b) * scale,
    ]
    return out, inverse


def source_kernel(psi_ref, pick_ref, ends_ref, send_ref, base_ref, left_ref, right_ref, up_ref, down_ref, stress, field, wrapped):
    zero = jnp.zeros((24, LANES), jnp.float32)
    for comp in (1, 3, 4):
        for row in (0, 1, 2, 3, 20, 21, 22, 23):
            stress[comp, row] = zero

    def relax_row(row, carry):
        psi = [psi_ref[comp, row] for comp in range(6)]
        grown, shrunk = exp_pair(psi)
        peterlin = (EXTENSIBILITY - 3.0) / (EXTENSIBILITY - (grown[0] + grown[3] + grown[5]))
        pad = jnp.zeros((8, LANES), jnp.float32)
        for comp in range(6):
            value = peterlin * grown[comp]
            back = shrunk[comp]
            if DIAG[comp]:
                value = value - 1.0
                back = back - peterlin
            stress[comp, row + 4, 0:16] = value
            stress[comp, row + 4, 16:24] = pad
            base_ref[comp, row] = psi[comp] + (TIME_STEP / WEISSENBERG) * back
        return carry

    lax.fori_loop(0, BLOCK, relax_row, 0)

    lane = lax.broadcasted_iota(jnp.int32, (24, LANES), 1)
    inner = [lane < LANES - 1, lane >= 1, lane < LANES - 2, lane >= 2]

    def along(value, shift):
        return pltpu.roll(value, shift % 24, 0)

    def shifted(value, shift):
        return pltpu.roll(value, shift % LANES, 1)

    def emit(row, plain, once, twice):
        parts = [shifted(once, -1), -shifted(once, 1), shifted(twice, -2), shifted(twice, 2)]
        total = plain - 2.0 * twice
        beyond = zero
        for part, mask in zip(parts, inner):
            kept = jnp.where(mask, part, 0.0)
            total = total + kept
            beyond = beyond + (part - kept)
        at = row * 24 if isinstance(row, int) else pl.multiple_of(row * 24, 8)
        field[pl.ds(at, 24)] = total
        wrapped[pl.ds(at, 24)] = beyond

    def body(row, carry):
        here = row + 2
        s11 = 0.25 * (stress[3, here + 2] - 2.0 * stress[3, here] + stress[3, here - 2])
        u12 = 0.5 * (stress[4, here + 1] - stress[4, here - 1])
        u01 = 0.5 * (stress[1, here + 1] - stress[1, here - 1])
        s22, s02, s00 = stress[5, here], stress[2, here], stress[0, here]
        c22 = 0.25 * (along(s22, -2) - 2.0 * s22 + along(s22, 2))
        c12 = along(u12, -1) - along(u12, 1)
        c02 = 0.5 * (along(s02, -1) - along(s02, 1))
        emit(row, s11 + c22 + c12, u01 + c02, 0.25 * s00)
        return carry

    lax.fori_loop(2, 18, body, 0)
    for row in (0, 1, 18, 19):
        here = row + 2
        other = here + 2 if row < 2 else here - 2
        s11 = 0.25 * stress[3, other]
        if row in (1, 18):
            near = here + 1 if row == 1 else here - 1
            sign = 0.5 if row == 1 else -0.5
            u12 = sign * stress[4, near]
            u01 = sign * stress[1, near]
            emit(row, s11 + along(u12, -1) - along(u12, 1), u01, zero)
        else:
            emit(row, s11, zero, zero)
    wrapped[480:488] = jnp.zeros((8, LANES), jnp.float32)
    pick = pick_ref[...]
    for part in range(PARTS):
        send_ref[part, 0:LINES] = field[part * LINES : part * LINES + LINES]
        lines = dot_nt(pick, wrapped[part * LINES : part * LINES + ROWS])
        send_ref[part, LINES:ROWS, 0:ROWS] = lines[0:4]
        send_ref[part, LINES:ROWS, ROWS:LANES] = jnp.zeros((4, LANES - ROWS), jnp.float32)

    ends = ends_ref[...]
    for comp in range(6):
        found = dot_nt(ends, psi_ref[comp].reshape(BLOCK * BLOCK, LANES))
        left_ref[comp * 4 : comp * 4 + 4] = found[0:4]
        right_ref[comp * 4 : comp * 4 + 4] = found[4:8]
        for near in range(3):
            down_ref[comp, near] = psi_ref[comp, :, near]
            up_ref[comp, near] = psi_ref[comp, :, BLOCK - 3 + near]


def local_source(psi):
    shape = jax.ShapeDtypeStruct
    return pl.pallas_call(
        source_kernel,
        out_shape=(
            shape((PARTS, ROWS, LANES), jnp.float32),
            shape(psi.shape, jnp.float32),
            shape((24, BLOCK * BLOCK), jnp.float32),
            shape((24, BLOCK * BLOCK), jnp.float32),
            shape((6, 3, BLOCK, LANES), jnp.float32),
            shape((6, 3, BLOCK, LANES), jnp.float32),
        ),
        in_specs=[VMEM] * 3,
        out_specs=[VMEM] * 6,
        scratch_shapes=[
            pltpu.VMEM((6, 24, 24, LANES), jnp.float32),
            pltpu.VMEM((480, LANES), jnp.float32),
            pltpu.VMEM((488, LANES), jnp.float32),
        ],
        compiler_params=params(),
        cost_estimate=pl.CostEstimate(flops=20_000_000, bytes_accessed=3_000_000, transcendentals=0),
        name="local_source",
    )(psi, jnp.asarray(PICK), jnp.asarray(ENDS))


def transform_kernel(lines_ref, high_ref, low_ref, edge_high_ref, edge_low_ref, out_ref):
    lines = jnp.concatenate([lines_ref[part] for part in range(PARTS)], axis=1)
    high = lines.astype(jnp.bfloat16)
    low = (lines - high.astype(jnp.float32)).astype(jnp.bfloat16)
    edges = jnp.concatenate([lines_ref[part, LINES:ROWS] for part in range(PARTS)], axis=0)
    edges_high = edges.astype(jnp.bfloat16).astype(jnp.float32)
    edges_low = edges - edges_high
    edges_high = edges_high.astype(jnp.bfloat16)
    edges_low = edges_low.astype(jnp.bfloat16)
    both = jnp.concatenate([high, low], axis=0)
    for part in range(PARTS):
        cols = slice(part * LANES, (part + 1) * LANES)
        table = high_ref[:, cols]
        first = jnp.dot(both, table, preferred_element_type=jnp.float32)
        second = jnp.dot(high, low_ref[:, cols], preferred_element_type=jnp.float32)
        edge_table = edge_high_ref[:, cols]
        third = dot_tn(edges_high, edge_table) + dot_tn(edges_low, edge_table)
        third = third + dot_tn(edges_high, edge_low_ref[:, cols])
        out_ref[part] = (first[0:ROWS] + third[0:ROWS]) + (first[ROWS:] + second)


def transform(lines):
    return pl.pallas_call(
        transform_kernel,
        out_shape=jax.ShapeDtypeStruct((PARTS, ROWS, LANES), jnp.float32),
        in_specs=[VMEM] * 5,
        out_specs=VMEM,
        compiler_params=params(),
        cost_estimate=pl.CostEstimate(flops=400_000_000, bytes_accessed=5_000_000, transcendentals=0),
        name="transform",
    )(lines, jnp.asarray(TABLE_HIGH), jnp.asarray(TABLE_LOW), jnp.asarray(EDGE_HIGH), jnp.asarray(EDGE_LOW))


def radial_kernel(place_ref, own_ref, low_ref, high_ref, out_ref, up_ref, down_ref, flat, flat_low, flat_high):
    for part in range(PARTS):
        flat[part * LINES : part * LINES + LINES] = own_ref[part, 0:LINES]
    for part in range(3):
        flat_low[part * LINES + 4 : part * LINES + 4 + LINES] = low_ref[part, 0:LINES]
        flat_high[part * LINES : part * LINES + LINES] = high_ref[part, 0:LINES]
    has_low = place_ref[1] > 0
    has_high = place_ref[1] < 7

    def own(row):
        return flat[row * 24 : row * 24 + 24]

    def low(row):
        at = (row - 13) * 24 + 16
        return jnp.where(has_low, flat_low[at : at + 24], 0.0)

    def high(row):
        return jnp.where(has_high, flat_high[row * 24 : row * 24 + 24], 0.0)

    for row in range(26):
        if row < 3:
            value = low(row + 13)
        elif row < 5:
            value = low(row + 13) + jnp.where(has_low, own(row - 3), 0.0)
        elif row < 7:
            value = low(row + 13) + own(row - 3)
        elif row < 19:
            value = own(row - 3)
        elif row < 21:
            value = own(row - 3) + high(row - 19)
        elif row < 23:
            value = jnp.where(has_high, own(row - 3), 0.0) + high(row - 19)
        else:
            value = high(row - 19)
        out_ref[row] = value
        up_ref[row] = pltpu.roll(value, 24 - 11, 0)[0:8]
        down_ref[row] = pltpu.roll(value, 2, 0)[0:8]


def radial_assembly(place, own, low, high):
    shape = jax.ShapeDtypeStruct
    return pl.pallas_call(
        radial_kernel,
        out_shape=(
            shape((26, 24, LANES), jnp.float32),
            shape((26, 8, LANES), jnp.float32),
            shape((26, 8, LANES), jnp.float32),
        ),
        in_specs=[SMEM] + [VMEM] * 3,
        out_specs=[VMEM] * 3,
        scratch_shapes=[
            pltpu.VMEM((480, LANES), jnp.float32),
            pltpu.VMEM((192, LANES), jnp.float32),
            pltpu.VMEM((184, LANES), jnp.float32),
        ],
        compiler_params=params(),
        cost_estimate=pl.CostEstimate(flops=300_000, bytes_accessed=1_000_000, transcendentals=0),
        name="radial_assembly",
    )(place, own, low, high)


def relax_kernel(place_ref, modes_ref, rows_ref, low_ref, high_ref, out_ref, source, even, odd):
    radial, span = place_ref[1], place_ref[2]
    has_low = span > 0
    has_high = span < 3
    sublane = lax.broadcasted_iota(jnp.int32, (8, LANES), 0)
    cell = lax.broadcasted_iota(jnp.int32, (32, LANES), 0)
    inside = ((cell < 16) | ((cell < 24) & has_high)) | ((cell >= 24) & has_low)
    modes = modes_ref[place_ref[0]]
    weights = [
        jnp.where(inside, jnp.broadcast_to(modes[2 * j : 2 * j + 1], (32, LANES)), 0.0) for j in range(6)
    ]
    keeps = [jnp.broadcast_to(modes[2 * j + 1 : 2 * j + 2], (32, LANES)) for j in range(6)]
    pad = jnp.zeros((24, LANES), jnp.float32)
    for row in range(26):
        own = rows_ref[row]
        tail = own[16:24]
        own = jnp.concatenate(
            [own[0:16], jnp.where(sublane < 2, tail, 0.0), jnp.where(sublane >= 6, tail, 0.0)], axis=0
        )
        low = jnp.concatenate([jnp.where(has_low, low_ref[row], 0.0), pad], axis=0)
        high = jnp.concatenate([jnp.where(has_high, high_ref[row], 0.0), pad], axis=0)
        value = own + pltpu.roll(low, 27, 0) + pltpu.roll(high, 14, 0)
        source[row] = value
        even[row] = value * weights[0]

    no_low = radial == 0
    no_high = radial == 7

    @pl.when(no_low)
    def _():
        for row in range(5):
            even[row] = jnp.zeros((32, LANES), jnp.float32)
            odd[row] = jnp.zeros((32, LANES), jnp.float32)

    @pl.when(no_high)
    def _():
        for row in range(21, 26):
            even[row] = jnp.zeros((32, LANES), jnp.float32)
            odd[row] = jnp.zeros((32, LANES), jnp.float32)

    old, new = even, odd
    for sweep in range(1, 6):
        weight, keep = weights[sweep], keeps[sweep]
        for row in range(sweep, 26 - sweep):
            middle = old[row]
            beside = (old[row - 1] + old[row + 1]) + (pltpu.roll(middle, 1, 0) + pltpu.roll(middle, 31, 0))
            value = keep * middle + weight * (source[row] + beside)
            if sweep == 5:
                out_ref[row - 5] = value[0:16]
            elif row < 5:
                new[row] = jnp.where(no_low, 0.0, value)
            elif row > 20:
                new[row] = jnp.where(no_high, 0.0, value)
            else:
                new[row] = value
        old, new = new, old


def relaxation(place, rows, low, high):
    return pl.pallas_call(
        relax_kernel,
        out_shape=jax.ShapeDtypeStruct((BLOCK, BLOCK, LANES), jnp.float32),
        in_specs=[SMEM] + [VMEM] * 4,
        out_specs=VMEM,
        scratch_shapes=[pltpu.VMEM((26, 32, LANES), jnp.float32)] * 3,
        compiler_params=params(),
        cost_estimate=pl.CostEstimate(flops=5_000_000, bytes_accessed=1_000_000, transcendentals=0),
        name="relaxation",
    )(place, jnp.asarray(MODES), rows, low, high)


def weno(positive, d):
    a = jnp.where(positive, d[0], d[5])
    b = jnp.where(positive, d[1], d[4])
    c = jnp.where(positive, d[2], d[3])
    e = jnp.where(positive, d[3], d[2])
    g = jnp.where(positive, d[4], d[1])
    p0, p1, p2, p3 = a - b, b - c, c - e, e - g
    t0, t1, t2 = p0 - p1, p1 - p2, p2 - p3
    h0, h1, h2 = t0 - 2.0 * p1, p1 + p2, t2 + 2.0 * p2
    q0 = (13.0 / 3.0) * (t0 * t0) + (h0 * h0 + 4.0 * EPSILON)
    q1 = (13.0 / 3.0) * (t1 * t1) + (h1 * h1 + 4.0 * EPSILON)
    q2 = (13.0 / 3.0) * (t2 * t2) + (h2 * h2 + 4.0 * EPSILON)
    q0, q1, q2 = q0 * q0, q1 * q1, q2 * q2
    w0 = q1 * q2
    w1 = 6.0 * (q0 * q2)
    w2 = 3.0 * (q0 * q1)
    top = w0 * (2.0 * p0 - 5.0 * p1) - w1 * (p1 + 2.0 * p2) + w2 * (p3 - 4.0 * p2)
    return c + top / (6.0 * (w0 + w1 + w2))


def advect_kernel(place_ref, ends_ref, psi_ref, velocity_ref, base_ref, low_ref, high_ref, down_ref, up_ref, left_ref, right_ref, out_ref, radial, beside, ahead):
    has_low, has_high = place_ref[1] > 0, place_ref[1] < 7
    has_down, has_up = place_ref[2] > 0, place_ref[2] < 3
    for comp in range(6):
        for near in range(3):
            radial[comp, near] = jnp.where(has_low, low_ref[comp, near], 0.0)
            radial[comp, 19 + near] = jnp.where(has_high, high_ref[comp, near], 0.0)
            beside[comp, :, near] = jnp.where(has_up, up_ref[comp, near], 0.0)
            beside[comp, :, 5 + near] = jnp.where(has_down, down_ref[comp, near], 0.0)
        for row in range(BLOCK):
            radial[comp, 3 + row] = psi_ref[comp, row]
        ends = jnp.concatenate([right_ref[comp * 4 : comp * 4 + 4], left_ref[comp * 4 : comp * 4 + 4]], axis=0)
        found = dot_tn(ends, ends_ref[...], lax.Precision.HIGHEST)
        ahead[comp] = found.reshape(BLOCK, BLOCK, LANES)
    lane = lax.broadcasted_iota(jnp.int32, (BLOCK, LANES), 1)

    def step(number, carry):
        comp, row = number // BLOCK, number % BLOCK
        speeds = [velocity_ref[direction, row] for direction in range(3)]
        psi = radial[comp, row + 3]
        lines = [radial[comp, row + k] for k in range(7)]
        total = speeds[1] * weno(speeds[1] > 0, [lines[k + 1] - lines[k] for k in range(6)])

        far = ahead[comp, row]
        lines = []
        for k in range(-3, 4):
            if k > 0:
                mixed = jnp.where(lane < k, far, psi)
            else:
                mixed = jnp.where(lane >= LANES + k, far, psi)
            lines.append(pltpu.roll(mixed, (-k) % LANES, 1) if k else psi)
        total = total + speeds[0] * weno(speeds[0] > 0, [lines[k + 1] - lines[k] for k in range(6)])

        column = jnp.concatenate([psi, beside[comp, row]], axis=0)
        column = pltpu.roll(column, 23, 0) - column
        steps = [pltpu.roll(column, (-k) % 24, 0)[0:16] if k else column[0:16] for k in range(-3, 3)]
        total = total + speeds[2] * weno(speeds[2] > 0, steps)
        out_ref[comp, row] = base_ref[comp, row] - TIME_STEP * total
        return carry

    lax.fori_loop(0, 6 * BLOCK, step, 0)


def advect(place, psi, velocity, base, low, high, down, up, left, right):
    return pl.pallas_call(
        advect_kernel,
        out_shape=jax.ShapeDtypeStruct(psi.shape, jnp.float32),
        in_specs=[SMEM] + [VMEM] * 10,
        out_specs=VMEM,
        scratch_shapes=[
            pltpu.VMEM((6, 22, BLOCK, LANES), jnp.float32),
            pltpu.VMEM((6, BLOCK, 8, LANES), jnp.float32),
            pltpu.VMEM((6, BLOCK, BLOCK, LANES), jnp.float32),
        ],
        compiler_params=params(),
        cost_estimate=pl.CostEstimate(flops=50_000_000, bytes_accessed=4_000_000, transcendentals=0),
        name="advect",
    )(place, jnp.asarray(ENDS), psi, velocity, base, low, high, down, up, left, right)


def ring(axis, step):
    count = lax.axis_size(axis)
    return [(i, (i + step) % count) for i in range(count)]


def exchange(to_next, to_previous, axis):
    return (
        lax.ppermute(to_next, axis, ring(axis, 1)),
        lax.ppermute(to_previous, axis, ring(axis, -1)),
    )


def shards(psi, velocity):
    place = jnp.stack([lax.axis_index(axis) for axis in ("stream", "radial", "span")]).astype(jnp.int32)
    send, base, ends_left, ends_right, up, down = local_source(psi)
    low, high = exchange(psi[:, BLOCK - 3 :], psi[:, :3], "radial")
    from_down, from_up = exchange(up, down, "span")
    from_left, from_right = exchange(ends_right, ends_left, "stream")

    lines = lax.all_to_all(send, "stream", split_axis=0, concat_axis=0, tiled=True)
    spectrum = transform(lines)
    own = lax.all_to_all(spectrum, "stream", split_axis=0, concat_axis=0, tiled=True)
    below, above = exchange(own[5:], own[:3], "radial")
    rows, rows_up, rows_down = radial_assembly(place, own, below, above)
    before, after = exchange(rows_up, rows_down, "span")
    modes = relaxation(place, rows, before, after)
    following = advect(place, psi, velocity, base, low, high, from_down, from_up, from_left, from_right)
    return following, modes


def solution(mesh):
    return jax.shard_map(
        shards,
        mesh=mesh,
        in_specs=(P(None, "radial", "span", "stream"), P(None, "radial", "span", "stream")),
        out_specs=(P(None, "radial", "span", "stream"), P("radial", "span", "stream")),
        check_vma=False,
    )
```

time: 235 us -> 71.5 us (0.30)
  the two profiles are of different devices: /device:TPU:129 before, /device:TPU:1 now
where the time goes in v1:
time: 71.5 us; the launch traced here: 71 us
  starting transfers between devices  26.8 us (37%)
  Pallas kernels  22.8 us (32%)
  blocking collectives  11.9 us (17%)
  local copies, waits for them, and re-layouts  8.05 us (11%)
  between operations  0.74 us (1%)
    ppermute x5, starting transfers between devices, exchange(): lax.ppermute(to_next, axis, ring(axis, 1))  14.8 us
    pallas_call x1, Pallas kernels, advect(): pl.pallas_call(advect_kernel, out_shape=jax.ShapeDtypeStruct(psi.shape, j...  14.3 us
    all_to_all x1, blocking collectives, shards(): lax.all_to_all(send, 'stream', split_axis=0, concat_axis=0, tiled=True)  11.9 us
    ppermute x5, starting transfers between devices, exchange(): lax.ppermute(to_previous, axis, ring(axis, -1))  8.44 us
    unnamed x22, local copies, waits for them, and re-layouts  7.38 us
    pallas_call x1, Pallas kernels, local_source(): pl.pallas_call(source_kernel, out_shape=(shape((PARTS, ROWS, LANES), jnp....  3.89 us
    all_to_all x1, starting transfers between devices, shards(): lax.all_to_all(spectrum, 'stream', split_axis=0, concat_axis=0, tiled=True)  3.54 us
    pallas_call x1, Pallas kernels, transform(): pl.pallas_call(transform_kernel, out_shape=jax.ShapeDtypeStruct((PARTS, R...  2.12 us
  transfers between devices with their start and end apart: 11, of which 2 were waited for; matrix products, arithmetic and copies ran while one was open for 1% of the time, Pallas kernels for 21%

profile of v1, /device:TPU:1, one launch (start us, length us, event | category | flops | bytes accessed | tf_op | source)
XLA Modules:
  0.0 71.0 jit_solution(4968954252119501610)
XLA Ops:
  0.6 0.0 copy-start
  0.6 1.1 %copy-done = f32[6,16,16,128]{3,2,1,0:T(8,128)S(1)} copy-done((f32[6,16,16,128]{3,2,1,0:T(8,128)S(1)}, f32[6,16,16,128]{3,2,1,0:T(8,128)}, u32[]{:S(2)}) %copy-start) | copy-done | bytes 786456
  1.8 0.7 copy-done.8
  2.5 0.7 copy-done.10
  3.1 3.9 %local_source.1 = (f32[8,64,128]{2,1,0:T(8,128)S(1)}, f32[6,16,16,128]{3,2,1,0:T(8,128)S(1)}, f32[24,256]{1,0:T(8,128)S(1)}, f32[24,256]{1,0:T(8,128)S(1)}, f32[...) custom-call(f32[6,16,16,128]{3,2,1,0:T(8,128)S(1)} %copy-done, f32[8,128]{1,0:T(8,128)S(1)} %copy-done.10, ...), custom_call_target="tpu_custom_call" | custom-call | flops 20000000 | bytes 3000000 | tf_op jit(solution)/shard_map/local_source/pallas_call | solution.py:244
  7.0 11.9 %all_to_all.10.lines_ref = f32[8,64,128]{2,1,0:T(8,128)S(1)} all-to-all(f32[8,64,128]{2,1,0:T(8,128)S(1)} %get-tuple-element.16), channel_id=1, replica_groups=mesh['stream'=8,'radial'=8,'span'=4] {'stream'}, dimensions={0} | all-to-all | bytes 524288 | tf_op jit(solution)/shard_map/all_to_all | solution.py:531
  19.0 1.6 %copy-done.2 = bf16[1024,1024]{1,0:T(8,128)(2,1)S(1)} copy-done((bf16[1024,1024]{1,0:T(8,128)(2,1)S(1)}, bf16[1024,1024]{1,0:T(8,128)(2,1)}, u32[]{:S(2)}) %copy-start.2) | copy-done | bytes 2097176
  20.6 1.6 %copy-done.3 = bf16[1024,1024]{1,0:T(8,128)(2,1)S(1)} copy-done((bf16[1024,1024]{1,0:T(8,128)(2,1)S(1)}, bf16[1024,1024]{1,0:T(8,128)(2,1)}, u32[]{:S(2)}) %copy-start.3) | copy-done | bytes 2097176
  22.2 0.8 %copy-done.5 = bf16[32,1024]{1,0:T(8,128)(2,1)S(1)} copy-done((bf16[32,1024]{1,0:T(8,128)(2,1)S(1)}, bf16[32,1024]{1,0:T(8,128)(2,1)}, u32[]{:S(2)}) %copy-start.5) | copy-done | bytes 65560
  23.0 0.8 %copy-done.6 = bf16[32,1024]{1,0:T(8,128)(2,1)S(1)} copy-done((bf16[32,1024]{1,0:T(8,128)(2,1)S(1)}, bf16[32,1024]{1,0:T(8,128)(2,1)}, u32[]{:S(2)}) %copy-start.6) | copy-done | bytes 65560
  23.8 2.1 %transform.1 = f32[8,64,128]{2,1,0:T(8,128)} custom-call(f32[8,64,128]{2,1,0:T(8,128)S(1)} %all_to_all.10.lines_ref, bf16[1024,1024]{1,0:T(8,128)(2,1)S(1)} %copy-done.2, bf16[1024,1024]{1,0:T(8,128)(2,1)S(1)} %copy-done.3, bf16[32,1024]{1,0:T(8,128)(2,1)S(1)} %copy-done.5, bf16[32,1024]{1,0:T(8,128)(2,1)S(1)} %copy-done.6), custom_call_target="tpu_custom_call" | custom-call | flops 400000000 | bytes 5000000 | tf_op jit(solution)/shard_map/transform/pallas_call | solution.py:289
  26.0 3.5 %all-to-all-start.1 = ((f32[8,64,128]{2,1,0:T(8,128)}), f32[8,64,128]{2,1,0:T(8,128)S(1)}, u32[]{:S(2)}, u32[]{:S(2)}) async-start(f32[8,64,128]{2,1,0:T(8,128)} %transform.1), calls=%async_computation.1 | async-start | bytes 524288 | tf_op jit(solution)/shard_map/all_to_all | solution.py:533
  29.5 4.5 %collective-permute-start.2 = (f32[6,3,16,128]{3,2,1,0:T(8,128)S(1)}, f32[6,3,16,128]{3,2,1,0:T(8,128)S(1)}, u32[]{:S(2)}, u32[]{:S(2)}) collective-permute-start(f32[6,3,16,128]{3,2,1,0:T(8,128)S(1)} %get-tuple-element.12), channel_id=1, source_target_pairs={{0,1},{1,2},{2,3},{3,0},{4,5},{5,6},{6,7},{7,4},{8,9},{9,10},{10,1... | collective-permute-start | bytes 442376 | tf_op jit(solution)/shard_map/ppermute | solution.py:519
  34.0 0.0 collective-permute-start.3
  34.0 1.6 %collective-permute-start.4 = (f32[24,256]{1,0:T(8,128)S(1)}, f32[24,256]{1,0:T(8,128)S(1)}, u32[]{:S(2)}, u32[]{:S(2)}) collective-permute-start(f32[24,256]{1,0:T(8,128)S(1)} %get-tuple-element.14), channel_id=1, source_target_pairs={{0,32},{32,64},{64,96},{96,128},{128,160},{160,192},{192,224},{224... | collective-permute-start | bytes 73736 | tf_op jit(solution)/shard_map/ppermute | solution.py:519
  35.6 0.3 all-to-all-done.1.own_ref
  35.9 0.7 fusion.1
  36.5 1.6 %collective-permute-start.6 = (f32[3,64,128]{2,1,0:T(8,128)}, f32[3,64,128]{2,1,0:T(8,128)S(1)}, u32[]{:S(2)}, u32[]{:S(2)}) collective-permute-start(f32[3,64,128]{2,1,0:T(8,128)} %get-tuple-element.23), channel_id=1, source_target_pairs={{0,4},{4,8},{8,12},{12,16},{16,20},{20,24},{24,28},{28,0},{1,5},{5... | collective-permute-start | bytes 294920 | tf_op jit(solution)/shard_map/ppermute | solution.py:519
  38.2 3.9 %collective-permute-start.7 = (f32[3,64,128]{2,1,0:T(8,128)S(1)}, f32[3,64,128]{2,1,0:T(8,128)S(1)}, u32[]{:S(2)}, u32[]{:S(2)}) collective-permute-start(f32[3,64,128]{2,1,0:T(8,128)S(1)} %get-tuple-element.22), channel_id=1, source_target_pairs={{0,28},{4,0},{8,4},{12,8},{16,12},{20,16},{24,20},{28,24},{1,29},{... | collective-permute-start | bytes 294920 | tf_op jit(solution)/shard_map/ppermute | solution.py:520
  42.2 0.0 collective-permute-done.4.left_ref
  42.2 1.8 %collective-permute-start.5 = (f32[24,256]{1,0:T(8,128)S(1)}, f32[24,256]{1,0:T(8,128)S(1)}, u32[]{:S(2)}, u32[]{:S(2)}) collective-permute-start(f32[24,256]{1,0:T(8,128)S(1)} %get-tuple-element.15), channel_id=1, source_target_pairs={{0,224},{32,0},{64,32},{96,64},{128,96},{160,128},{192,160},{224,1... | collective-permute-start | bytes 73736 | tf_op jit(solution)/shard_map/ppermute | solution.py:520
  44.0 0.3 collective-permute-done.6.low_ref
  44.3 2.7 %collective-permute-start.1 = (f32[6,3,16,128]{3,2,1,0:T(8,128)S(1)}, f32[6,3,16,128]{3,2,1,0:T(8,128)S(1)}, u32[]{:S(2)}, u32[]{:S(2)}) collective-permute-start(f32[6,3,16,128]{3,2,1,0:T(8,128)S(1)} %get-tuple-element.20), channel_id=1, source_target_pairs={{0,28},{4,0},{8,4},{12,8},{16,12},{20,16},{24,20},{28,24},{1,29},{... | collective-permute-start | bytes 442376 | tf_op jit(solution)/shard_map/ppermute | solution.py:520
  47.0 0.1 pad_add_fusion.place_ref
  47.1 0.6 radial_assembly.1
  47.7 7.1 %collective-permute-start.8 = (f32[26,8,128]{2,1,0:T(8,128)S(1)}, f32[26,8,128]{2,1,0:T(8,128)S(1)}, u32[]{:S(2)}, u32[]{:S(2)}) collective-permute-start(f32[26,8,128]{2,1,0:T(8,128)S(1)} %get-tuple-element.18), channel_id=1, source_target_pairs={{0,1},{1,2},{2,3},{3,0},{4,5},{5,6},{6,7},{7,4},{8,9},{9,10},{10,1... | collective-permute-start | bytes 319496 | tf_op jit(solution)/shard_map/ppermute | solution.py:519
  54.8 0.0 collective-permute-done.2.down_ref
  54.8 0.0 collective-permute-done.low_ref
  54.8 14.3 %advect.1 = f32[6,16,16,128]{3,2,1,0:T(8,128)} custom-call(s32[3]{0:T(128)S(1)} %pad_add_fusion.place_ref, f32[8,128]{1,0:T(8,128)S(1)} %copy-done.9, f32[6,16,16,128]{3,2,1,0:T(8,128)S(1)} %copy-done.1, f32[3,16,16,128]{3,2,1,0:T(8,128)S(1)} %copy-done.4, f32[6,16,16,128]{3,2,1,0:T(8,128)S(1)} %get-tuple-element.11.base_ref, ...), custom_call_target="tpu_custom_call" | custom-call | flops 50000000 | bytes 4000000 | tf_op jit(solution)/shard_map/advect/pallas_call | solution.py:496
  69.2 0.0 collective-permute-done.8.low_ref
  69.2 0.0 collective-permute-done.9.high_ref
  69.2 1.8 %relaxation.1 = f32[16,16,128]{2,1,0:T(8,128)} custom-call(s32[3]{0:T(128)S(1)} %pad_add_fusion.place_ref, f32[8,16,128]{2,1,0:T(8,128)S(1)} %copy-done.7, f32[26,24,128]{2,1,0:T(8,128)S(1)} %get-tuple-element.17.rows_ref, f32[26,8,128]{2,1,0:T(8,128)S(1)} %collective-permute-done.8.low_ref, f32[26,8,128]{2,1,0:T(8,128)S(1)} %collective-permute-done.9.high_ref), custom_call_target="tpu_custom_call" | custom-call | flops 5000000 | bytes 1000000 | tf_op jit(solution)/shard_map/relaxation/pallas_call | solution.py:420
  (21 shorter events, 0.1 us)
Async XLA Ops:
  0.6 1.1 %copy-start = (f32[6,16,16,128]{3,2,1,0:T(8,128)S(1)}, f32[6,16,16,128]{3,2,1,0:T(8,128)}, u32[]{:S(2)}) copy-start(f32[6,16,16,128]{3,2,1,0:T(8,128)} %psi_ref.3) | copy-start | bytes 2359300
  1.8 0.7 copy-start.8
  2.5 0.7 copy-start.10
  19.0 1.6 %copy-start.2 = (bf16[1024,1024]{1,0:T(8,128)(2,1)S(1)}, bf16[1024,1024]{1,0:T(8,128)(2,1)}, u32[]{:S(2)}) copy-start(bf16[1024,1024]{1,0:T(8,128)(2,1)} %constant.29.clone.high_ref) | copy-start | bytes 6291460
  20.6 1.6 %copy-start.3 = (bf16[1024,1024]{1,0:T(8,128)(2,1)S(1)}, bf16[1024,1024]{1,0:T(8,128)(2,1)}, u32[]{:S(2)}) copy-start(bf16[1024,1024]{1,0:T(8,128)(2,1)} %constant.30.clone.low_ref) | copy-start | bytes 6291460
  22.2 0.8 %copy-start.5 = (bf16[32,1024]{1,0:T(8,128)(2,1)S(1)}, bf16[32,1024]{1,0:T(8,128)(2,1)}, u32[]{:S(2)}) copy-start(bf16[32,1024]{1,0:T(8,128)(2,1)} %constant.31.clone.edge_high_ref) | copy-start | bytes 196612
  23.0 0.8 %copy-start.6 = (bf16[32,1024]{1,0:T(8,128)(2,1)S(1)}, bf16[32,1024]{1,0:T(8,128)(2,1)}, u32[]{:S(2)}) copy-start(bf16[32,1024]{1,0:T(8,128)(2,1)} %constant.32.clone.edge_low_ref) | copy-start | bytes 196612
  23.8 18.3 %copy-start.1 = (f32[6,16,16,128]{3,2,1,0:T(8,128)S(1)}, f32[6,16,16,128]{3,2,1,0:T(8,128)}, u32[]{:S(2)}) copy-start(f32[6,16,16,128]{3,2,1,0:T(8,128)} %psi_ref.3) | copy-start | bytes 2359300
  23.8 31.0 %copy-start.9 = (f32[8,128]{1,0:T(8,128)S(1)}, f32[8,128]{1,0:T(8,128)}, u32[]{:S(2)}) copy-start(f32[8,128]{1,0:T(8,128)} %constant.28.clone.ends_ref) | copy-start | bytes 12292
  26.0 28.9 %copy-start.4 = (f32[3,16,16,128]{3,2,1,0:T(8,128)S(1)}, f32[3,16,16,128]{3,2,1,0:T(8,128)}, u32[]{:S(2)}) copy-start(f32[3,16,16,128]{3,2,1,0:T(8,128)} %velocity_ref.1) | copy-start | bytes 1179652
  26.0 9.9 %all-to-all-start.1 = ((f32[8,64,128]{2,1,0:T(8,128)}), f32[8,64,128]{2,1,0:T(8,128)S(1)}, u32[]{:S(2)}, u32[]{:S(2)}) async-start(f32[8,64,128]{2,1,0:T(8,128)} %transform.1), calls=%async_computation.1 | async-start | bytes 524288 | tf_op jit(solution)/shard_map/all_to_all | solution.py:533
  29.5 25.3 %collective-permute-start.2 = (f32[6,3,16,128]{3,2,1,0:T(8,128)S(1)}, f32[6,3,16,128]{3,2,1,0:T(8,128)S(1)}, u32[]{:S(2)}, u32[]{:S(2)}) collective-permute-start(f32[6,3,16,128]{3,2,1,0:T(8,128)S(1)} %get-tuple-element.12), channel_id=1, source_target_pairs={{0,1},{1,2},{2,3},{3,0},{4,5},{5,6},{6,7},{7,4},{8,9},{9,10},{10,1... | collective-permute-start | bytes 442376 | tf_op jit(solution)/shard_map/ppermute | solution.py:519
  34.0 20.8 %collective-permute-start.3 = (f32[6,3,16,128]{3,2,1,0:T(8,128)S(1)}, f32[6,3,16,128]{3,2,1,0:T(8,128)S(1)}, u32[]{:S(2)}, u32[]{:S(2)}) collective-permute-start(f32[6,3,16,128]{3,2,1,0:T(8,128)S(1)} %get-tuple-element.13), channel_id=1, source_target_pairs={{0,3},{1,0},{2,1},{3,2},{4,7},{5,4},{6,5},{7,6},{8,11},{9,8},{10,9... | collective-permute-start | bytes 442376 | tf_op jit(solution)/shard_map/ppermute | solution.py:520
  34.0 8.1 %collective-permute-start.4 = (f32[24,256]{1,0:T(8,128)S(1)}, f32[24,256]{1,0:T(8,128)S(1)}, u32[]{:S(2)}, u32[]{:S(2)}) collective-permute-start(f32[24,256]{1,0:T(8,128)S(1)} %get-tuple-element.14), channel_id=1, source_target_pairs={{0,32},{32,64},{64,96},{96,128},{128,160},{160,192},{192,224},{224... | collective-permute-start | bytes 73736 | tf_op jit(solution)/shard_map/ppermute | solution.py:519
  36.5 7.8 %collective-permute-start.6 = (f32[3,64,128]{2,1,0:T(8,128)}, f32[3,64,128]{2,1,0:T(8,128)S(1)}, u32[]{:S(2)}, u32[]{:S(2)}) collective-permute-start(f32[3,64,128]{2,1,0:T(8,128)} %get-tuple-element.23), channel_id=1, source_target_pairs={{0,4},{4,8},{8,12},{12,16},{16,20},{20,24},{24,28},{28,0},{1,5},{5... | collective-permute-start | bytes 294920 | tf_op jit(solution)/shard_map/ppermute | solution.py:519
  38.2 31.0 %copy-start.7 = (f32[8,16,128]{2,1,0:T(8,128)S(1)}, f32[8,16,128]{2,1,0:T(8,128)}, u32[]{:S(2)}) copy-start(f32[8,16,128]{2,1,0:T(8,128)} %constant.33.clone.modes_ref) | copy-start | bytes 196612
  38.2 6.2 %collective-permute-start.7 = (f32[3,64,128]{2,1,0:T(8,128)S(1)}, f32[3,64,128]{2,1,0:T(8,128)S(1)}, u32[]{:S(2)}, u32[]{:S(2)}) collective-permute-start(f32[3,64,128]{2,1,0:T(8,128)S(1)} %get-tuple-element.22), channel_id=1, source_target_pairs={{0,28},{4,0},{8,4},{12,8},{16,12},{20,16},{24,20},{28,24},{1,29},{... | collective-permute-start | bytes 294920 | tf_op jit(solution)/shard_map/ppermute | solution.py:520
  42.2 5.5 %collective-permute-start.5 = (f32[24,256]{1,0:T(8,128)S(1)}, f32[24,256]{1,0:T(8,128)S(1)}, u32[]{:S(2)}, u32[]{:S(2)}) collective-permute-start(f32[24,256]{1,0:T(8,128)S(1)} %get-tuple-element.15), channel_id=1, source_target_pairs={{0,224},{32,0},{64,32},{96,64},{128,96},{160,128},{192,160},{224,1... | collective-permute-start | bytes 73736 | tf_op jit(solution)/shard_map/ppermute | solution.py:520
  44.3 10.5 %collective-permute-start = (f32[6,3,16,128]{3,2,1,0:T(8,128)S(1)}, f32[6,3,16,128]{3,2,1,0:T(8,128)S(1)}, u32[]{:S(2)}, u32[]{:S(2)}) collective-permute-start(f32[6,3,16,128]{3,2,1,0:T(8,128)S(1)} %get-tuple-element.21), channel_id=1, source_target_pairs={{0,4},{4,8},{8,12},{12,16},{16,20},{20,24},{24,28},{28,0},{1,5},{5... | collective-permute-start | bytes 442376 | tf_op jit(solution)/shard_map/ppermute | solution.py:519
  44.3 10.5 %collective-permute-start.1 = (f32[6,3,16,128]{3,2,1,0:T(8,128)S(1)}, f32[6,3,16,128]{3,2,1,0:T(8,128)S(1)}, u32[]{:S(2)}, u32[]{:S(2)}) collective-permute-start(f32[6,3,16,128]{3,2,1,0:T(8,128)S(1)} %get-tuple-element.20), channel_id=1, source_target_pairs={{0,28},{4,0},{8,4},{12,8},{16,12},{20,16},{24,20},{28,24},{1,29},{... | collective-permute-start | bytes 442376 | tf_op jit(solution)/shard_map/ppermute | solution.py:520
  47.7 21.5 %collective-permute-start.8 = (f32[26,8,128]{2,1,0:T(8,128)S(1)}, f32[26,8,128]{2,1,0:T(8,128)S(1)}, u32[]{:S(2)}, u32[]{:S(2)}) collective-permute-start(f32[26,8,128]{2,1,0:T(8,128)S(1)} %get-tuple-element.18), channel_id=1, source_target_pairs={{0,1},{1,2},{2,3},{3,0},{4,5},{5,6},{6,7},{7,4},{8,9},{9,10},{10,1... | collective-permute-start | bytes 319496 | tf_op jit(solution)/shard_map/ppermute | solution.py:519
  54.8 14.4 %collective-permute-start.9 = (f32[26,8,128]{2,1,0:T(8,128)S(1)}, f32[26,8,128]{2,1,0:T(8,128)S(1)}, u32[]{:S(2)}, u32[]{:S(2)}) collective-permute-start(f32[26,8,128]{2,1,0:T(8,128)S(1)} %get-tuple-element.19), channel_id=1, source_target_pairs={{0,3},{1,0},{2,1},{3,2},{4,7},{5,4},{6,5},{7,6},{8,11},{9,8},{10,9... | collective-permute-start | bytes 319496 | tf_op jit(solution)/shard_map/ppermute | solution.py:520

commit v2 on v1

v2 whole, which is shorter than its diff:
```python
import functools
import math

import jax
import jax.numpy as jnp
import ml_dtypes
import numpy as np
from jax import lax
from jax.experimental import pallas as pl
from jax.experimental.pallas import tpu as pltpu
from jax.sharding import PartitionSpec as P

NX = 1024
LANES = 128
BLOCK = 16
PARTS = 8
FULL = (6, BLOCK, BLOCK, LANES)
LINES = 60
ROWS = 64

WEISSENBERG = 20.0
EXTENSIBILITY = 100.0
TIME_STEP = 2.0
EPSILON = 1e-06
COSINES = tuple((math.cos((2 * number + 1) * math.pi / 12.0) for number in range(6)))
QUARTER = NX // 4
VMEM_LIMIT = 16 * 1024 * 1024


def split_bf16(table):
    high = table.astype(np.float32).astype(ml_dtypes.bfloat16)
    low = (table - high.astype(np.float64)).astype(np.float32).astype(ml_dtypes.bfloat16)
    return high, low


def tables():
    ordinal = np.arange(NX)
    wave = np.where(ordinal <= NX // 2, ordinal, ordinal - NX // 2)
    angle = 2.0 * np.pi / NX * ((ordinal[:, None] * wave[None, :]) % NX)
    fourier = -np.where((ordinal <= NX // 2)[None, :], np.cos(angle), np.sin(angle)) * NX**-0.5
    places = []
    for part in range(PARTS):
        start = part * LANES
        places += [start - 2, start - 1, start + LANES, start + LANES + 1]
    high, low = split_bf16(fourier[:QUARTER])
    edge_high, edge_low = split_bf16(fourier[np.array(places) % NX])
    return high, low, np.concatenate([edge_high, edge_high, edge_low])


def mode_table():
    ordinal = np.arange(NX)
    wave = np.where(ordinal <= NX // 2, ordinal, ordinal - NX // 2)
    diagonal = 4.0 + 4.0 * np.sin(np.pi * wave / NX) ** 2
    ratio = 4.0 / diagonal
    upper = 1.0 + ratio
    lower = np.maximum(0.3, 1.0 - ratio)
    rows = []
    for cosine in COSINES:
        omega = 1.0 / (0.5 * (upper + lower) + 0.5 * (upper - lower) * cosine)
        rows += [omega / diagonal, 1.0 - omega]
    modes = np.stack(rows).reshape(12, PARTS, LANES).transpose(1, 0, 2)
    found = np.zeros((PARTS, 8, 4, 24, LANES), np.float32)
    found[:, :, :, 0:12] = modes[:, None, None]
    found[:, 1:, :, 16] = 1.0
    found[:, :7, :, 17] = 1.0
    found[:, :, 1:, 18] = 1.0
    found[:, :, :3, 19] = 1.0
    found[:, :, ::2, 20] = 1.0
    return found.reshape(PARTS * 32, 24, LANES)


def flag(place_ref, number, rows=8):
    return jnp.broadcast_to(place_ref[16 + number : 17 + number], (rows, LANES)) > 0.5


TABLE = tables()
PLACES = mode_table()


def params(limit=VMEM_LIMIT):
    return pltpu.CompilerParams(vmem_limit_bytes=limit)


def cost(microseconds):
    return pl.CostEstimate(
        flops=int(microseconds * 1.1e9), bytes_accessed=int(microseconds * 3.6e6), transcendentals=0
    )


VMEM = pl.BlockSpec(memory_space=pltpu.VMEM)
SMEM = pl.BlockSpec(memory_space=pltpu.SMEM)
HBM = pl.BlockSpec(memory_space=pltpu.HBM)
ANY = pl.BlockSpec(memory_space=pl.ANY)


def dot_nt(left, right):
    return lax.dot_general(left, right, (((1,), (1,)), ((), ())), preferred_element_type=jnp.float32)


def dot_tn(left, right):
    return lax.dot_general(left, right, (((0,), (0,)), ((), ())), preferred_element_type=jnp.float32)


def pieces(value, count):
    found = []
    for _ in range(count):
        found.append(value.astype(jnp.bfloat16))
        value = value - found[-1].astype(jnp.float32)
    return found


def selection(shape, pairs):
    row = lax.broadcasted_iota(jnp.int32, shape, 0)
    column = lax.broadcasted_iota(jnp.int32, shape, 1)
    hit = None
    for first, last, shift in pairs:
        here = (row >= first) & (row <= last) & (column == row + shift)
        hit = here if hit is None else hit | here
    return jnp.where(hit, 1.0, 0.0).astype(jnp.bfloat16)


def sym_square(m):
    a, b, c, d, e, f = m
    bb, cc, ee = b * b, c * c, e * e
    return [
        a * a + bb + cc,
        b * (a + d) + c * e,
        c * (a + f) + b * e,
        bb + d * d + ee,
        e * (d + f) + b * c,
        cc + ee + f * f,
    ]


def sym_times(m, n):
    a, b, c, d, e, f = m
    p, q, r, s, t, u = n
    return [
        a * p + b * q + c * r,
        a * q + b * s + c * t,
        a * r + b * t + c * u,
        b * q + d * s + e * t,
        b * r + d * t + e * u,
        c * r + e * t + f * u,
    ]


DIAG = (1.0, 0.0, 0.0, 1.0, 0.0, 1.0)


def with_diag(m, value):
    return [m[i] + value if DIAG[i] else m[i] for i in range(6)]


def sym_exp(psi):
    m = [0.125 * v for v in psi]
    m2 = sym_square(m)
    m3 = sym_times(m, m2)
    tail = [m[i] * (1.0 / 24) + m2[i] * (1.0 / 120) + m3[i] * (1.0 / 720) for i in range(6)]
    tail = sym_times(m3, with_diag(tail, 1.0 / 6))
    out = with_diag([m[i] + 0.5 * m2[i] + tail[i] for i in range(6)], 1.0)
    for _ in range(3):
        out = sym_square(out)
    return out


def sym_inverse(grown, psi):
    a, b, c, d, e, f = grown
    scale = jnp.exp(-(psi[0] + psi[3] + psi[5]))
    return [
        (d * f - e * e) * scale,
        (c * e - b * f) * scale,
        (b * e - c * d) * scale,
        (a * f - c * c) * scale,
        (b * c - a * e) * scale,
        (a * d - b * b) * scale,
    ]


def spring(grown):
    return (EXTENSIBILITY - 3.0) / (EXTENSIBILITY - (grown[0] + grown[3] + grown[5]))


def source_kernel(psi_ref, send_ref, token_ref, stress, field, wrapped):
    token_ref[...] = jnp.zeros_like(token_ref)
    zero = jnp.zeros((24, LANES), jnp.float32)
    for comp in (1, 3, 4):
        for row in (0, 1, 2, 3, 20, 21, 22, 23):
            stress[comp, row] = zero

    def relax_row(row, carry):
        psi = [psi_ref[comp, row] for comp in range(6)]
        grown = sym_exp(psi)
        peterlin = spring(grown)
        pad = jnp.zeros((8, LANES), jnp.float32)
        for comp in range(6):
            value = peterlin * grown[comp]
            stress[comp, row + 4, 0:16] = value - 1.0 if DIAG[comp] else value
            stress[comp, row + 4, 16:24] = pad
        return carry

    lax.fori_loop(0, BLOCK, relax_row, 0, unroll=EXP_UNROLL)

    lane = lax.broadcasted_iota(jnp.int32, (24, LANES), 1)
    inner = [lane < LANES - 1, lane >= 1, lane < LANES - 2, lane >= 2]

    def along(value, shift):
        return pltpu.roll(value, shift % 24, 0)

    def shifted(value, shift):
        return pltpu.roll(value, shift % LANES, 1)

    def emit(row, plain, once, twice):
        parts = [shifted(once, -1), -shifted(once, 1), shifted(twice, -2), shifted(twice, 2)]
        total = plain - 2.0 * twice
        beyond = zero
        for part, mask in zip(parts, inner):
            kept = jnp.where(mask, part, 0.0)
            total = total + kept
            beyond = beyond + (part - kept)
        at = row * 24 if isinstance(row, int) else pl.multiple_of(row * 24, 8)
        field[pl.ds(at, 24)] = total
        wrapped[pl.ds(at, 24)] = beyond

    def body(row, carry):
        here = row + 2
        s11 = 0.25 * (stress[3, here + 2] - 2.0 * stress[3, here] + stress[3, here - 2])
        u12 = 0.5 * (stress[4, here + 1] - stress[4, here - 1])
        u01 = 0.5 * (stress[1, here + 1] - stress[1, here - 1])
        s22, s02, s00 = stress[5, here], stress[2, here], stress[0, here]
        c22 = 0.25 * (along(s22, -2) - 2.0 * s22 + along(s22, 2))
        c12 = along(u12, -1) - along(u12, 1)
        c02 = 0.5 * (along(s02, -1) - along(s02, 1))
        emit(row, s11 + c22 + c12, u01 + c02, 0.25 * s00)
        return carry

    lax.fori_loop(2, 18, body, 0, unroll=SOURCE_UNROLL)
    for row in (0, 1, 18, 19):
        here = row + 2
        other = here + 2 if row < 2 else here - 2
        s11 = 0.25 * stress[3, other]
        if row in (1, 18):
            near = here + 1 if row == 1 else here - 1
            sign = 0.5 if row == 1 else -0.5
            u12 = sign * stress[4, near]
            u01 = sign * stress[1, near]
            emit(row, s11 + along(u12, -1) - along(u12, 1), u01, zero)
        else:
            emit(row, s11, zero, zero)
    wrapped[480:488] = jnp.zeros((8, LANES), jnp.float32)
    pick = selection((8, 2 * LANES), ((0, 1, 126), (2, 3, -2)))
    pick = pick + selection((8, 2 * LANES), ((0, 1, 126 + LANES), (2, 3, LANES - 2)))
    for part in range(PARTS):
        send_ref[part, 0:LINES] = field[part * LINES : part * LINES + LINES]
        lines = jnp.concatenate(pieces(wrapped[part * LINES : part * LINES + ROWS], 2), axis=1)
        lines = dot_nt(pick, lines)
        send_ref[part, LINES:ROWS, 0:ROWS] = lines[0:4]
        send_ref[part, LINES:ROWS, ROWS:LANES] = jnp.zeros((4, LANES - ROWS), jnp.float32)


EXP_UNROLL = 2
SOURCE_UNROLL = 4


def local_source(psi):
    shape = jax.ShapeDtypeStruct
    return pl.pallas_call(
        source_kernel,
        out_shape=(
            shape((PARTS, ROWS, LANES), jnp.float32),
            shape((8, LANES), jnp.float32),
        ),
        in_specs=[VMEM],
        out_specs=[VMEM] * 2,
        scratch_shapes=[
            pltpu.VMEM((6, 24, 24, LANES), jnp.float32),
            pltpu.VMEM((480, LANES), jnp.float32),
            pltpu.VMEM((488, LANES), jnp.float32),
        ],
        compiler_params=params(),
        cost_estimate=cost(3.0),
        name="local_source",
    )(psi)


def message_kernel(place_ref, psi_ref, after_ref, left_ref, right_ref, first_ref, second_ref, high_ref, low_ref):
    even = flag(place_ref, 4, BLOCK)
    ends = sum(
        (selection((8, 3 * LANES), ((0, 2, k * LANES), (4, 6, k * LANES + 121))) for k in range(1, 3)),
        selection((8, 3 * LANES), ((0, 2, 0), (4, 6, 121))),
    )
    for comp in range(6):
        lines = jnp.concatenate(pieces(psi_ref[comp].reshape(BLOCK * BLOCK, LANES), 3), axis=1)
        found = dot_nt(ends, lines)
        left_ref[comp * 4 : comp * 4 + 4] = found[0:4]
        right_ref[comp * 4 : comp * 4 + 4] = found[4:8]
        for near in range(3):
            down = psi_ref[comp, :, near]
            up = psi_ref[comp, :, BLOCK - 3 + near]
            first_ref[comp, near] = jnp.where(even, up, down)
            second_ref[comp, near] = jnp.where(even, down, up)
            low_ref[comp, near] = psi_ref[comp, near]
            high_ref[comp, near] = psi_ref[comp, BLOCK - 3 + near]


def messages(place, psi, after):
    shape = jax.ShapeDtypeStruct
    return pl.pallas_call(
        message_kernel,
        out_shape=[shape((24, BLOCK * BLOCK), jnp.float32)] * 2
        + [shape((6, 3, BLOCK, LANES), jnp.float32)] * 4,
        in_specs=[VMEM, VMEM, ANY],
        out_specs=[VMEM] * 6,
        compiler_params=params(),
        cost_estimate=cost(4.0),
        name="messages",
    )(place, psi, after)


def transform_kernel(lines_ref, high_ref, low_ref, edge_ref, *rest):
    out_ref = rest[-1]
    quarter = [jnp.concatenate([lines_ref[2 * k], lines_ref[2 * k + 1]], axis=1) for k in range(4)]
    even = [quarter[k] + quarter[k + 2] for k in range(2)]
    odd = [quarter[k] - quarter[k + 2] for k in range(2)]
    high, low = pieces(jnp.concatenate([even[0] + even[1], even[0] - even[1]] + odd, axis=0), 2)
    both = jnp.concatenate([high, low], axis=0)
    edges = jnp.concatenate([lines_ref[part, LINES:ROWS] for part in range(PARTS)], axis=0)
    edges_high, edges_low = pieces(jnp.transpose(edges)[0:ROWS], 2)
    edges = jnp.concatenate([edges_high, edges_low, edges_high], axis=1)
    wide = 2 * LANES
    found = []
    for part in range(4):
        cols = slice(part * wide, (part + 1) * wide)
        first = jnp.dot(both, high_ref[:, cols], preferred_element_type=jnp.float32)
        second = jnp.dot(high, low_ref[:, cols], preferred_element_type=jnp.float32)
        found.append(first[0 : 4 * ROWS] + (first[4 * ROWS :] + second))
    phase = lax.broadcasted_iota(jnp.int32, (ROWS, wide), 1) % 4
    turn = jnp.where(phase == 1, -1.0, 1.0)
    for part in range(4):
        cols = slice(part * wide, (part + 1) * wide)
        beyond = jnp.dot(edges, edge_ref[:, cols], preferred_element_type=jnp.float32)
        crossed = turn * found[(part + 2) % 4][3 * ROWS :]
        straight = found[part][2 * ROWS : 3 * ROWS]
        total = straight + crossed if part < 2 else straight - crossed
        total = jnp.where(phase == 0, found[part][0:ROWS], total)
        total = jnp.where(phase == 2, found[part][ROWS : 2 * ROWS], total) + beyond
        out_ref[2 * part] = total[:, 0:LANES]
        out_ref[2 * part + 1] = total[:, LANES:]


def transform(lines, after):
    return pl.pallas_call(
        transform_kernel,
        out_shape=jax.ShapeDtypeStruct((PARTS, ROWS, LANES), jnp.float32),
        in_specs=[VMEM] * 4 + [ANY] * len(after),
        out_specs=VMEM,
        compiler_params=params(),
        cost_estimate=cost(1.5),
        name="transform",
    )(lines, *(jnp.asarray(table) for table in TABLE), *after)


def radial_kernel(place_ref, own_ref, low_ref, high_ref, after_ref, out_ref, first_ref, second_ref, flat, flat_low, flat_high):
    for part in range(PARTS):
        flat[part * LINES : part * LINES + LINES] = own_ref[part, 0:LINES]
    for part in range(3):
        flat_low[part * LINES + 4 : part * LINES + 4 + LINES] = low_ref[part, 0:LINES]
        flat_high[part * LINES : part * LINES + LINES] = high_ref[part, 0:LINES]
    has_low, has_high = flag(place_ref, 0, 24), flag(place_ref, 1, 24)
    even = flag(place_ref, 4)

    def own(row):
        return flat[row * 24 : row * 24 + 24]

    def low(row):
        at = (row - 13) * 24 + 16
        return jnp.where(has_low, flat_low[at : at + 24], 0.0)

    def high(row):
        return jnp.where(has_high, flat_high[row * 24 : row * 24 + 24], 0.0)

    for row in range(26):
        if row < 3:
            value = low(row + 13)
        elif row < 5:
            value = low(row + 13) + jnp.where(has_low, own(row - 3), 0.0)
        elif row < 7:
            value = low(row + 13) + own(row - 3)
        elif row < 19:
            value = own(row - 3)
        elif row < 21:
            value = own(row - 3) + high(row - 19)
        elif row < 23:
            value = jnp.where(has_high, own(row - 3), 0.0) + high(row - 19)
        else:
            value = high(row - 19)
        out_ref[row] = value
        up = pltpu.roll(value, 24 - 11, 0)[0:8]
        down = pltpu.roll(value, 2, 0)[0:8]
        first_ref[row] = jnp.where(even, up, down)
        second_ref[row] = jnp.where(even, down, up)


def radial_assembly(place, own, low, high, after):
    shape = jax.ShapeDtypeStruct
    return pl.pallas_call(
        radial_kernel,
        out_shape=(
            shape((26, 24, LANES), jnp.float32),
            shape((26, 8, LANES), jnp.float32),
            shape((26, 8, LANES), jnp.float32),
        ),
        in_specs=[VMEM] * 4 + [ANY],
        out_specs=[VMEM] * 3,
        scratch_shapes=[
            pltpu.VMEM((480, LANES), jnp.float32),
            pltpu.VMEM((192, LANES), jnp.float32),
            pltpu.VMEM((184, LANES), jnp.float32),
        ],
        compiler_params=params(),
        cost_estimate=cost(0.6),
        name="radial_assembly",
    )(place, own, low, high, after)


def relax_kernel(place_ref, rows_ref, first_ref, second_ref, *rest):
    whole_ref, out_ref, following_hbm, source, even, odd, sem = rest
    copy = pltpu.make_async_copy(whole_ref, following_hbm, sem)
    copy.start()
    has_low, has_high, even_span = (flag(place_ref, number) for number in (2, 3, 4))
    open_low, open_high = flag(place_ref, 0, 32), flag(place_ref, 1, 32)
    sublane = lax.broadcasted_iota(jnp.int32, (8, LANES), 0)
    always = sublane >= 0
    inside = jnp.concatenate(
        [jnp.where(part, 1.0, 0.0) for part in (always, always, has_high, has_low)], axis=0
    )
    modes = place_ref[0:12]
    weights = [
        inside * jnp.broadcast_to(modes[2 * j : 2 * j + 1], (32, LANES)) for j in range(6)
    ]
    keeps = [jnp.broadcast_to(modes[2 * j + 1 : 2 * j + 2], (32, LANES)) for j in range(6)]
    pad = jnp.zeros((24, LANES), jnp.float32)
    for row in range(26):
        own = rows_ref[row]
        tail = own[16:24]
        own = jnp.concatenate(
            [own[0:16], jnp.where(sublane < 2, tail, 0.0), jnp.where(sublane >= 6, tail, 0.0)], axis=0
        )
        first, other = first_ref[row], second_ref[row]
        low = jnp.where(has_low, jnp.where(even_span, other, first), 0.0)
        high = jnp.where(has_high, jnp.where(even_span, first, other), 0.0)
        low = jnp.concatenate([low, pad], axis=0)
        high = jnp.concatenate([high, pad], axis=0)
        value = own + pltpu.roll(low, 27, 0) + pltpu.roll(high, 14, 0)
        source[row] = value
        value = value * weights[0]
        if row < 5:
            value = jnp.where(open_low, value, 0.0)
        elif row > 20:
            value = jnp.where(open_high, value, 0.0)
        even[row] = value

    old, new = even, odd
    for sweep in range(1, 6):
        weight, keep = weights[sweep], keeps[sweep]
        for row in range(sweep, 26 - sweep):
            middle = old[row]
            beside = (old[row - 1] + old[row + 1]) + (pltpu.roll(middle, 1, 0) + pltpu.roll(middle, 31, 0))
            value = keep * middle + weight * (source[row] + beside)
            if sweep == 5:
                out_ref[row - 5] = value[0:16]
            elif row < 5:
                new[row] = jnp.where(open_low, value, 0.0)
            elif row > 20:
                new[row] = jnp.where(open_high, value, 0.0)
            else:
                new[row] = value
        old, new = new, old
    copy.wait()


def relaxation(place, rows, low, high, whole):
    shape = jax.ShapeDtypeStruct
    return pl.pallas_call(
        relax_kernel,
        out_shape=(
            shape((BLOCK, BLOCK, LANES), jnp.float32),
            shape((6, BLOCK, BLOCK, LANES), jnp.float32),
        ),
        in_specs=[VMEM] * 5,
        out_specs=(VMEM, HBM),
        scratch_shapes=[pltpu.VMEM((26, 32, LANES), jnp.float32)] * 3 + [pltpu.SemaphoreType.DMA],
        compiler_params=params(),
        cost_estimate=cost(1.8),
        name="relaxation",
    )(place, rows, low, high, whole)


def weno(positive, p):
    p0 = jnp.where(positive, p[0], p[4])
    p1 = jnp.where(positive, p[1], p[3])
    p2 = p[2]
    p3 = jnp.where(positive, p[3], p[1])
    k1 = (0.609375 * p1) * p1 + 0.75 * EPSILON
    k2 = (0.609375 * p2) * p2 + 0.75 * EPSILON
    r0 = p0 - 1.375 * p1
    r1 = p1 - 0.625 * p2
    r2 = p3 - 1.375 * p2
    q0, q1, q2 = r0 * r0 + k1, r1 * r1 + k2, r2 * r2 + k2
    q01, q02, q12 = q0 * q1, q0 * q2, q1 * q2
    w0, w1, w2 = q12 * q12, 6.0 * (q02 * q02), 3.0 * (q01 * q01)
    middle = p1 - p2
    t0 = (p0 - p1) - middle
    t2 = middle - (p2 - p3)
    total = (w0 + w1) + w2
    guess = pl_reciprocal(total, approx=True)
    inverse = guess * (2.0 - total * guess)
    return ((w0 + w0) * t0 + w2 * t2) * inverse - p1


pl_reciprocal = pltpu.reciprocal


def wind(velocity_ref, direction, row):
    speed = velocity_ref[direction, row]
    positive = speed > 0
    straight = TIME_STEP * speed
    bent = (TIME_STEP / 6) * jnp.abs(speed)
    return positive, straight, bent, jnp.where(positive, 1.0 / 3, 2.0 / 3)


def advected(blow, behind, p):
    positive, straight, bent, side = blow
    return straight * (behind - side * p[2]) + bent * weno(positive, p)


def stream_kernel(psi_ref, velocity_ref, left_ref, right_ref, *rest):
    out_ref, ahead = rest[-2:]
    spread = []
    for comp in range(6):
        ends = jnp.concatenate([right_ref[comp * 4 : comp * 4 + 4], left_ref[comp * 4 : comp * 4 + 4]], axis=0)
        spread += pieces(ends, 3)
    spread = jnp.concatenate([v.astype(jnp.float32) for v in spread], axis=0)
    spread = jnp.transpose(spread).astype(jnp.bfloat16)
    for comp in range(6):
        pairs = []
        for piece in range(3):
            start = comp * 24 + piece * 8
            pairs += [(start, start + 2, -start), (start + 4, start + 6, 121 - start)]
        found = jnp.dot(spread, selection((144, LANES), pairs), preferred_element_type=jnp.float32)
        ahead[comp] = found.reshape(BLOCK, BLOCK, LANES)
    lane = lax.broadcasted_iota(jnp.int32, (BLOCK, LANES), 1)

    def step(row, carry):
        blow = wind(velocity_ref, 0, row)
        tensor = [psi_ref[comp, row] for comp in range(6)]
        grown = sym_exp(tensor)
        peterlin = spring(grown)
        shrunk = sym_inverse(grown, tensor)
        for comp in range(6):
            back = shrunk[comp] - peterlin if DIAG[comp] else shrunk[comp]
            psi = tensor[comp]
            far = ahead[comp, row]
            lines = []
            for j in range(-3, 4):
                if j > 0:
                    mixed = jnp.where(lane < j, far, psi)
                else:
                    mixed = jnp.where(lane >= LANES + j, far, psi)
                lines.append(pltpu.roll(mixed, (-j) % LANES, 1) if j else psi)
            steps = [lines[j + 1] - lines[j] for j in range(6)]
            change = advected(blow, steps[2], [steps[j] - steps[j + 1] for j in range(5)])
            out_ref[comp, row] = (psi + (TIME_STEP / WEISSENBERG) * back) - change
        return carry

    lax.fori_loop(0, BLOCK, step, 0, unroll=STEP_UNROLL)


def span_kernel(place_ref, psi_ref, velocity_ref, base_ref, first_ref, second_ref, *rest):
    out_ref, column, second = rest[-3:]
    has_down, has_up, even = (flag(place_ref, number, BLOCK) for number in (2, 3, 4))
    for comp in range(6):
        for near in range(3):
            first, other = first_ref[comp, near], second_ref[comp, near]
            column[comp, :, 5 + near] = jnp.where(has_down, jnp.where(even, other, first), 0.0)
            column[comp, :, 24 + near] = jnp.where(has_up, jnp.where(even, first, other), 0.0)

    def bend(row, carry):
        for comp in range(6):
            column[comp, row, 8:24] = psi_ref[comp, row]
            one, two, three = column[comp, row, 5:25], column[comp, row, 6:26], column[comp, row, 7:27]
            second[comp, row, 5:25] = (two - one) - (three - two)
        return carry

    lax.fori_loop(0, BLOCK, bend, 0)

    def step(row, carry):
        blow = wind(velocity_ref, 2, row)
        for comp in range(6):
            behind = psi_ref[comp, row] - column[comp, row, 7:23]
            change = advected(blow, behind, [second[comp, row, 5 + j : 21 + j] for j in range(5)])
            out_ref[comp, row] = base_ref[comp, row] - change
        return carry

    lax.fori_loop(0, BLOCK, step, 0, unroll=STEP_UNROLL)


def radial_kernel_step(place_ref, psi_ref, velocity_ref, base_ref, low_ref, high_ref, *rest):
    out_ref, column, second = rest[-3:]
    has_low, has_high = flag(place_ref, 0, BLOCK), flag(place_ref, 1, BLOCK)
    for comp in range(6):
        for near in range(3):
            column[comp, near] = jnp.where(has_low, low_ref[comp, near], 0.0)
            column[comp, 19 + near] = jnp.where(has_high, high_ref[comp, near], 0.0)

    def copy_in(row, carry):
        for comp in range(6):
            column[comp, row + 3] = psi_ref[comp, row]
        return carry

    lax.fori_loop(0, BLOCK, copy_in, 0)

    def bend(row, carry):
        for comp in range(6):
            one, two, three = column[comp, row], column[comp, row + 1], column[comp, row + 2]
            second[comp, row] = (two - one) - (three - two)
        return carry

    lax.fori_loop(0, 20, bend, 0)

    def step(row, carry):
        blow = wind(velocity_ref, 1, row)
        for comp in range(6):
            behind = column[comp, row + 3] - column[comp, row + 2]
            change = advected(blow, behind, [second[comp, row + j] for j in range(5)])
            out_ref[comp, row] = base_ref[comp, row] - change
        return carry

    lax.fori_loop(0, BLOCK, step, 0, unroll=STEP_UNROLL)


STEP_UNROLL = 1


def advect(kernel, name, scratch, arrays, after):
    return pl.pallas_call(
        kernel,
        out_shape=jax.ShapeDtypeStruct(FULL, jnp.float32),
        in_specs=[VMEM] * len(arrays) + [ANY] * len(after),
        out_specs=VMEM,
        scratch_shapes=[pltpu.VMEM(shape, jnp.float32) for shape in scratch],
        compiler_params=params(),
        cost_estimate=cost(2.5),
        name=name,
    )(*arrays, *after)


def ring(axis, step):
    count = lax.axis_size(axis)
    return [(i, (i + step) % count) for i in range(count)]


def exchange(to_next, to_previous, axis):
    return (
        lax.ppermute(to_next, axis, ring(axis, 1)),
        lax.ppermute(to_previous, axis, ring(axis, -1)),
    )


def trade(first, second, axis):
    count = lax.axis_size(axis)
    inner = [(i, i ^ 1) for i in range(count)]
    outer = [(i, (i - 1) % count if i % 2 == 0 else (i + 1) % count) for i in range(count)]
    return lax.ppermute(first, axis, inner), lax.ppermute(second, axis, outer)


def shards(psi, velocity):
    number = (lax.axis_index("stream") * 8 + lax.axis_index("radial")) * 4 + lax.axis_index("span")
    place = lax.dynamic_index_in_dim(jnp.asarray(PLACES), number, 0, keepdims=False)
    wide = (6, BLOCK, 32, LANES)
    tall = [(6, 22, BLOCK, LANES), (6, 20, BLOCK, LANES)]
    send, token = local_source(psi)
    lines = lax.all_to_all(send, "stream", split_axis=0, concat_axis=0, tiled=True)
    to_left, to_right, to_first, to_second, to_high, to_low = messages(place, psi, token)
    ends = exchange(to_right, to_left, "stream")
    sides = trade(to_first, to_second, "span")
    spectrum = transform(lines, ends)
    own = lax.all_to_all(spectrum, "stream", split_axis=0, concat_axis=0, tiled=True)
    state = advect(stream_kernel, "advect_stream", [FULL], (psi, velocity) + ends, (spectrum,))
    below, above = exchange(own[5:], own[:3], "radial")
    to_high, to_low = lax.optimization_barrier((to_high, to_low, spectrum))[:2]
    walls = exchange(to_high, to_low, "radial")
    state = advect(span_kernel, "advect_span", [wide, wide], (place, psi, velocity, state) + sides, (own,))
    rows, rows_first, rows_second = radial_assembly(place, own, below, above, state)
    first, second = trade(rows_first, rows_second, "span")
    state = advect(radial_kernel_step, "advect_radial", tall, (place, psi, velocity, state) + walls, (rows,))
    modes, following = relaxation(place, rows, first, second, state)
    return following, modes


def solution(mesh):
    return jax.shard_map(
        shards,
        mesh=mesh,
        in_specs=(P(None, "radial", "span", "stream"), P(None, "radial", "span", "stream")),
        out_specs=(P(None, "radial", "span", "stream"), P("radial", "span", "stream")),
        check_vma=False,
    )
```

time: 71.5 us -> 54.1 us (0.76)
  blocking collectives: 11.9 us -> 0 us
  Pallas kernels: 22.8 us -> 13.9 us
  starting transfers between devices: 26.8 us -> 32.1 us
  local copies, waits for them, and re-layouts: 8.05 us -> 2.9 us
  waiting for transfers between devices: 0.64 us -> 4.03 us
    all_to_all x1 -> x0, blocking collectives: 11.9 us -> none  [shards(): lax.all_to_all(send, 'stream', split_axis=0, concat_axis=0, tiled=True)]
    ppermute x5 -> x3, starting transfers between devices: 14.8 us -> 3.18 us  [exchange(): lax.ppermute(to_next, axis, ring(axis, 1))]
    ppermute x0 -> x4, starting transfers between devices: none -> 11.2 us  [trade(): return (lax.ppermute(first, axis, inner), lax.ppermute(second, axis, outer))]
    pallas_call x2 -> x5, Pallas kernels: 16.2 us -> 10 us  [the longest x3 7.98 us: advect(): pl.pallas_call(kernel, out_shape=jax.ShapeDtypeStruct(FULL, jnp.float32),...]
    all_to_all x0 -> x1, starting transfers between devices: none -> 5.86 us  [shards(): lax.all_to_all(send, 'stream', split_axis=0, concat_axis=0, tiled=True)]
    unnamed x22 -> x12, local copies, waits for them, and re-layouts: 7.38 us -> 2.18 us
    ppermute x5 -> x3, waiting for transfers between devices: 0.35 us -> 2.44 us  [exchange(): lax.ppermute(to_next, axis, ring(axis, 1))]
    ppermute x0 -> x4, waiting for transfers between devices: none -> 1.57 us  [trade(): return (lax.ppermute(first, axis, inner), lax.ppermute(second, axis, outer))]
  transfers between devices with their start and end apart: 11 -> 12, of which waited for: 2 -> 2; matrix products, arithmetic and copies ran while one was open for 1% -> 1% of each run, Pallas kernels for 21% -> 18%
where the time goes in v2:
time: 54.1 us; the launch traced here: 53.7 us
  starting transfers between devices  32.1 us (59%)
  Pallas kernels  13.9 us (26%)
  waiting for transfers between devices  4.03 us (7%)
  local copies, waits for them, and re-layouts  2.9 us (5%)
  between operations  0.74 us (1%)
    ppermute x4, starting transfers between devices, trade(): return (lax.ppermute(first, axis, inner), lax.ppermute(second, axis, outer))  11.2 us
    ppermute x3, starting transfers between devices, exchange(): lax.ppermute(to_previous, axis, ring(axis, -1))  8.42 us
    pallas_call x3, Pallas kernels, advect(): pl.pallas_call(kernel, out_shape=jax.ShapeDtypeStruct(FULL, jnp.float32),...  7.98 us
    all_to_all x1, starting transfers between devices, shards(): lax.all_to_all(send, 'stream', split_axis=0, concat_axis=0, tiled=True)  5.86 us
    all_to_all x1, starting transfers between devices, shards(): lax.all_to_all(spectrum, 'stream', split_axis=0, concat_axis=0, tiled=True)  3.41 us
    ppermute x3, starting transfers between devices, exchange(): lax.ppermute(to_next, axis, ring(axis, 1))  3.18 us
    pallas_call x1, Pallas kernels, local_source(): pl.pallas_call(source_kernel, out_shape=(shape((PARTS, ROWS, LANES), jnp....  2.52 us
    ppermute x3, waiting for transfers between devices, exchange(): lax.ppermute(to_next, axis, ring(axis, 1))  2.44 us
  transfers between devices with their start and end apart: 12, of which 2 were waited for; matrix products, arithmetic and copies ran while one was open for 1% of the time, Pallas kernels for 18%

profile of v2, /device:TPU:1, one launch (start us, length us, event | category | flops | bytes accessed | tf_op | source)
XLA Modules:
  0.0 53.7 jit_solution(9403425195051959155)
XLA Ops:
  0.6 1.1 %copy-done = f32[6,16,16,128]{3,2,1,0:T(8,128)S(1)} copy-done((f32[6,16,16,128]{3,2,1,0:T(8,128)S(1)}, f32[6,16,16,128]{3,2,1,0:T(8,128)}, u32[]{:S(2)}) %copy-start) | copy-done | bytes 786456
  1.8 2.5 %local_source.1 = (f32[8,64,128]{2,1,0:T(8,128)}, f32[8,128]{1,0:T(8,128)S(1)}) custom-call(f32[6,16,16,128]{3,2,1,0:T(8,128)S(1)} %copy-done), custom_call_target="tpu_custom_call" | custom-call | flops 3300000000 | bytes 10800000 | tf_op jit(solution)/shard_map/local_source/pallas_call | solution.py:267
  4.3 5.9 %all-to-all-start = ((f32[8,64,128]{2,1,0:T(8,128)}), f32[8,64,128]{2,1,0:T(8,128)S(1)}, u32[]{:S(2)}, u32[]{:S(2)}) async-start(f32[8,64,128]{2,1,0:T(8,128)} %get-tuple-element.17), calls=%async_computation | async-start | bytes 524288 | tf_op jit(solution)/shard_map/all_to_all | solution.py:683
  10.2 0.7 %dynamic-slice_bitcast_fusion.place_ref = f32[24,128]{1,0:T(8,128)S(1)} fusion(f32[256,24,128]{2,1,0:T(8,128)} %constant.31.clone, s32[]{:T(128)S(6)} %select_n.4), kind=kLoop, calls=%fused_computation | loop fusion | bytes 24580 | tf_op jit(solution)/shard_map/jit(dynamic_index_in_dim)/squeeze | solution.py:679
  10.9 0.5 messages.1
  11.4 1.5 %collective-permute-start = (f32[24,256]{1,0:T(8,128)S(1)}, f32[24,256]{1,0:T(8,128)S(1)}, u32[]{:S(2)}, u32[]{:S(2)}) collective-permute-start(f32[24,256]{1,0:T(8,128)S(1)} %get-tuple-element.19), channel_id=1, source_target_pairs={{0,32},{32,64},{64,96},{96,128},{128,160},{160,192},{192,224},{224... | collective-permute-start | bytes 73736 | tf_op jit(solution)/shard_map/ppermute | solution.py:665
  12.8 2.2 %collective-permute-start.1 = (f32[24,256]{1,0:T(8,128)S(1)}, f32[24,256]{1,0:T(8,128)S(1)}, u32[]{:S(2)}, u32[]{:S(2)}) collective-permute-start(f32[24,256]{1,0:T(8,128)S(1)} %get-tuple-element.20), channel_id=1, source_target_pairs={{0,224},{32,0},{64,32},{96,64},{128,96},{160,128},{192,160},{224,1... | collective-permute-start | bytes 73736 | tf_op jit(solution)/shard_map/ppermute | solution.py:666
  15.0 1.5 %collective-permute-start.4 = (f32[6,3,16,128]{3,2,1,0:T(8,128)S(1)}, f32[6,3,16,128]{3,2,1,0:T(8,128)S(1)}, u32[]{:S(2)}, u32[]{:S(2)}) collective-permute-start(f32[6,3,16,128]{3,2,1,0:T(8,128)S(1)} %get-tuple-element.21), channel_id=1, source_target_pairs={{0,1},{1,0},{2,3},{3,2},{4,5},{5,4},{6,7},{7,6},{8,9},{9,8},{10,11... | collective-permute-start | bytes 442376 | tf_op jit(solution)/shard_map/ppermute | solution.py:674
  16.5 2.5 %collective-permute-start.5 = (f32[6,3,16,128]{3,2,1,0:T(8,128)S(1)}, f32[6,3,16,128]{3,2,1,0:T(8,128)S(1)}, u32[]{:S(2)}, u32[]{:S(2)}) collective-permute-start(f32[6,3,16,128]{3,2,1,0:T(8,128)S(1)} %get-tuple-element.22), channel_id=1, source_target_pairs={{0,3},{1,2},{2,1},{3,0},{4,7},{5,6},{6,5},{7,4},{8,11},{9,10},{10,... | collective-permute-start | bytes 442376 | tf_op jit(solution)/shard_map/ppermute | solution.py:674
  19.1 0.0 collective-permute-done.rest_0_.left_ref
  19.1 0.0 collective-permute-done.1.rest_1_.right_ref
  19.1 0.0 all-to-all-done.lines_ref
  19.1 0.0 copy-start.4
  19.1 1.0 %copy-done.4 = bf16[256,1024]{1,0:T(8,128)(2,1)S(1)} copy-done((bf16[256,1024]{1,0:T(8,128)(2,1)S(1)}, bf16[256,1024]{1,0:T(8,128)(2,1)}, u32[]{:S(2)}) %copy-start.4) | copy-done | bytes 524312
  20.1 1.3 %transform.1.rest_0_ = f32[8,64,128]{2,1,0:T(8,128)} custom-call(f32[8,64,128]{2,1,0:T(8,128)S(1)} %all-to-all-done.lines_ref, bf16[256,1024]{1,0:T(8,128)(2,1)S(1)} %copy-done.4, bf16[256,1024]{1,0:T(8,128)(2,1)S(1)} %copy-done.3, bf16[96,1024]{1,0:T(8,128)(2,1)S(1)} %copy-done.5, f32[24,256]{1,0:T(8,128)S(1)} %collective-permute-done.rest_0_.left_ref, ...), custom_call_target="tpu_custom_call" | custom-call | flops 1650000000 | bytes 5400000 | tf_op jit(solution)/shard_map/transform/pallas_call | solution.py:352
  21.5 3.4 %all-to-all-start.1 = ((f32[8,64,128]{2,1,0:T(8,128)}), f32[8,64,128]{2,1,0:T(8,128)S(1)}, u32[]{:S(2)}, u32[]{:S(2)}) async-start(f32[8,64,128]{2,1,0:T(8,128)} %transform.1.rest_0_), calls=%async_computation.1 | async-start | bytes 524288 | tf_op jit(solution)/shard_map/all_to_all | solution.py:688
  24.9 1.7 %collective-permute-start.8 = (f32[6,3,16,128]{3,2,1,0:T(8,128)S(1)}, f32[6,3,16,128]{3,2,1,0:T(8,128)S(1)}, u32[]{:S(2)}, u32[]{:S(2)}) collective-permute-start(f32[6,3,16,128]{3,2,1,0:T(8,128)S(1)} %get-tuple-element.28), channel_id=1, source_target_pairs={{0,4},{4,8},{8,12},{12,16},{16,20},{20,24},{24,28},{28,0},{1,5},{5... | collective-permute-start | bytes 442376 | tf_op jit(solution)/shard_map/ppermute | solution.py:665
  26.6 4.0 %collective-permute-start.9 = (f32[6,3,16,128]{3,2,1,0:T(8,128)S(1)}, f32[6,3,16,128]{3,2,1,0:T(8,128)S(1)}, u32[]{:S(2)}, u32[]{:S(2)}) collective-permute-start(f32[6,3,16,128]{3,2,1,0:T(8,128)S(1)} %get-tuple-element.29), channel_id=1, source_target_pairs={{0,28},{4,0},{8,4},{12,8},{16,12},{20,16},{24,20},{28,24},{1,29},{... | collective-permute-start | bytes 442376 | tf_op jit(solution)/shard_map/ppermute | solution.py:666
  30.6 3.8 %advect_stream.1.base_ref = f32[6,16,16,128]{3,2,1,0:T(8,128)S(1)} custom-call(f32[6,16,16,128]{3,2,1,0:T(8,128)S(1)} %copy-done.1, f32[3,16,16,128]{3,2,1,0:T(8,128)S(1)} %copy-done.2, f32[24,256]{1,0:T(8,128)S(1)} %collective-permute-done.rest_0_.left_ref, f32[24,256]{1,0:T(8,128)S(1)} %collective-permute-done.1.rest_1_.right_ref, ...), custom_call_target="tpu_custom_call" | custom-call | flops 2750000128 | bytes 9000000 | tf_op jit(solution)/shard_map/advect_stream/pallas_call | solution.py:646
  34.4 2.2 %collective-permute-start.3 = (f32[3,64,128]{2,1,0:T(8,128)S(1)}, f32[3,64,128]{2,1,0:T(8,128)S(1)}, u32[]{:S(2)}, u32[]{:S(2)}) collective-permute-start(f32[3,64,128]{2,1,0:T(8,128)S(1)} %get-tuple-element.32), channel_id=1, source_target_pairs={{0,28},{4,0},{8,4},{12,8},{16,12},{20,16},{24,20},{28,24},{1,29},{... | collective-permute-start | bytes 294920 | tf_op jit(solution)/shard_map/ppermute | solution.py:666
  36.6 0.0 collective-permute-done.4.first_ref
  36.6 2.2 %advect_span.1.after_ref.base_ref = f32[6,16,16,128]{3,2,1,0:T(8,128)S(1)} custom-call(f32[24,128]{1,0:T(8,128)S(1)} %dynamic-slice_bitcast_fusion.place_ref, f32[6,16,16,128]{3,2,1,0:T(8,128)S(1)} %copy-done.1, f32[3,16,16,128]{3,2,1,0:T(8,128)S(1)} %copy-done.2, f32[6,16,16,128]{3,2,1,0:T(8,128)S(1)} %advect_stream.1.base_ref, ...), custom_call_target="tpu_custom_call" | custom-call | flops 2750000128 | bytes 9000000 | tf_op jit(solution)/shard_map/advect_span/pallas_call | solution.py:646
  38.9 0.0 collective-permute-done.3.high_ref
  38.9 2.4 %collective-permute-done.2.low_ref = f32[3,64,128]{2,1,0:T(8,128)S(1)} collective-permute-done((f32[3,64,128]{2,1,0:T(8,128)S(1)}, f32[3,64,128]{2,1,0:T(8,128)S(1)}, u32[]{:S(2)}, u32[]{:S(2)}) %collective-permute-start.2) | collective-permute-done | bytes 98336 | tf_op jit(solution)/shard_map/ppermute | solution.py:665
  41.3 0.1 radial_assembly.1
  41.4 4.6 %collective-permute-start.6 = (f32[26,8,128]{2,1,0:T(8,128)S(1)}, f32[26,8,128]{2,1,0:T(8,128)S(1)}, u32[]{:S(2)}, u32[]{:S(2)}) collective-permute-start(f32[26,8,128]{2,1,0:T(8,128)S(1)} %get-tuple-element.24), channel_id=1, source_target_pairs={{0,1},{1,0},{2,3},{3,2},{4,5},{5,4},{6,7},{7,6},{8,9},{9,8},{10,11... | collective-permute-start | bytes 319496 | tf_op jit(solution)/shard_map/ppermute | solution.py:674
  45.9 2.6 %collective-permute-start.7 = (f32[26,8,128]{2,1,0:T(8,128)S(1)}, f32[26,8,128]{2,1,0:T(8,128)S(1)}, u32[]{:S(2)}, u32[]{:S(2)}) collective-permute-start(f32[26,8,128]{2,1,0:T(8,128)S(1)} %get-tuple-element.25), channel_id=1, source_target_pairs={{0,3},{1,2},{2,1},{3,0},{4,7},{5,6},{6,5},{7,4},{8,11},{9,10},{10,... | collective-permute-start | bytes 319496 | tf_op jit(solution)/shard_map/ppermute | solution.py:674
  48.5 0.0 collective-permute-done.8.low_ref
  48.5 0.0 collective-permute-done.9.high_ref
  48.5 2.0 %advect_radial.1.rest_0_ = f32[6,16,16,128]{3,2,1,0:T(8,128)S(1)} custom-call(f32[24,128]{1,0:T(8,128)S(1)} %dynamic-slice_bitcast_fusion.place_ref, f32[6,16,16,128]{3,2,1,0:T(8,128)S(1)} %copy-done.1, f32[3,16,16,128]{3,2,1,0:T(8,128)S(1)} %copy-done.2, f32[6,16,16,128]{3,2,1,0:T(8,128)S(1)} %advect_span.1.after_ref.base_ref, ...), custom_call_target="tpu_custom_call" | custom-call | flops 2750000128 | bytes 9000000 | tf_op jit(solution)/shard_map/advect_radial/pallas_call | solution.py:646
  50.6 1.6 %collective-permute-done.7.second_ref = f32[26,8,128]{2,1,0:T(8,128)S(1)} collective-permute-done((f32[26,8,128]{2,1,0:T(8,128)S(1)}, f32[26,8,128]{2,1,0:T(8,128)S(1)}, u32[]{:S(2)}, u32[]{:S(2)}) %collective-permute-start.7) | collective-permute-done | bytes 106528 | tf_op jit(solution)/shard_map/ppermute | solution.py:674
  52.1 1.5 %relaxation.1 = (f32[16,16,128]{2,1,0:T(8,128)}, f32[6,16,16,128]{3,2,1,0:T(8,128)}) custom-call(f32[24,128]{1,0:T(8,128)S(1)} %dynamic-slice_bitcast_fusion.place_ref, f32[26,24,128]{2,1,0:T(8,128)S(1)} %get-tuple-element.23.rest_0_.rows_ref, f32[26,8,128]{2,1,0:T(8,128)S(1)} %collective-permute-done.6.first_ref, ...), custom_call_target="tpu_custom_call" | custom-call | flops 1980000000 | bytes 6480000 | tf_op jit(solution)/shard_map/relaxation/pallas_call | solution.py:484
  (14 shorter events, 0.0 us)
Async XLA Ops:
  0.6 1.1 %copy-start = (f32[6,16,16,128]{3,2,1,0:T(8,128)S(1)}, f32[6,16,16,128]{3,2,1,0:T(8,128)}, u32[]{:S(2)}) copy-start(f32[6,16,16,128]{3,2,1,0:T(8,128)} %psi_ref.9) | copy-start | bytes 2359300
  1.8 9.1 %copy-start.1 = (f32[6,16,16,128]{3,2,1,0:T(8,128)S(1)}, f32[6,16,16,128]{3,2,1,0:T(8,128)}, u32[]{:S(2)}) copy-start(f32[6,16,16,128]{3,2,1,0:T(8,128)} %psi_ref.9) | copy-start | bytes 2359300
  4.3 14.8 %all-to-all-start = ((f32[8,64,128]{2,1,0:T(8,128)}), f32[8,64,128]{2,1,0:T(8,128)S(1)}, u32[]{:S(2)}, u32[]{:S(2)}) async-start(f32[8,64,128]{2,1,0:T(8,128)} %get-tuple-element.17), calls=%async_computation | async-start | bytes 524288 | tf_op jit(solution)/shard_map/all_to_all | solution.py:683
  10.9 8.2 %copy-start.3 = (bf16[256,1024]{1,0:T(8,128)(2,1)S(1)}, bf16[256,1024]{1,0:T(8,128)(2,1)}, u32[]{:S(2)}) copy-start(bf16[256,1024]{1,0:T(8,128)(2,1)} %constant.33.clone.low_ref) | copy-start | bytes 1572868
  10.9 8.2 %copy-start.5 = (bf16[96,1024]{1,0:T(8,128)(2,1)S(1)}, bf16[96,1024]{1,0:T(8,128)(2,1)}, u32[]{:S(2)}) copy-start(bf16[96,1024]{1,0:T(8,128)(2,1)} %constant.34.clone.edge_ref) | copy-start | bytes 589828
  11.4 7.7 %collective-permute-start = (f32[24,256]{1,0:T(8,128)S(1)}, f32[24,256]{1,0:T(8,128)S(1)}, u32[]{:S(2)}, u32[]{:S(2)}) collective-permute-start(f32[24,256]{1,0:T(8,128)S(1)} %get-tuple-element.19), channel_id=1, source_target_pairs={{0,32},{32,64},{64,96},{96,128},{128,160},{160,192},{192,224},{224... | collective-permute-start | bytes 73736 | tf_op jit(solution)/shard_map/ppermute | solution.py:665
  12.8 6.2 %collective-permute-start.1 = (f32[24,256]{1,0:T(8,128)S(1)}, f32[24,256]{1,0:T(8,128)S(1)}, u32[]{:S(2)}, u32[]{:S(2)}) collective-permute-start(f32[24,256]{1,0:T(8,128)S(1)} %get-tuple-element.20), channel_id=1, source_target_pairs={{0,224},{32,0},{64,32},{96,64},{128,96},{160,128},{192,160},{224,1... | collective-permute-start | bytes 73736 | tf_op jit(solution)/shard_map/ppermute | solution.py:666
  15.0 21.6 %collective-permute-start.4 = (f32[6,3,16,128]{3,2,1,0:T(8,128)S(1)}, f32[6,3,16,128]{3,2,1,0:T(8,128)S(1)}, u32[]{:S(2)}, u32[]{:S(2)}) collective-permute-start(f32[6,3,16,128]{3,2,1,0:T(8,128)S(1)} %get-tuple-element.21), channel_id=1, source_target_pairs={{0,1},{1,0},{2,3},{3,2},{4,5},{5,4},{6,7},{7,6},{8,9},{9,8},{10,11... | collective-permute-start | bytes 442376 | tf_op jit(solution)/shard_map/ppermute | solution.py:674
  16.5 14.1 %copy-start.2 = (f32[3,16,16,128]{3,2,1,0:T(8,128)S(1)}, f32[3,16,16,128]{3,2,1,0:T(8,128)}, u32[]{:S(2)}) copy-start(f32[3,16,16,128]{3,2,1,0:T(8,128)} %velocity_ref.5) | copy-start | bytes 1179652
  16.5 20.1 %collective-permute-start.5 = (f32[6,3,16,128]{3,2,1,0:T(8,128)S(1)}, f32[6,3,16,128]{3,2,1,0:T(8,128)S(1)}, u32[]{:S(2)}, u32[]{:S(2)}) collective-permute-start(f32[6,3,16,128]{3,2,1,0:T(8,128)S(1)} %get-tuple-element.22), channel_id=1, source_target_pairs={{0,3},{1,2},{2,1},{3,0},{4,7},{5,6},{6,5},{7,4},{8,11},{9,10},{10,... | collective-permute-start | bytes 442376 | tf_op jit(solution)/shard_map/ppermute | solution.py:674
  19.1 1.0 %copy-start.4 = (bf16[256,1024]{1,0:T(8,128)(2,1)S(1)}, bf16[256,1024]{1,0:T(8,128)(2,1)}, u32[]{:S(2)}) copy-start(bf16[256,1024]{1,0:T(8,128)(2,1)} %constant.32.clone.high_ref) | copy-start | bytes 1572868
  21.5 12.9 %all-to-all-start.1 = ((f32[8,64,128]{2,1,0:T(8,128)}), f32[8,64,128]{2,1,0:T(8,128)S(1)}, u32[]{:S(2)}, u32[]{:S(2)}) async-start(f32[8,64,128]{2,1,0:T(8,128)} %transform.1.rest_0_), calls=%async_computation.1 | async-start | bytes 524288 | tf_op jit(solution)/shard_map/all_to_all | solution.py:688
  24.9 23.7 %collective-permute-start.8 = (f32[6,3,16,128]{3,2,1,0:T(8,128)S(1)}, f32[6,3,16,128]{3,2,1,0:T(8,128)S(1)}, u32[]{:S(2)}, u32[]{:S(2)}) collective-permute-start(f32[6,3,16,128]{3,2,1,0:T(8,128)S(1)} %get-tuple-element.28), channel_id=1, source_target_pairs={{0,4},{4,8},{8,12},{12,16},{16,20},{20,24},{24,28},{28,0},{1,5},{5... | collective-permute-start | bytes 442376 | tf_op jit(solution)/shard_map/ppermute | solution.py:665
  26.6 22.0 %collective-permute-start.9 = (f32[6,3,16,128]{3,2,1,0:T(8,128)S(1)}, f32[6,3,16,128]{3,2,1,0:T(8,128)S(1)}, u32[]{:S(2)}, u32[]{:S(2)}) collective-permute-start(f32[6,3,16,128]{3,2,1,0:T(8,128)S(1)} %get-tuple-element.29), channel_id=1, source_target_pairs={{0,28},{4,0},{8,4},{12,8},{16,12},{20,16},{24,20},{28,24},{1,29},{... | collective-permute-start | bytes 442376 | tf_op jit(solution)/shard_map/ppermute | solution.py:666
  34.4 4.4 %collective-permute-start.3 = (f32[3,64,128]{2,1,0:T(8,128)S(1)}, f32[3,64,128]{2,1,0:T(8,128)S(1)}, u32[]{:S(2)}, u32[]{:S(2)}) collective-permute-start(f32[3,64,128]{2,1,0:T(8,128)S(1)} %get-tuple-element.32), channel_id=1, source_target_pairs={{0,28},{4,0},{8,4},{12,8},{16,12},{20,16},{24,20},{28,24},{1,29},{... | collective-permute-start | bytes 294920 | tf_op jit(solution)/shard_map/ppermute | solution.py:666
  36.6 4.7 %collective-permute-start.2 = (f32[3,64,128]{2,1,0:T(8,128)S(1)}, f32[3,64,128]{2,1,0:T(8,128)S(1)}, u32[]{:S(2)}, u32[]{:S(2)}) collective-permute-start(f32[3,64,128]{2,1,0:T(8,128)S(1)} %get-tuple-element.33), channel_id=1, source_target_pairs={{0,4},{4,8},{8,12},{12,16},{16,20},{20,24},{24,28},{28,0},{1,5},{5... | collective-permute-start | bytes 294920 | tf_op jit(solution)/shard_map/ppermute | solution.py:665
  41.4 9.2 %collective-permute-start.6 = (f32[26,8,128]{2,1,0:T(8,128)S(1)}, f32[26,8,128]{2,1,0:T(8,128)S(1)}, u32[]{:S(2)}, u32[]{:S(2)}) collective-permute-start(f32[26,8,128]{2,1,0:T(8,128)S(1)} %get-tuple-element.24), channel_id=1, source_target_pairs={{0,1},{1,0},{2,3},{3,2},{4,5},{5,4},{6,7},{7,6},{8,9},{9,8},{10,11... | collective-permute-start | bytes 319496 | tf_op jit(solution)/shard_map/ppermute | solution.py:674
  45.9 6.2 %collective-permute-start.7 = (f32[26,8,128]{2,1,0:T(8,128)S(1)}, f32[26,8,128]{2,1,0:T(8,128)S(1)}, u32[]{:S(2)}, u32[]{:S(2)}) collective-permute-start(f32[26,8,128]{2,1,0:T(8,128)S(1)} %get-tuple-element.25), channel_id=1, source_target_pairs={{0,3},{1,2},{2,1},{3,0},{4,7},{5,6},{6,5},{7,4},{8,11},{9,10},{10,... | collective-permute-start | bytes 319496 | tf_op jit(solution)/shard_map/ppermute | solution.py:674

commit v3 on v2

--- a/solution.py
+++ b/solution.py
@@ -23,8 +23,8 @@
 TIME_STEP = 2.0
 EPSILON = 1e-06
 COSINES = tuple((math.cos((2 * number + 1) * math.pi / 12.0) for number in range(6)))
-QUARTER = NX // 4
 VMEM_LIMIT = 16 * 1024 * 1024
+SOURCE_VMEM = 62 * 1024 * 1024
 
 
 def split_bf16(table):
@@ -38,13 +38,7 @@
     wave = np.where(ordinal <= NX // 2, ordinal, ordinal - NX // 2)
     angle = 2.0 * np.pi / NX * ((ordinal[:, None] * wave[None, :]) % NX)
     fourier = -np.where((ordinal <= NX // 2)[None, :], np.cos(angle), np.sin(angle)) * NX**-0.5
-    places = []
-    for part in range(PARTS):
-        start = part * LANES
-        places += [start - 2, start - 1, start + LANES, start + LANES + 1]
-    high, low = split_bf16(fourier[:QUARTER])
-    edge_high, edge_low = split_bf16(fourier[np.array(places) % NX])
-    return high, low, np.concatenate([edge_high, edge_high, edge_low])
+    return split_bf16(fourier[:LANES])
 
 
 def mode_table():
@@ -181,8 +175,13 @@
     return (EXTENSIBILITY - 3.0) / (EXTENSIBILITY - (grown[0] + grown[3] + grown[5]))
 
 
-def source_kernel(psi_ref, send_ref, token_ref, stress, field, wrapped):
-    token_ref[...] = jnp.zeros_like(token_ref)
+def source_kernel(psi_hbm, send_ref, psi_ref, stress, field, wrapped, sems):
+    chunk = BLOCK // SOURCE_CHUNKS
+    arrivals = []
+    for part in range(SOURCE_CHUNKS):
+        rows = pl.ds(part * chunk, chunk)
+        arrivals.append(pltpu.make_async_copy(psi_hbm.at[:, rows], psi_ref.at[:, rows], sems.at[part]))
+        arrivals[-1].start()
     zero = jnp.zeros((24, LANES), jnp.float32)
     for comp in (1, 3, 4):
         for row in (0, 1, 2, 3, 20, 21, 22, 23):
@@ -199,7 +198,9 @@
             stress[comp, row + 4, 16:24] = pad
         return carry
 
-    lax.fori_loop(0, BLOCK, relax_row, 0, unroll=EXP_UNROLL)
+    for part in range(SOURCE_CHUNKS):
+        arrivals[part].wait()
+        lax.fori_loop(part * chunk, part * chunk + chunk, relax_row, 0, unroll=EXP_UNROLL)
 
     lane = lax.broadcasted_iota(jnp.int32, (24, LANES), 1)
     inner = [lane < LANES - 1, lane >= 1, lane < LANES - 2, lane >= 2]
@@ -259,31 +260,31 @@
 
 
 EXP_UNROLL = 2
-SOURCE_UNROLL = 4
+SOURCE_CHUNKS = 4
+SOURCE_UNROLL = 8
 
 
 def local_source(psi):
     shape = jax.ShapeDtypeStruct
     return pl.pallas_call(
         source_kernel,
-        out_shape=(
-            shape((PARTS, ROWS, LANES), jnp.float32),
-            shape((8, LANES), jnp.float32),
-        ),
-        in_specs=[VMEM],
-        out_specs=[VMEM] * 2,
+        out_shape=shape((PARTS, ROWS, LANES), jnp.float32),
+        in_specs=[HBM],
+        out_specs=VMEM,
         scratch_shapes=[
+            pltpu.VMEM(FULL, jnp.float32),
             pltpu.VMEM((6, 24, 24, LANES), jnp.float32),
             pltpu.VMEM((480, LANES), jnp.float32),
             pltpu.VMEM((488, LANES), jnp.float32),
+            pltpu.SemaphoreType.DMA((SOURCE_CHUNKS,)),
         ],
-        compiler_params=params(),
+        compiler_params=params(SOURCE_VMEM),
         cost_estimate=cost(3.0),
         name="local_source",
     )(psi)
 
 
-def message_kernel(place_ref, psi_ref, after_ref, left_ref, right_ref, first_ref, second_ref, high_ref, low_ref):
+def message_kernel(place_ref, psi_ref, left_ref, right_ref, first_ref, second_ref, high_ref, low_ref):
     even = flag(place_ref, 4, BLOCK)
     ends = sum(
         (selection((8, 3 * LANES), ((0, 2, k * LANES), (4, 6, k * LANES + 121))) for k in range(1, 3)),
@@ -303,47 +304,57 @@
             high_ref[comp, near] = psi_ref[comp, BLOCK - 3 + near]
 
 
-def messages(place, psi, after):
+def messages(place, psi):
     shape = jax.ShapeDtypeStruct
     return pl.pallas_call(
         message_kernel,
         out_shape=[shape((24, BLOCK * BLOCK), jnp.float32)] * 2
         + [shape((6, 3, BLOCK, LANES), jnp.float32)] * 4,
-        in_specs=[VMEM, VMEM, ANY],
+        in_specs=[VMEM, VMEM],
         out_specs=[VMEM] * 6,
         compiler_params=params(),
         cost_estimate=cost(4.0),
         name="messages",
-    )(place, psi, after)
-
-
-def transform_kernel(lines_ref, high_ref, low_ref, edge_ref, *rest):
+    )(place, psi)
+
+
+def transform_kernel(lines_ref, high_ref, low_ref, *rest):
     out_ref = rest[-1]
-    quarter = [jnp.concatenate([lines_ref[2 * k], lines_ref[2 * k + 1]], axis=1) for k in range(4)]
-    even = [quarter[k] + quarter[k + 2] for k in range(2)]
-    odd = [quarter[k] - quarter[k + 2] for k in range(2)]
-    high, low = pieces(jnp.concatenate([even[0] + even[1], even[0] - even[1]] + odd, axis=0), 2)
-    both = jnp.concatenate([high, low], axis=0)
     edges = jnp.concatenate([lines_ref[part, LINES:ROWS] for part in range(PARTS)], axis=0)
-    edges_high, edges_low = pieces(jnp.transpose(edges)[0:ROWS], 2)
-    edges = jnp.concatenate([edges_high, edges_low, edges_high], axis=1)
+    edges = jnp.concatenate(pieces(jnp.transpose(edges)[0:ROWS], 2), axis=1)
+    row = lax.broadcasted_iota(jnp.int32, (8 * PARTS, NX), 0) & (4 * PARTS - 1)
+    lane = lax.broadcasted_iota(jnp.int32, (8 * PARTS, NX), 1)
+    offset = jnp.where((row & 3) < 2, (row & 3) - 2, (row & 3) + LANES - 2)
+    target = ((row >> 2) * LANES + offset + NX) & (NX - 1)
+    target = jnp.where(lane == target, 1.0, 0.0).astype(jnp.bfloat16)
+    beyond = jnp.dot(edges, target, preferred_element_type=jnp.float32)
+    f = [lines_ref[part] + beyond[:, part * LANES : (part + 1) * LANES] for part in range(PARTS)]
+    s = [f[k] + f[k + 4] for k in range(4)]
+    o = [f[k] - f[k + 4] for k in range(4)]
+    half = math.sqrt(0.5)
+    p0, p1, q0, q1 = s[0] + s[2], s[1] + s[3], s[0] - s[2], s[1] - s[3]
+    minus, plus = half * (o[1] - o[3]), half * (o[1] + o[3])
+    left = [p0 + p1, p0 - p1, q0, o[0] + minus, o[0] - minus, q1, plus + o[2], plus - o[2]]
+    high, low = pieces(jnp.concatenate(left, axis=0), 2)
+    both = jnp.concatenate([high, low], axis=1)
     wide = 2 * LANES
     found = []
     for part in range(4):
         cols = slice(part * wide, (part + 1) * wide)
-        first = jnp.dot(both, high_ref[:, cols], preferred_element_type=jnp.float32)
+        table = jnp.concatenate([high_ref[:, cols]] * 2, axis=0)
+        first = jnp.dot(both, table, preferred_element_type=jnp.float32)
         second = jnp.dot(high, low_ref[:, cols], preferred_element_type=jnp.float32)
-        found.append(first[0 : 4 * ROWS] + (first[4 * ROWS :] + second))
-    phase = lax.broadcasted_iota(jnp.int32, (ROWS, wide), 1) % 4
-    turn = jnp.where(phase == 1, -1.0, 1.0)
+        found.append([first[k * ROWS : (k + 1) * ROWS] + second[k * ROWS : (k + 1) * ROWS] for k in range(8)])
+    phase = lax.broadcasted_iota(jnp.int32, (ROWS, wide), 1) % 8
+    outer = (phase == 1) | (phase == 7)
+    middle = phase % 4 == 2
+    turn = jnp.where(phase % 4 == 0, 0.0, jnp.where(phase < 4, 1.0, -1.0))
     for part in range(4):
-        cols = slice(part * wide, (part + 1) * wide)
-        beyond = jnp.dot(edges, edge_ref[:, cols], preferred_element_type=jnp.float32)
-        crossed = turn * found[(part + 2) % 4][3 * ROWS :]
-        straight = found[part][2 * ROWS : 3 * ROWS]
-        total = straight + crossed if part < 2 else straight - crossed
-        total = jnp.where(phase == 0, found[part][0:ROWS], total)
-        total = jnp.where(phase == 2, found[part][ROWS : 2 * ROWS], total) + beyond
+        here, there = found[part], found[(part + 2) % 4]
+        straight = jnp.where(middle, here[2], jnp.where(outer, here[3], here[4]))
+        straight = jnp.where(phase == 0, here[0], jnp.where(phase == 4, here[1], straight))
+        crossed = turn * jnp.where(middle, there[5], jnp.where(outer, there[6], there[7]))
+        total = straight - crossed if part < 2 else straight + crossed
         out_ref[2 * part] = total[:, 0:LANES]
         out_ref[2 * part + 1] = total[:, LANES:]
 
@@ -352,7 +363,7 @@
     return pl.pallas_call(
         transform_kernel,
         out_shape=jax.ShapeDtypeStruct((PARTS, ROWS, LANES), jnp.float32),
-        in_specs=[VMEM] * 4 + [ANY] * len(after),
+        in_specs=[VMEM] * 3 + [ANY] * len(after),
         out_specs=VMEM,
         compiler_params=params(),
         cost_estimate=cost(1.5),
@@ -423,7 +434,7 @@
     )(place, own, low, high, after)
 
 
-def relax_kernel(place_ref, rows_ref, first_ref, second_ref, *rest):
+def relax_kernel(place_ref, rows_ref, second_ref, first_ref, *rest):
     whole_ref, out_ref, following_hbm, source, even, odd, sem = rest
     copy = pltpu.make_async_copy(whole_ref, following_hbm, sem)
     copy.start()
@@ -553,13 +564,8 @@
 
     def step(row, carry):
         blow = wind(velocity_ref, 0, row)
-        tensor = [psi_ref[comp, row] for comp in range(6)]
-        grown = sym_exp(tensor)
-        peterlin = spring(grown)
-        shrunk = sym_inverse(grown, tensor)
         for comp in range(6):
-            back = shrunk[comp] - peterlin if DIAG[comp] else shrunk[comp]
-            psi = tensor[comp]
+            psi = psi_ref[comp, row]
             far = ahead[comp, row]
             lines = []
             for j in range(-3, 4):
@@ -570,7 +576,7 @@
                 lines.append(pltpu.roll(mixed, (-j) % LANES, 1) if j else psi)
             steps = [lines[j + 1] - lines[j] for j in range(6)]
             change = advected(blow, steps[2], [steps[j] - steps[j + 1] for j in range(5)])
-            out_ref[comp, row] = (psi + (TIME_STEP / WEISSENBERG) * back) - change
+            out_ref[comp, row] = psi - change
         return carry
 
     lax.fori_loop(0, BLOCK, step, 0, unroll=STEP_UNROLL)
@@ -630,16 +636,21 @@
 
     def step(row, carry):
         blow = wind(velocity_ref, 1, row)
+        tensor = [psi_ref[comp, row] for comp in range(6)]
+        grown = sym_exp(tensor)
+        peterlin = spring(grown)
+        shrunk = sym_inverse(grown, tensor)
         for comp in range(6):
-            behind = column[comp, row + 3] - column[comp, row + 2]
+            back = shrunk[comp] - peterlin if DIAG[comp] else shrunk[comp]
+            behind = tensor[comp] - column[comp, row + 2]
             change = advected(blow, behind, [second[comp, row + j] for j in range(5)])
-            out_ref[comp, row] = base_ref[comp, row] - change
+            out_ref[comp, row] = (base_ref[comp, row] + (TIME_STEP / WEISSENBERG) * back) - change
         return carry
 
     lax.fori_loop(0, BLOCK, step, 0, unroll=STEP_UNROLL)
 
 
-STEP_UNROLL = 1
+STEP_UNROLL = 2
 
 
 def advect(kernel, name, scratch, arrays, after):
@@ -671,7 +682,8 @@
     count = lax.axis_size(axis)
     inner = [(i, i ^ 1) for i in range(count)]
     outer = [(i, (i - 1) % count if i % 2 == 0 else (i + 1) % count) for i in range(count)]
-    return lax.ppermute(first, axis, inner), lax.ppermute(second, axis, outer)
+    second = lax.ppermute(second, axis, outer)
+    return lax.ppermute(first, axis, inner), second
 
 
 def shards(psi, velocity):
@@ -679,12 +691,13 @@
     place = lax.dynamic_index_in_dim(jnp.asarray(PLACES), number, 0, keepdims=False)
     wide = (6, BLOCK, 32, LANES)
     tall = [(6, 22, BLOCK, LANES), (6, 20, BLOCK, LANES)]
-    send, token = local_source(psi)
+    send = local_source(psi)
+    later, send = lax.optimization_barrier((psi, send))
     lines = lax.all_to_all(send, "stream", split_axis=0, concat_axis=0, tiled=True)
-    to_left, to_right, to_first, to_second, to_high, to_low = messages(place, psi, token)
+    to_left, to_right, to_first, to_second, to_high, to_low = messages(place, later)
     ends = exchange(to_right, to_left, "stream")
     sides = trade(to_first, to_second, "span")
-    spectrum = transform(lines, ends)
+    spectrum = transform(lines, (to_left,))
     own = lax.all_to_all(spectrum, "stream", split_axis=0, concat_axis=0, tiled=True)
     state = advect(stream_kernel, "advect_stream", [FULL], (psi, velocity) + ends, (spectrum,))
     below, above = exchange(own[5:], own[:3], "radial")
@@ -694,7 +707,7 @@
     rows, rows_first, rows_second = radial_assembly(place, own, below, above, state)
     first, second = trade(rows_first, rows_second, "span")
     state = advect(radial_kernel_step, "advect_radial", tall, (place, psi, velocity, state) + walls, (rows,))
-    modes, following = relaxation(place, rows, first, second, state)
+    modes, following = relaxation(place, rows, second, first, state)
     return following, modes
 
 

time: 54.1 us -> 50.1 us (0.926)
  local copies, waits for them, and re-layouts: 2.9 us -> 0.74 us
  starting transfers between devices: 32.1 us -> 30.6 us
  waiting for transfers between devices: 4.03 us -> 2.63 us
  Pallas kernels: 13.9 us -> 15 us
    ppermute x4, starting transfers between devices: 11.2 us -> 7.52 us  [the longest x2 6 us: trade(): second = lax.ppermute(second, axis, outer)]
    ppermute x3, starting transfers between devices: 8.42 us -> 10.6 us  [exchange(): lax.ppermute(to_previous, axis, ring(axis, -1))]
    unnamed x12 -> x8, local copies, waits for them, and re-layouts: 2.18 us -> 0.02 us
    ppermute x4, waiting for transfers between devices: 1.57 us -> 0.01 us  [the longest x2 0.01 us: trade(): return (lax.ppermute(first, axis, inner), second)]
    pallas_call x1, Pallas kernels: 2.52 us -> 3.4 us  [local_source(): pl.pallas_call(source_kernel, out_shape=shape((PARTS, ROWS, LANES), jnp.f...]
  transfers between devices with their start and end apart: 12 -> 12, of which waited for: 2 -> 1; matrix products, arithmetic and copies ran while one was open for 1% -> 1% of each run, Pallas kernels for 18% -> 20%
where the time goes in v3:
time: 50.1 us; the launch traced here: 49.7 us
  starting transfers between devices  30.6 us (61%)
  Pallas kernels  15 us (30%)
  waiting for transfers between devices  2.63 us (5%)
  local copies, waits for them, and re-layouts  0.74 us (1%)
  between operations  0.73 us (1%)
    ppermute x3, starting transfers between devices, exchange(): lax.ppermute(to_previous, axis, ring(axis, -1))  10.6 us
    pallas_call x3, Pallas kernels, advect(): pl.pallas_call(kernel, out_shape=jax.ShapeDtypeStruct(FULL, jnp.float32),...  7.86 us
    ppermute x2, starting transfers between devices, trade(): second = lax.ppermute(second, axis, outer)  6 us
    all_to_all x1, starting transfers between devices, shards(): lax.all_to_all(send, 'stream', split_axis=0, concat_axis=0, tiled=True)  5.87 us
    all_to_all x1, starting transfers between devices, shards(): lax.all_to_all(spectrum, 'stream', split_axis=0, concat_axis=0, tiled=True)  3.41 us
    pallas_call x1, Pallas kernels, local_source(): pl.pallas_call(source_kernel, out_shape=shape((PARTS, ROWS, LANES), jnp.f...  3.4 us
    ppermute x3, starting transfers between devices, exchange(): lax.ppermute(to_next, axis, ring(axis, 1))  3.19 us
    ppermute x3, waiting for transfers between devices, exchange(): lax.ppermute(to_next, axis, ring(axis, 1))  2.6 us
  transfers between devices with their start and end apart: 12, of which 1 were waited for; matrix products, arithmetic and copies ran while one was open for 1% of the time, Pallas kernels for 20%

profile of v3, /device:TPU:1, one launch (start us, length us, event | category | flops | bytes accessed | tf_op | source)
XLA Modules:
  0.0 49.7 jit_solution(16572243250903740900)
XLA Ops:
  0.6 3.4 %local_source.1 = f32[8,64,128]{2,1,0:T(8,128)} custom-call(f32[6,16,16,128]{3,2,1,0:T(8,128)} %psi_ref.6), custom_call_target="tpu_custom_call" | custom-call | flops 3300000000 | bytes 10800000 | tf_op jit(solution)/shard_map/local_source/pallas_call | solution.py:269
  4.0 5.9 %all-to-all-start = ((f32[8,64,128]{2,1,0:T(8,128)}), f32[8,64,128]{2,1,0:T(8,128)S(1)}, u32[]{:S(2)}, u32[]{:S(2)}) async-start(f32[8,64,128]{2,1,0:T(8,128)} %local_source.1), calls=%async_computation | async-start | bytes 524288 | tf_op jit(solution)/shard_map/all_to_all | solution.py:696
  9.9 0.7 %dynamic-slice_bitcast_fusion.place_ref = f32[24,128]{1,0:T(8,128)S(1)} fusion(f32[256,24,128]{2,1,0:T(8,128)} %constant.29.clone, s32[]{:T(128)S(6)} %select_n.4), kind=kLoop, calls=%fused_computation | loop fusion | bytes 24580 | tf_op jit(solution)/shard_map/jit(dynamic_index_in_dim)/squeeze | solution.py:691
  10.6 0.5 messages.1
  11.1 1.5 %collective-permute-start.2 = (f32[24,256]{1,0:T(8,128)S(1)}, f32[24,256]{1,0:T(8,128)S(1)}, u32[]{:S(2)}, u32[]{:S(2)}) collective-permute-start(f32[24,256]{1,0:T(8,128)S(1)} %get-tuple-element.20), channel_id=1, source_target_pairs={{0,32},{32,64},{64,96},{96,128},{128,160},{160,192},{192,224},{224... | collective-permute-start | bytes 73736 | tf_op jit(solution)/shard_map/ppermute | solution.py:676
  12.6 2.2 %collective-permute-start.3 = (f32[24,256]{1,0:T(8,128)S(1)}, f32[24,256]{1,0:T(8,128)S(1)}, u32[]{:S(2)}, u32[]{:S(2)}) collective-permute-start(f32[24,256]{1,0:T(8,128)S(1)} %get-tuple-element.19.rest_0_), channel_id=1, source_target_pairs={{0,224},{32,0},{64,32},{96,64},{128,96},{160,128},{192,160},{224,1... | collective-permute-start | bytes 73736 | tf_op jit(solution)/shard_map/ppermute | solution.py:677
  14.8 1.5 %collective-permute-start.4 = (f32[6,3,16,128]{3,2,1,0:T(8,128)S(1)}, f32[6,3,16,128]{3,2,1,0:T(8,128)S(1)}, u32[]{:S(2)}, u32[]{:S(2)}) collective-permute-start(f32[6,3,16,128]{3,2,1,0:T(8,128)S(1)} %get-tuple-element.21), channel_id=1, source_target_pairs={{0,1},{1,0},{2,3},{3,2},{4,5},{5,4},{6,7},{7,6},{8,9},{9,8},{10,11... | collective-permute-start | bytes 442376 | tf_op jit(solution)/shard_map/ppermute | solution.py:686
  16.3 2.5 %collective-permute-start.5 = (f32[6,3,16,128]{3,2,1,0:T(8,128)S(1)}, f32[6,3,16,128]{3,2,1,0:T(8,128)S(1)}, u32[]{:S(2)}, u32[]{:S(2)}) collective-permute-start(f32[6,3,16,128]{3,2,1,0:T(8,128)S(1)} %get-tuple-element.22), channel_id=1, source_target_pairs={{0,3},{1,2},{2,1},{3,0},{4,7},{5,6},{6,5},{7,4},{8,11},{9,10},{10,... | collective-permute-start | bytes 442376 | tf_op jit(solution)/shard_map/ppermute | solution.py:685
  18.8 0.0 all-to-all-done.lines_ref
  18.8 1.7 %transform.1.rest_0_ = f32[8,64,128]{2,1,0:T(8,128)} custom-call(f32[8,64,128]{2,1,0:T(8,128)S(1)} %all-to-all-done.lines_ref, bf16[128,1024]{1,0:T(8,128)(2,1)S(1)} %copy-done.3, bf16[128,1024]{1,0:T(8,128)(2,1)S(1)} %copy-done.2, f32[24,256]{1,0:T(8,128)S(1)} %get-tuple-element.19.rest_0_), custom_call_target="tpu_custom_call" | custom-call | flops 1650000000 | bytes 5400000 | tf_op jit(solution)/shard_map/transform/pallas_call | solution.py:363
  20.5 3.4 %all-to-all-start.1 = ((f32[8,64,128]{2,1,0:T(8,128)}), f32[8,64,128]{2,1,0:T(8,128)S(1)}, u32[]{:S(2)}, u32[]{:S(2)}) async-start(f32[8,64,128]{2,1,0:T(8,128)} %transform.1.rest_0_), calls=%async_computation.1 | async-start | bytes 524288 | tf_op jit(solution)/shard_map/all_to_all | solution.py:701
  23.9 1.7 %collective-permute-start.8 = (f32[6,3,16,128]{3,2,1,0:T(8,128)S(1)}, f32[6,3,16,128]{3,2,1,0:T(8,128)S(1)}, u32[]{:S(2)}, u32[]{:S(2)}) collective-permute-start(f32[6,3,16,128]{3,2,1,0:T(8,128)S(1)} %get-tuple-element.28), channel_id=1, source_target_pairs={{0,4},{4,8},{8,12},{12,16},{16,20},{20,24},{24,28},{28,0},{1,5},{5... | collective-permute-start | bytes 442376 | tf_op jit(solution)/shard_map/ppermute | solution.py:676
  25.6 0.0 collective-permute-done.2.left_ref
  25.6 4.0 %collective-permute-start.9 = (f32[6,3,16,128]{3,2,1,0:T(8,128)S(1)}, f32[6,3,16,128]{3,2,1,0:T(8,128)S(1)}, u32[]{:S(2)}, u32[]{:S(2)}) collective-permute-start(f32[6,3,16,128]{3,2,1,0:T(8,128)S(1)} %get-tuple-element.29), channel_id=1, source_target_pairs={{0,28},{4,0},{8,4},{12,8},{16,12},{20,16},{24,20},{28,24},{1,29},{... | collective-permute-start | bytes 442376 | tf_op jit(solution)/shard_map/ppermute | solution.py:677
  29.7 0.0 collective-permute-done.3.right_ref
  29.7 2.8 %advect_stream.1.base_ref = f32[6,16,16,128]{3,2,1,0:T(8,128)S(1)} custom-call(f32[6,16,16,128]{3,2,1,0:T(8,128)S(1)} %copy-done, f32[3,16,16,128]{3,2,1,0:T(8,128)S(1)} %copy-done.1, f32[24,256]{1,0:T(8,128)S(1)} %collective-permute-done.2.left_ref, f32[24,256]{1,0:T(8,128)S(1)} %collective-permute-done.3.right_ref, f32[8,64,128]{2,1,0:T(8,128)} %transform.1.rest_0_), custom_call_target="tpu_custom_call" | custom-call | flops 2750000128 | bytes 9000000 | tf_op jit(solution)/shard_map/advect_stream/pallas_call | solution.py:657
  32.5 0.0 all-to-all-done.1.rest_0_.own_ref
  32.6 4.4 %collective-permute-start.1 = (f32[3,64,128]{2,1,0:T(8,128)S(1)}, f32[3,64,128]{2,1,0:T(8,128)S(1)}, u32[]{:S(2)}, u32[]{:S(2)}) collective-permute-start(f32[3,64,128]{2,1,0:T(8,128)S(1)} %get-tuple-element.32), channel_id=1, source_target_pairs={{0,28},{4,0},{8,4},{12,8},{16,12},{20,16},{24,20},{28,24},{1,29},{... | collective-permute-start | bytes 294920 | tf_op jit(solution)/shard_map/ppermute | solution.py:677
  37.0 0.0 collective-permute-done.4.first_ref
  37.0 0.0 collective-permute-start
  37.0 0.0 collective-permute-done.5.second_ref
  37.0 2.1 %advect_span.1.after_ref.base_ref = f32[6,16,16,128]{3,2,1,0:T(8,128)S(1)} custom-call(f32[24,128]{1,0:T(8,128)S(1)} %dynamic-slice_bitcast_fusion.place_ref, f32[6,16,16,128]{3,2,1,0:T(8,128)S(1)} %copy-done, f32[3,16,16,128]{3,2,1,0:T(8,128)S(1)} %copy-done.1, f32[6,16,16,128]{3,2,1,0:T(8,128)S(1)} %advect_stream.1.base_ref, ...), custom_call_target="tpu_custom_call" | custom-call | flops 2750000128 | bytes 9000000 | tf_op jit(solution)/shard_map/advect_span/pallas_call | solution.py:657
  39.0 0.0 collective-permute-done.1.high_ref
  39.0 2.6 %collective-permute-done.low_ref = f32[3,64,128]{2,1,0:T(8,128)S(1)} collective-permute-done((f32[3,64,128]{2,1,0:T(8,128)S(1)}, f32[3,64,128]{2,1,0:T(8,128)S(1)}, u32[]{:S(2)}, u32[]{:S(2)}) %collective-permute-start) | collective-permute-done | bytes 98336 | tf_op jit(solution)/shard_map/ppermute | solution.py:676
  41.6 0.1 radial_assembly.1
  41.7 3.5 %collective-permute-start.6 = (f32[26,8,128]{2,1,0:T(8,128)S(1)}, f32[26,8,128]{2,1,0:T(8,128)S(1)}, u32[]{:S(2)}, u32[]{:S(2)}) collective-permute-start(f32[26,8,128]{2,1,0:T(8,128)S(1)} %get-tuple-element.24), channel_id=1, source_target_pairs={{0,3},{1,2},{2,1},{3,0},{4,7},{5,6},{6,5},{7,4},{8,11},{9,10},{10,... | collective-permute-start | bytes 319496 | tf_op jit(solution)/shard_map/ppermute | solution.py:685
  45.2 0.0 collective-permute-start.7
  45.2 0.0 collective-permute-done.8.low_ref
  45.2 0.0 collective-permute-done.9.high_ref
  45.2 3.0 %advect_radial.1.rest_0_ = f32[6,16,16,128]{3,2,1,0:T(8,128)S(1)} custom-call(f32[24,128]{1,0:T(8,128)S(1)} %dynamic-slice_bitcast_fusion.place_ref, f32[6,16,16,128]{3,2,1,0:T(8,128)S(1)} %copy-done, f32[3,16,16,128]{3,2,1,0:T(8,128)S(1)} %copy-done.1, f32[6,16,16,128]{3,2,1,0:T(8,128)S(1)} %advect_span.1.after_ref.base_ref, ...), custom_call_target="tpu_custom_call" | custom-call | flops 2750000128 | bytes 9000000 | tf_op jit(solution)/shard_map/advect_radial/pallas_call | solution.py:657
  48.2 0.0 collective-permute-done.6.second_ref
  48.2 1.5 %relaxation.1 = (f32[16,16,128]{2,1,0:T(8,128)}, f32[6,16,16,128]{3,2,1,0:T(8,128)}) custom-call(f32[24,128]{1,0:T(8,128)S(1)} %dynamic-slice_bitcast_fusion.place_ref, f32[26,24,128]{2,1,0:T(8,128)S(1)} %get-tuple-element.23.rest_0_.rows_ref, f32[26,8,128]{2,1,0:T(8,128)S(1)} %collective-permute-done.6.second_ref, ...), custom_call_target="tpu_custom_call" | custom-call | flops 1980000000 | bytes 6480000 | tf_op jit(solution)/shard_map/relaxation/pallas_call | solution.py:495
  (10 shorter events, 0.0 us)
Async XLA Ops:
  0.6 10.0 %copy-start = (f32[6,16,16,128]{3,2,1,0:T(8,128)S(1)}, f32[6,16,16,128]{3,2,1,0:T(8,128)}, u32[]{:S(2)}) copy-start(f32[6,16,16,128]{3,2,1,0:T(8,128)} %psi_ref.6) | copy-start | bytes 2359300
  4.0 14.8 %all-to-all-start = ((f32[8,64,128]{2,1,0:T(8,128)}), f32[8,64,128]{2,1,0:T(8,128)S(1)}, u32[]{:S(2)}, u32[]{:S(2)}) async-start(f32[8,64,128]{2,1,0:T(8,128)} %local_source.1), calls=%async_computation | async-start | bytes 524288 | tf_op jit(solution)/shard_map/all_to_all | solution.py:696
  10.6 8.2 %copy-start.2 = (bf16[128,1024]{1,0:T(8,128)(2,1)S(1)}, bf16[128,1024]{1,0:T(8,128)(2,1)}, u32[]{:S(2)}) copy-start(bf16[128,1024]{1,0:T(8,128)(2,1)} %constant.31.clone.low_ref) | copy-start | bytes 786436
  10.6 8.2 %copy-start.3 = (bf16[128,1024]{1,0:T(8,128)(2,1)S(1)}, bf16[128,1024]{1,0:T(8,128)(2,1)}, u32[]{:S(2)}) copy-start(bf16[128,1024]{1,0:T(8,128)(2,1)} %constant.30.clone.high_ref) | copy-start | bytes 786436
  11.1 14.5 %collective-permute-start.2 = (f32[24,256]{1,0:T(8,128)S(1)}, f32[24,256]{1,0:T(8,128)S(1)}, u32[]{:S(2)}, u32[]{:S(2)}) collective-permute-start(f32[24,256]{1,0:T(8,128)S(1)} %get-tuple-element.20), channel_id=1, source_target_pairs={{0,32},{32,64},{64,96},{96,128},{128,160},{160,192},{192,224},{224... | collective-permute-start | bytes 73736 | tf_op jit(solution)/shard_map/ppermute | solution.py:676
  12.6 17.1 %collective-permute-start.3 = (f32[24,256]{1,0:T(8,128)S(1)}, f32[24,256]{1,0:T(8,128)S(1)}, u32[]{:S(2)}, u32[]{:S(2)}) collective-permute-start(f32[24,256]{1,0:T(8,128)S(1)} %get-tuple-element.19.rest_0_), channel_id=1, source_target_pairs={{0,224},{32,0},{64,32},{96,64},{128,96},{160,128},{192,160},{224,1... | collective-permute-start | bytes 73736 | tf_op jit(solution)/shard_map/ppermute | solution.py:677
  14.8 22.2 %collective-permute-start.4 = (f32[6,3,16,128]{3,2,1,0:T(8,128)S(1)}, f32[6,3,16,128]{3,2,1,0:T(8,128)S(1)}, u32[]{:S(2)}, u32[]{:S(2)}) collective-permute-start(f32[6,3,16,128]{3,2,1,0:T(8,128)S(1)} %get-tuple-element.21), channel_id=1, source_target_pairs={{0,1},{1,0},{2,3},{3,2},{4,5},{5,4},{6,7},{7,6},{8,9},{9,8},{10,11... | collective-permute-start | bytes 442376 | tf_op jit(solution)/shard_map/ppermute | solution.py:686
  16.3 13.4 %copy-start.1 = (f32[3,16,16,128]{3,2,1,0:T(8,128)S(1)}, f32[3,16,16,128]{3,2,1,0:T(8,128)}, u32[]{:S(2)}) copy-start(f32[3,16,16,128]{3,2,1,0:T(8,128)} %velocity_ref.5) | copy-start | bytes 1179652
  16.3 20.7 %collective-permute-start.5 = (f32[6,3,16,128]{3,2,1,0:T(8,128)S(1)}, f32[6,3,16,128]{3,2,1,0:T(8,128)S(1)}, u32[]{:S(2)}, u32[]{:S(2)}) collective-permute-start(f32[6,3,16,128]{3,2,1,0:T(8,128)S(1)} %get-tuple-element.22), channel_id=1, source_target_pairs={{0,3},{1,2},{2,1},{3,0},{4,7},{5,6},{6,5},{7,4},{8,11},{9,10},{10,... | collective-permute-start | bytes 442376 | tf_op jit(solution)/shard_map/ppermute | solution.py:685
  20.5 12.0 %all-to-all-start.1 = ((f32[8,64,128]{2,1,0:T(8,128)}), f32[8,64,128]{2,1,0:T(8,128)S(1)}, u32[]{:S(2)}, u32[]{:S(2)}) async-start(f32[8,64,128]{2,1,0:T(8,128)} %transform.1.rest_0_), calls=%async_computation.1 | async-start | bytes 524288 | tf_op jit(solution)/shard_map/all_to_all | solution.py:701
  23.9 21.3 %collective-permute-start.8 = (f32[6,3,16,128]{3,2,1,0:T(8,128)S(1)}, f32[6,3,16,128]{3,2,1,0:T(8,128)S(1)}, u32[]{:S(2)}, u32[]{:S(2)}) collective-permute-start(f32[6,3,16,128]{3,2,1,0:T(8,128)S(1)} %get-tuple-element.28), channel_id=1, source_target_pairs={{0,4},{4,8},{8,12},{12,16},{16,20},{20,24},{24,28},{28,0},{1,5},{5... | collective-permute-start | bytes 442376 | tf_op jit(solution)/shard_map/ppermute | solution.py:676
  25.6 19.6 %collective-permute-start.9 = (f32[6,3,16,128]{3,2,1,0:T(8,128)S(1)}, f32[6,3,16,128]{3,2,1,0:T(8,128)S(1)}, u32[]{:S(2)}, u32[]{:S(2)}) collective-permute-start(f32[6,3,16,128]{3,2,1,0:T(8,128)S(1)} %get-tuple-element.29), channel_id=1, source_target_pairs={{0,28},{4,0},{8,4},{12,8},{16,12},{20,16},{24,20},{28,24},{1,29},{... | collective-permute-start | bytes 442376 | tf_op jit(solution)/shard_map/ppermute | solution.py:677
  32.6 6.5 %collective-permute-start.1 = (f32[3,64,128]{2,1,0:T(8,128)S(1)}, f32[3,64,128]{2,1,0:T(8,128)S(1)}, u32[]{:S(2)}, u32[]{:S(2)}) collective-permute-start(f32[3,64,128]{2,1,0:T(8,128)S(1)} %get-tuple-element.32), channel_id=1, source_target_pairs={{0,28},{4,0},{8,4},{12,8},{16,12},{20,16},{24,20},{28,24},{1,29},{... | collective-permute-start | bytes 294920 | tf_op jit(solution)/shard_map/ppermute | solution.py:677
  37.0 4.7 %collective-permute-start = (f32[3,64,128]{2,1,0:T(8,128)S(1)}, f32[3,64,128]{2,1,0:T(8,128)S(1)}, u32[]{:S(2)}, u32[]{:S(2)}) collective-permute-start(f32[3,64,128]{2,1,0:T(8,128)S(1)} %get-tuple-element.33), channel_id=1, source_target_pairs={{0,4},{4,8},{8,12},{12,16},{16,20},{20,24},{24,28},{28,0},{1,5},{5... | collective-permute-start | bytes 294920 | tf_op jit(solution)/shard_map/ppermute | solution.py:676
  41.7 6.5 %collective-permute-start.6 = (f32[26,8,128]{2,1,0:T(8,128)S(1)}, f32[26,8,128]{2,1,0:T(8,128)S(1)}, u32[]{:S(2)}, u32[]{:S(2)}) collective-permute-start(f32[26,8,128]{2,1,0:T(8,128)S(1)} %get-tuple-element.24), channel_id=1, source_target_pairs={{0,3},{1,2},{2,1},{3,0},{4,7},{5,6},{6,5},{7,4},{8,11},{9,10},{10,... | collective-permute-start | bytes 319496 | tf_op jit(solution)/shard_map/ppermute | solution.py:685
  45.2 3.0 %collective-permute-start.7 = (f32[26,8,128]{2,1,0:T(8,128)S(1)}, f32[26,8,128]{2,1,0:T(8,128)S(1)}, u32[]{:S(2)}, u32[]{:S(2)}) collective-permute-start(f32[26,8,128]{2,1,0:T(8,128)S(1)} %get-tuple-element.25), channel_id=1, source_target_pairs={{0,1},{1,0},{2,3},{3,2},{4,5},{5,4},{6,7},{7,6},{8,9},{9,8},{10,11... | collective-permute-start | bytes 319496 | tf_op jit(solution)/shard_map/ppermute | solution.py:686

commit v4 on v3

--- a/solution.py
+++ b/solution.py
@@ -52,23 +52,16 @@
     for cosine in COSINES:
         omega = 1.0 / (0.5 * (upper + lower) + 0.5 * (upper - lower) * cosine)
         rows += [omega / diagonal, 1.0 - omega]
-    modes = np.stack(rows).reshape(12, PARTS, LANES).transpose(1, 0, 2)
-    found = np.zeros((PARTS, 8, 4, 24, LANES), np.float32)
-    found[:, :, :, 0:12] = modes[:, None, None]
-    found[:, 1:, :, 16] = 1.0
-    found[:, :7, :, 17] = 1.0
-    found[:, :, 1:, 18] = 1.0
-    found[:, :, :3, 19] = 1.0
-    found[:, :, ::2, 20] = 1.0
-    return found.reshape(PARTS * 32, 24, LANES)
+    rows += [np.zeros(NX)] * 4
+    return np.stack(rows).astype(np.float32).reshape(16, PARTS, LANES).transpose(1, 0, 2)
 
 
 def flag(place_ref, number, rows=8):
-    return jnp.broadcast_to(place_ref[16 + number : 17 + number], (rows, LANES)) > 0.5
+    return jnp.broadcast_to(place_ref[number : number + 1], (rows, LANES)) > 0.5
 
 
 TABLE = tables()
-PLACES = mode_table()
+MODES = mode_table()
 
 
 def params(limit=VMEM_LIMIT):
@@ -371,12 +364,43 @@
     )(lines, *(jnp.asarray(table) for table in TABLE), *after)
 
 
+def radial_message_kernel(own_ref, up_ref, down_ref):
+    def copy(to, at, line, count):
+        while count:
+            part, row = divmod(line, LINES)
+            some = min(count, LINES - row)
+            to[at : at + some] = own_ref[part, row : row + some]
+            at, line, count = at + some, line + some, count - some
+
+    for k in range(7):
+        for to, row in ((down_ref, k), (up_ref, k + 13)):
+            copy(to, k * 20, row * 24, 18)
+            copy(to, k * 20 + 18, row * 24 + 22, 2)
+    for to in (down_ref, up_ref):
+        to[140:144] = jnp.zeros((4, LANES), jnp.float32)
+
+
+def radial_messages(own):
+    return pl.pallas_call(
+        radial_message_kernel,
+        out_shape=[jax.ShapeDtypeStruct((144, LANES), jnp.float32)] * 2,
+        in_specs=[VMEM],
+        out_specs=[VMEM] * 2,
+        compiler_params=params(),
+        cost_estimate=cost(0.3),
+        name="radial_messages",
+    )(own)
+
+
 def radial_kernel(place_ref, own_ref, low_ref, high_ref, after_ref, out_ref, first_ref, second_ref, flat, flat_low, flat_high):
     for part in range(PARTS):
         flat[part * LINES : part * LINES + LINES] = own_ref[part, 0:LINES]
-    for part in range(3):
-        flat_low[part * LINES + 4 : part * LINES + 4 + LINES] = low_ref[part, 0:LINES]
-        flat_high[part * LINES : part * LINES + LINES] = high_ref[part, 0:LINES]
+    flat_low[...] = jnp.zeros_like(flat_low)
+    flat_high[...] = jnp.zeros_like(flat_high)
+    for k in range(7):
+        for to, message in ((flat_low, low_ref), (flat_high, high_ref)):
+            to[k * 24 : k * 24 + 18] = message[k * 20 : k * 20 + 18]
+            to[k * 24 + 22 : k * 24 + 24] = message[k * 20 + 18 : k * 20 + 20]
     has_low, has_high = flag(place_ref, 0, 24), flag(place_ref, 1, 24)
     even = flag(place_ref, 4)
 
@@ -384,7 +408,7 @@
         return flat[row * 24 : row * 24 + 24]
 
     def low(row):
-        at = (row - 13) * 24 + 16
+        at = (row - 13) * 24
         return jnp.where(has_low, flat_low[at : at + 24], 0.0)
 
     def high(row):
@@ -425,8 +449,8 @@
         out_specs=[VMEM] * 3,
         scratch_shapes=[
             pltpu.VMEM((480, LANES), jnp.float32),
-            pltpu.VMEM((192, LANES), jnp.float32),
-            pltpu.VMEM((184, LANES), jnp.float32),
+            pltpu.VMEM((168, LANES), jnp.float32),
+            pltpu.VMEM((168, LANES), jnp.float32),
         ],
         compiler_params=params(),
         cost_estimate=cost(0.6),
@@ -434,7 +458,7 @@
     )(place, own, low, high, after)
 
 
-def relax_kernel(place_ref, rows_ref, second_ref, first_ref, *rest):
+def relax_kernel(place_ref, modes_ref, rows_ref, second_ref, first_ref, *rest):
     whole_ref, out_ref, following_hbm, source, even, odd, sem = rest
     copy = pltpu.make_async_copy(whole_ref, following_hbm, sem)
     copy.start()
@@ -445,7 +469,7 @@
     inside = jnp.concatenate(
         [jnp.where(part, 1.0, 0.0) for part in (always, always, has_high, has_low)], axis=0
     )
-    modes = place_ref[0:12]
+    modes = sum(modes_ref[k] * jnp.broadcast_to(place_ref[8 + k : 9 + k], (16, LANES)) for k in range(PARTS))
     weights = [
         inside * jnp.broadcast_to(modes[2 * j : 2 * j + 1], (32, LANES)) for j in range(6)
     ]
@@ -498,13 +522,13 @@
             shape((BLOCK, BLOCK, LANES), jnp.float32),
             shape((6, BLOCK, BLOCK, LANES), jnp.float32),
         ),
-        in_specs=[VMEM] * 5,
+        in_specs=[VMEM] * 6,
         out_specs=(VMEM, HBM),
         scratch_shapes=[pltpu.VMEM((26, 32, LANES), jnp.float32)] * 3 + [pltpu.SemaphoreType.DMA],
         compiler_params=params(),
         cost_estimate=cost(1.8),
         name="relaxation",
-    )(place, rows, low, high, whole)
+    )(place, jnp.asarray(MODES), rows, low, high, whole)
 
 
 def weno(positive, p):
@@ -553,12 +577,15 @@
         spread += pieces(ends, 3)
     spread = jnp.concatenate([v.astype(jnp.float32) for v in spread], axis=0)
     spread = jnp.transpose(spread).astype(jnp.bfloat16)
+    place = selection((8, LANES), ((0, 2, 0), (4, 6, 121))).astype(jnp.float32)
     for comp in range(6):
-        pairs = []
-        for piece in range(3):
-            start = comp * 24 + piece * 8
-            pairs += [(start, start + 2, -start), (start + 4, start + 6, 121 - start)]
-        found = jnp.dot(spread, selection((144, LANES), pairs), preferred_element_type=jnp.float32)
+        rows = [place] * 3
+        if comp > 0:
+            rows = [jnp.zeros((comp * 24, LANES), jnp.float32)] + rows
+        if comp < 5:
+            rows = rows + [jnp.zeros((120 - comp * 24, LANES), jnp.float32)]
+        rows = jnp.concatenate(rows, axis=0).astype(jnp.bfloat16)
+        found = jnp.dot(spread, rows, preferred_element_type=jnp.float32)
         ahead[comp] = found.reshape(BLOCK, BLOCK, LANES)
     lane = lax.broadcasted_iota(jnp.int32, (BLOCK, LANES), 1)
 
@@ -687,8 +714,11 @@
 
 
 def shards(psi, velocity):
-    number = (lax.axis_index("stream") * 8 + lax.axis_index("radial")) * 4 + lax.axis_index("span")
-    place = lax.dynamic_index_in_dim(jnp.asarray(PLACES), number, 0, keepdims=False)
+    radial, span = lax.axis_index("radial"), lax.axis_index("span")
+    bits = (radial > 0) + 2 * (radial < 7) + 4 * (span > 0) + 8 * (span < 3) + 16 * (span % 2 == 0)
+    number = lax.broadcasted_iota(jnp.int32, (16, LANES), 0)
+    place = ((bits >> number) & (number < 8)) | (number == lax.axis_index("stream") + 8)
+    place = place.astype(jnp.float32)
     wide = (6, BLOCK, 32, LANES)
     tall = [(6, 22, BLOCK, LANES), (6, 20, BLOCK, LANES)]
     send = local_source(psi)
@@ -700,15 +730,15 @@
     spectrum = transform(lines, (to_left,))
     own = lax.all_to_all(spectrum, "stream", split_axis=0, concat_axis=0, tiled=True)
     state = advect(stream_kernel, "advect_stream", [FULL], (psi, velocity) + ends, (spectrum,))
-    below, above = exchange(own[5:], own[:3], "radial")
+    below, above = exchange(*radial_messages(own), "radial")
     to_high, to_low = lax.optimization_barrier((to_high, to_low, spectrum))[:2]
     walls = exchange(to_high, to_low, "radial")
     state = advect(span_kernel, "advect_span", [wide, wide], (place, psi, velocity, state) + sides, (own,))
     rows, rows_first, rows_second = radial_assembly(place, own, below, above, state)
     first, second = trade(rows_first, rows_second, "span")
     state = advect(radial_kernel_step, "advect_radial", tall, (place, psi, velocity, state) + walls, (rows,))
-    modes, following = relaxation(place, rows, second, first, state)
-    return following, modes
+    pressure, following = relaxation(place, rows, second, first, state)
+    return following, pressure
 
 
 def solution(mesh):

time: 50.1 us -> 47.3 us (0.944)
  waiting for transfers between devices: 2.63 us -> 0.58 us
  local copies, waits for them, and re-layouts: 0.74 us -> 0.09 us
    ppermute x3, waiting for transfers between devices: 2.6 us -> 0.01 us  [exchange(): lax.ppermute(to_next, axis, ring(axis, 1))]
    squeeze x1 -> x0, local copies, waits for them, and re-layouts: 0.71 us -> none  [shards(): lax.dynamic_index_in_dim(jnp.asarray(PLACES), number, 0, keepdims=False)]
    ppermute x2, waiting for transfers between devices: 0.01 us -> 0.55 us  [trade(): second = lax.ppermute(second, axis, outer)]
  transfers between devices with their start and end apart: 12 -> 12, of which waited for: 1 -> 1; matrix products, arithmetic and copies ran while one was open for 1% -> 0% of each run, Pallas kernels for 20% -> 22%
where the time goes in v4:
time: 47.3 us; the launch traced here: 47 us
  starting transfers between devices  30.5 us (64%)
  Pallas kernels  15.1 us (32%)
  between operations  0.73 us (2%)
  waiting for transfers between devices  0.58 us (1%)
    ppermute x3, starting transfers between devices, exchange(): lax.ppermute(to_previous, axis, ring(axis, -1))  10.3 us
    pallas_call x3, Pallas kernels, advect(): pl.pallas_call(kernel, out_shape=jax.ShapeDtypeStruct(FULL, jnp.float32),...  7.87 us
    all_to_all x1, starting transfers between devices, shards(): lax.all_to_all(send, 'stream', split_axis=0, concat_axis=0, tiled=True)  5.87 us
    ppermute x2, starting transfers between devices, trade(): second = lax.ppermute(second, axis, outer)  5.63 us
    ppermute x3, starting transfers between devices, exchange(): lax.ppermute(to_next, axis, ring(axis, 1))  3.65 us
    all_to_all x1, starting transfers between devices, shards(): lax.all_to_all(spectrum, 'stream', split_axis=0, concat_axis=0, tiled=True)  3.54 us
    pallas_call x1, Pallas kernels, local_source(): pl.pallas_call(source_kernel, out_shape=shape((PARTS, ROWS, LANES), jnp.f...  3.4 us
    pallas_call x1, Pallas kernels, transform(): pl.pallas_call(transform_kernel, out_shape=jax.ShapeDtypeStruct((PARTS, R...  1.7 us
  transfers between devices with their start and end apart: 12, of which 1 were waited for; matrix products, arithmetic and copies ran while one was open for 0% of the time, Pallas kernels for 22%

profile of v4, /device:TPU:1, one launch (start us, length us, event | category | flops | bytes accessed | tf_op | source)
XLA Modules:
  0.0 47.0 jit_solution(12020344630228818446)
XLA Ops:
  0.6 3.4 %local_source.1 = f32[8,64,128]{2,1,0:T(8,128)} custom-call(f32[6,16,16,128]{3,2,1,0:T(8,128)} %psi_ref.6), custom_call_target="tpu_custom_call" | custom-call | flops 3300000000 | bytes 10800000 | tf_op jit(solution)/shard_map/local_source/pallas_call | solution.py:262
  4.0 5.9 %all-to-all-start = ((f32[8,64,128]{2,1,0:T(8,128)}), f32[8,64,128]{2,1,0:T(8,128)S(1)}, u32[]{:S(2)}, u32[]{:S(2)}) async-start(f32[8,64,128]{2,1,0:T(8,128)} %local_source.1), calls=%async_computation | async-start | bytes 524288 | tf_op jit(solution)/shard_map/all_to_all | solution.py:726
  9.9 0.1 iota.13.place_ref
  10.0 0.5 messages.1
  10.5 1.5 %collective-permute-start.2 = (f32[24,256]{1,0:T(8,128)S(1)}, f32[24,256]{1,0:T(8,128)S(1)}, u32[]{:S(2)}, u32[]{:S(2)}) collective-permute-start(f32[24,256]{1,0:T(8,128)S(1)} %get-tuple-element.24), channel_id=1, source_target_pairs={{0,32},{32,64},{64,96},{96,128},{128,160},{160,192},{192,224},{224... | collective-permute-start | bytes 73736 | tf_op jit(solution)/shard_map/ppermute | solution.py:703
  11.9 2.2 %collective-permute-start.3 = (f32[24,256]{1,0:T(8,128)S(1)}, f32[24,256]{1,0:T(8,128)S(1)}, u32[]{:S(2)}, u32[]{:S(2)}) collective-permute-start(f32[24,256]{1,0:T(8,128)S(1)} %get-tuple-element.21.rest_0_), channel_id=1, source_target_pairs={{0,224},{32,0},{64,32},{96,64},{128,96},{160,128},{192,160},{224,1... | collective-permute-start | bytes 73736 | tf_op jit(solution)/shard_map/ppermute | solution.py:704
  14.2 1.5 %collective-permute-start.4 = (f32[6,3,16,128]{3,2,1,0:T(8,128)S(1)}, f32[6,3,16,128]{3,2,1,0:T(8,128)S(1)}, u32[]{:S(2)}, u32[]{:S(2)}) collective-permute-start(f32[6,3,16,128]{3,2,1,0:T(8,128)S(1)} %get-tuple-element.25), channel_id=1, source_target_pairs={{0,1},{1,0},{2,3},{3,2},{4,5},{5,4},{6,7},{7,6},{8,9},{9,8},{10,11... | collective-permute-start | bytes 442376 | tf_op jit(solution)/shard_map/ppermute | solution.py:713
  15.7 2.5 %collective-permute-start.5 = (f32[6,3,16,128]{3,2,1,0:T(8,128)S(1)}, f32[6,3,16,128]{3,2,1,0:T(8,128)S(1)}, u32[]{:S(2)}, u32[]{:S(2)}) collective-permute-start(f32[6,3,16,128]{3,2,1,0:T(8,128)S(1)} %get-tuple-element.26), channel_id=1, source_target_pairs={{0,3},{1,2},{2,1},{3,0},{4,7},{5,6},{6,5},{7,4},{8,11},{9,10},{10,... | collective-permute-start | bytes 442376 | tf_op jit(solution)/shard_map/ppermute | solution.py:712
  18.2 0.0 all-to-all-done.lines_ref
  18.2 1.7 %transform.1.rest_0_ = f32[8,64,128]{2,1,0:T(8,128)} custom-call(f32[8,64,128]{2,1,0:T(8,128)S(1)} %all-to-all-done.lines_ref, bf16[128,1024]{1,0:T(8,128)(2,1)S(1)} %copy-done.3, bf16[128,1024]{1,0:T(8,128)(2,1)S(1)} %copy-done.2, f32[24,256]{1,0:T(8,128)S(1)} %get-tuple-element.21.rest_0_), custom_call_target="tpu_custom_call" | custom-call | flops 1650000000 | bytes 5400000 | tf_op jit(solution)/shard_map/transform/pallas_call | solution.py:356
  19.9 3.5 %all-to-all-start.1 = ((f32[8,64,128]{2,1,0:T(8,128)}), f32[8,64,128]{2,1,0:T(8,128)S(1)}, u32[]{:S(2)}, u32[]{:S(2)}) async-start(f32[8,64,128]{2,1,0:T(8,128)} %transform.1.rest_0_), calls=%async_computation.1 | async-start | bytes 524288 | tf_op jit(solution)/shard_map/all_to_all | solution.py:731
  23.4 1.7 %collective-permute-start.8 = (f32[6,3,16,128]{3,2,1,0:T(8,128)S(1)}, f32[6,3,16,128]{3,2,1,0:T(8,128)S(1)}, u32[]{:S(2)}, u32[]{:S(2)}) collective-permute-start(f32[6,3,16,128]{3,2,1,0:T(8,128)S(1)} %get-tuple-element.32), channel_id=1, source_target_pairs={{0,4},{4,8},{8,12},{12,16},{16,20},{20,24},{24,28},{28,0},{1,5},{5... | collective-permute-start | bytes 442376 | tf_op jit(solution)/shard_map/ppermute | solution.py:703
  25.2 0.0 collective-permute-done.2.left_ref
  25.2 4.0 %collective-permute-start.9 = (f32[6,3,16,128]{3,2,1,0:T(8,128)S(1)}, f32[6,3,16,128]{3,2,1,0:T(8,128)S(1)}, u32[]{:S(2)}, u32[]{:S(2)}) collective-permute-start(f32[6,3,16,128]{3,2,1,0:T(8,128)S(1)} %get-tuple-element.33), channel_id=1, source_target_pairs={{0,28},{4,0},{8,4},{12,8},{16,12},{20,16},{24,20},{28,24},{1,29},{... | collective-permute-start | bytes 442376 | tf_op jit(solution)/shard_map/ppermute | solution.py:704
  29.2 0.0 collective-permute-done.3.right_ref
  29.2 2.8 %advect_stream.1.base_ref = f32[6,16,16,128]{3,2,1,0:T(8,128)S(1)} custom-call(f32[6,16,16,128]{3,2,1,0:T(8,128)S(1)} %copy-done, f32[3,16,16,128]{3,2,1,0:T(8,128)S(1)} %copy-done.1, f32[24,256]{1,0:T(8,128)S(1)} %collective-permute-done.2.left_ref, f32[24,256]{1,0:T(8,128)S(1)} %collective-permute-done.3.right_ref, f32[8,64,128]{2,1,0:T(8,128)} %transform.1.rest_0_), custom_call_target="tpu_custom_call" | custom-call | flops 2750000128 | bytes 9000000 | tf_op jit(solution)/shard_map/advect_stream/pallas_call | solution.py:684
  32.0 0.0 all-to-all-done.1.own_ref.rest_0_
  32.1 0.5 collective-permute-start
  32.5 0.0 collective-permute-done.4.first_ref
  32.5 4.0 %collective-permute-start.1 = (f32[144,128]{1,0:T(8,128)S(1)}, f32[144,128]{1,0:T(8,128)S(1)}, u32[]{:S(2)}, u32[]{:S(2)}) collective-permute-start(f32[144,128]{1,0:T(8,128)S(1)} %get-tuple-element.23), channel_id=1, source_target_pairs={{0,28},{4,0},{8,4},{12,8},{16,12},{20,16},{24,20},{28,24},{1,29},{... | collective-permute-start | bytes 221192 | tf_op jit(solution)/shard_map/ppermute | solution.py:704
  36.6 0.0 collective-permute-done.5.second_ref
  36.6 2.1 %advect_span.1.after_ref.base_ref = f32[6,16,16,128]{3,2,1,0:T(8,128)S(1)} custom-call(f32[16,128]{1,0:T(8,128)S(1)} %iota.13.place_ref, f32[6,16,16,128]{3,2,1,0:T(8,128)S(1)} %copy-done, f32[3,16,16,128]{3,2,1,0:T(8,128)S(1)} %copy-done.1, f32[6,16,16,128]{3,2,1,0:T(8,128)S(1)} %advect_stream.1.base_ref, ...), custom_call_target="tpu_custom_call" | custom-call | flops 2750000128 | bytes 9000000 | tf_op jit(solution)/shard_map/advect_span/pallas_call | solution.py:684
  38.6 0.0 collective-permute-done.1.high_ref
  38.7 0.1 radial_assembly.1
  38.7 3.1 %collective-permute-start.6 = (f32[26,8,128]{2,1,0:T(8,128)S(1)}, f32[26,8,128]{2,1,0:T(8,128)S(1)}, u32[]{:S(2)}, u32[]{:S(2)}) collective-permute-start(f32[26,8,128]{2,1,0:T(8,128)S(1)} %get-tuple-element.28), channel_id=1, source_target_pairs={{0,3},{1,2},{2,1},{3,0},{4,7},{5,6},{6,5},{7,4},{8,11},{9,10},{10,... | collective-permute-start | bytes 319496 | tf_op jit(solution)/shard_map/ppermute | solution.py:712
  41.9 0.0 collective-permute-done.8.low_ref
  41.9 0.0 collective-permute-done.9.high_ref
  41.9 0.0 copy-start.4
  41.9 3.0 %advect_radial.1.rest_0_ = f32[6,16,16,128]{3,2,1,0:T(8,128)S(1)} custom-call(f32[16,128]{1,0:T(8,128)S(1)} %iota.13.place_ref, f32[6,16,16,128]{3,2,1,0:T(8,128)S(1)} %copy-done, f32[3,16,16,128]{3,2,1,0:T(8,128)S(1)} %copy-done.1, f32[6,16,16,128]{3,2,1,0:T(8,128)S(1)} %advect_span.1.after_ref.base_ref, ...), custom_call_target="tpu_custom_call" | custom-call | flops 2750000128 | bytes 9000000 | tf_op jit(solution)/shard_map/advect_radial/pallas_call | solution.py:684
  44.9 0.5 %collective-permute-done.6.second_ref = f32[26,8,128]{2,1,0:T(8,128)S(1)} collective-permute-done((f32[26,8,128]{2,1,0:T(8,128)S(1)}, f32[26,8,128]{2,1,0:T(8,128)S(1)}, u32[]{:S(2)}, u32[]{:S(2)}) %collective-permute-start.6) | collective-permute-done | bytes 106528 | tf_op jit(solution)/shard_map/ppermute | solution.py:712
  45.4 0.0 collective-permute-done.7.first_ref
  45.4 1.5 %relaxation.1 = (f32[16,16,128]{2,1,0:T(8,128)}, f32[6,16,16,128]{3,2,1,0:T(8,128)}) custom-call(f32[16,128]{1,0:T(8,128)S(1)} %iota.13.place_ref, f32[8,16,128]{2,1,0:T(8,128)S(1)} %copy-done.4, f32[26,24,128]{2,1,0:T(8,128)S(1)} %get-tuple-element.27.rest_0_.rows_ref, f32[26,8,128]{2,1,0:T(8,128)S(1)} %collective-permute-done.6.second_ref, ...), custom_call_target="tpu_custom_call" | custom-call | flops 1980000000 | bytes 6480000 | tf_op jit(solution)/shard_map/relaxation/pallas_call | solution.py:519
  (13 shorter events, 0.0 us)
Async XLA Ops:
  0.6 9.4 %copy-start = (f32[6,16,16,128]{3,2,1,0:T(8,128)S(1)}, f32[6,16,16,128]{3,2,1,0:T(8,128)}, u32[]{:S(2)}) copy-start(f32[6,16,16,128]{3,2,1,0:T(8,128)} %psi_ref.6) | copy-start | bytes 2359300
  4.0 14.1 %all-to-all-start = ((f32[8,64,128]{2,1,0:T(8,128)}), f32[8,64,128]{2,1,0:T(8,128)S(1)}, u32[]{:S(2)}, u32[]{:S(2)}) async-start(f32[8,64,128]{2,1,0:T(8,128)} %local_source.1), calls=%async_computation | async-start | bytes 524288 | tf_op jit(solution)/shard_map/all_to_all | solution.py:726
  10.0 8.2 %copy-start.2 = (bf16[128,1024]{1,0:T(8,128)(2,1)S(1)}, bf16[128,1024]{1,0:T(8,128)(2,1)}, u32[]{:S(2)}) copy-start(bf16[128,1024]{1,0:T(8,128)(2,1)} %constant.49.clone.low_ref) | copy-start | bytes 786436
  10.0 8.2 %copy-start.3 = (bf16[128,1024]{1,0:T(8,128)(2,1)S(1)}, bf16[128,1024]{1,0:T(8,128)(2,1)}, u32[]{:S(2)}) copy-start(bf16[128,1024]{1,0:T(8,128)(2,1)} %constant.48.clone.high_ref) | copy-start | bytes 786436
  10.5 14.7 %collective-permute-start.2 = (f32[24,256]{1,0:T(8,128)S(1)}, f32[24,256]{1,0:T(8,128)S(1)}, u32[]{:S(2)}, u32[]{:S(2)}) collective-permute-start(f32[24,256]{1,0:T(8,128)S(1)} %get-tuple-element.24), channel_id=1, source_target_pairs={{0,32},{32,64},{64,96},{96,128},{128,160},{160,192},{192,224},{224... | collective-permute-start | bytes 73736 | tf_op jit(solution)/shard_map/ppermute | solution.py:703
  11.9 17.2 %collective-permute-start.3 = (f32[24,256]{1,0:T(8,128)S(1)}, f32[24,256]{1,0:T(8,128)S(1)}, u32[]{:S(2)}, u32[]{:S(2)}) collective-permute-start(f32[24,256]{1,0:T(8,128)S(1)} %get-tuple-element.21.rest_0_), channel_id=1, source_target_pairs={{0,224},{32,0},{64,32},{96,64},{128,96},{160,128},{192,160},{224,1... | collective-permute-start | bytes 73736 | tf_op jit(solution)/shard_map/ppermute | solution.py:704
  14.2 18.4 %collective-permute-start.4 = (f32[6,3,16,128]{3,2,1,0:T(8,128)S(1)}, f32[6,3,16,128]{3,2,1,0:T(8,128)S(1)}, u32[]{:S(2)}, u32[]{:S(2)}) collective-permute-start(f32[6,3,16,128]{3,2,1,0:T(8,128)S(1)} %get-tuple-element.25), channel_id=1, source_target_pairs={{0,1},{1,0},{2,3},{3,2},{4,5},{5,4},{6,7},{7,6},{8,9},{9,8},{10,11... | collective-permute-start | bytes 442376 | tf_op jit(solution)/shard_map/ppermute | solution.py:713
  15.7 20.9 %collective-permute-start.5 = (f32[6,3,16,128]{3,2,1,0:T(8,128)S(1)}, f32[6,3,16,128]{3,2,1,0:T(8,128)S(1)}, u32[]{:S(2)}, u32[]{:S(2)}) collective-permute-start(f32[6,3,16,128]{3,2,1,0:T(8,128)S(1)} %get-tuple-element.26), channel_id=1, source_target_pairs={{0,3},{1,2},{2,1},{3,0},{4,7},{5,6},{6,5},{7,4},{8,11},{9,10},{10,... | collective-permute-start | bytes 442376 | tf_op jit(solution)/shard_map/ppermute | solution.py:712
  19.9 9.3 %copy-start.1 = (f32[3,16,16,128]{3,2,1,0:T(8,128)S(1)}, f32[3,16,16,128]{3,2,1,0:T(8,128)}, u32[]{:S(2)}) copy-start(f32[3,16,16,128]{3,2,1,0:T(8,128)} %velocity_ref.5) | copy-start | bytes 1179652
  19.9 12.2 %all-to-all-start.1 = ((f32[8,64,128]{2,1,0:T(8,128)}), f32[8,64,128]{2,1,0:T(8,128)S(1)}, u32[]{:S(2)}, u32[]{:S(2)}) async-start(f32[8,64,128]{2,1,0:T(8,128)} %transform.1.rest_0_), calls=%async_computation.1 | async-start | bytes 524288 | tf_op jit(solution)/shard_map/all_to_all | solution.py:731
  23.4 18.4 %collective-permute-start.8 = (f32[6,3,16,128]{3,2,1,0:T(8,128)S(1)}, f32[6,3,16,128]{3,2,1,0:T(8,128)S(1)}, u32[]{:S(2)}, u32[]{:S(2)}) collective-permute-start(f32[6,3,16,128]{3,2,1,0:T(8,128)S(1)} %get-tuple-element.32), channel_id=1, source_target_pairs={{0,4},{4,8},{8,12},{12,16},{16,20},{20,24},{24,28},{28,0},{1,5},{5... | collective-permute-start | bytes 442376 | tf_op jit(solution)/shard_map/ppermute | solution.py:703
  25.2 16.7 %collective-permute-start.9 = (f32[6,3,16,128]{3,2,1,0:T(8,128)S(1)}, f32[6,3,16,128]{3,2,1,0:T(8,128)S(1)}, u32[]{:S(2)}, u32[]{:S(2)}) collective-permute-start(f32[6,3,16,128]{3,2,1,0:T(8,128)S(1)} %get-tuple-element.33), channel_id=1, source_target_pairs={{0,28},{4,0},{8,4},{12,8},{16,12},{20,16},{24,20},{28,24},{1,29},{... | collective-permute-start | bytes 442376 | tf_op jit(solution)/shard_map/ppermute | solution.py:704
  32.1 6.6 %collective-permute-start = (f32[144,128]{1,0:T(8,128)S(1)}, f32[144,128]{1,0:T(8,128)S(1)}, u32[]{:S(2)}, u32[]{:S(2)}) collective-permute-start(f32[144,128]{1,0:T(8,128)S(1)} %get-tuple-element.22), channel_id=1, source_target_pairs={{0,4},{4,8},{8,12},{12,16},{16,20},{20,24},{24,28},{28,0},{1,5},{5... | collective-permute-start | bytes 221192 | tf_op jit(solution)/shard_map/ppermute | solution.py:703
  32.5 6.1 %collective-permute-start.1 = (f32[144,128]{1,0:T(8,128)S(1)}, f32[144,128]{1,0:T(8,128)S(1)}, u32[]{:S(2)}, u32[]{:S(2)}) collective-permute-start(f32[144,128]{1,0:T(8,128)S(1)} %get-tuple-element.23), channel_id=1, source_target_pairs={{0,28},{4,0},{8,4},{12,8},{16,12},{20,16},{24,20},{28,24},{1,29},{... | collective-permute-start | bytes 221192 | tf_op jit(solution)/shard_map/ppermute | solution.py:704
  38.7 6.7 %collective-permute-start.6 = (f32[26,8,128]{2,1,0:T(8,128)S(1)}, f32[26,8,128]{2,1,0:T(8,128)S(1)}, u32[]{:S(2)}, u32[]{:S(2)}) collective-permute-start(f32[26,8,128]{2,1,0:T(8,128)S(1)} %get-tuple-element.28), channel_id=1, source_target_pairs={{0,3},{1,2},{2,1},{3,0},{4,7},{5,6},{6,5},{7,4},{8,11},{9,10},{10,... | collective-permute-start | bytes 319496 | tf_op jit(solution)/shard_map/ppermute | solution.py:712
  41.9 3.5 %collective-permute-start.7 = (f32[26,8,128]{2,1,0:T(8,128)S(1)}, f32[26,8,128]{2,1,0:T(8,128)S(1)}, u32[]{:S(2)}, u32[]{:S(2)}) collective-permute-start(f32[26,8,128]{2,1,0:T(8,128)S(1)} %get-tuple-element.29), channel_id=1, source_target_pairs={{0,1},{1,0},{2,3},{3,2},{4,5},{5,4},{6,7},{7,6},{8,9},{9,8},{10,11... | collective-permute-start | bytes 319496 | tf_op jit(solution)/shard_map/ppermute | solution.py:713
  41.9 3.5 %copy-start.4 = (f32[8,16,128]{2,1,0:T(8,128)S(1)}, f32[8,16,128]{2,1,0:T(8,128)}, u32[]{:S(2)}) copy-start(f32[8,16,128]{2,1,0:T(8,128)} %constant.50.clone.modes_ref) | copy-start | bytes 196612

commit v5 on v4

--- a/solution.py
+++ b/solution.py
@@ -459,59 +459,77 @@
 
 
 def relax_kernel(place_ref, modes_ref, rows_ref, second_ref, first_ref, *rest):
-    whole_ref, out_ref, following_hbm, source, even, odd, sem = rest
-    copy = pltpu.make_async_copy(whole_ref, following_hbm, sem)
-    copy.start()
+    whole_ref, out_hbm, following_hbm, out_ref, source, one, two, sems = rest
+    copies = [pltpu.make_async_copy(whole_ref, following_hbm, sems.at[0])]
+    copies[0].start()
     has_low, has_high, even_span = (flag(place_ref, number) for number in (2, 3, 4))
     open_low, open_high = flag(place_ref, 0, 32), flag(place_ref, 1, 32)
     sublane = lax.broadcasted_iota(jnp.int32, (8, LANES), 0)
     always = sublane >= 0
     inside = jnp.concatenate(
-        [jnp.where(part, 1.0, 0.0) for part in (always, always, has_high, has_low)], axis=0
+        [jnp.where(part, 1.0, 0.0) for part in (has_low, always, always, has_high)], axis=0
     )
     modes = sum(modes_ref[k] * jnp.broadcast_to(place_ref[8 + k : 9 + k], (16, LANES)) for k in range(PARTS))
-    weights = [
-        inside * jnp.broadcast_to(modes[2 * j : 2 * j + 1], (32, LANES)) for j in range(6)
-    ]
+    weights = [inside * jnp.broadcast_to(modes[2 * j : 2 * j + 1], (32, LANES)) for j in range(6)]
     keeps = [jnp.broadcast_to(modes[2 * j + 1 : 2 * j + 2], (32, LANES)) for j in range(6)]
-    pad = jnp.zeros((24, LANES), jnp.float32)
+    pad = jnp.zeros((8, LANES), jnp.float32)
+
+    def walled(row, value):
+        if row < 5:
+            return jnp.where(open_low, value, 0.0)
+        if row > 20:
+            return jnp.where(open_high, value, 0.0)
+        return value
+
     for row in range(26):
         own = rows_ref[row]
         tail = own[16:24]
-        own = jnp.concatenate(
-            [own[0:16], jnp.where(sublane < 2, tail, 0.0), jnp.where(sublane >= 6, tail, 0.0)], axis=0
-        )
         first, other = first_ref[row], second_ref[row]
         low = jnp.where(has_low, jnp.where(even_span, other, first), 0.0)
         high = jnp.where(has_high, jnp.where(even_span, first, other), 0.0)
-        low = jnp.concatenate([low, pad], axis=0)
-        high = jnp.concatenate([high, pad], axis=0)
-        value = own + pltpu.roll(low, 27, 0) + pltpu.roll(high, 14, 0)
+        low = pltpu.roll(low, 3, 0)
+        high = pltpu.roll(high, 6, 0)
+        value = jnp.concatenate(
+            [
+                jnp.where(sublane >= 6, tail, 0.0) + jnp.where(sublane >= 3, low, 0.0),
+                own[0:8] + jnp.where(sublane < 3, low, 0.0),
+                own[8:16] + jnp.where(sublane >= 6, high, 0.0),
+                jnp.where(sublane < 2, tail, 0.0) + jnp.where(sublane < 6, high, 0.0),
+            ],
+            axis=0,
+        )
         source[row] = value
-        value = value * weights[0]
-        if row < 5:
-            value = jnp.where(open_low, value, 0.0)
-        elif row > 20:
-            value = jnp.where(open_high, value, 0.0)
-        even[row] = value
-
-    old, new = even, odd
+        one[row, 8:40] = walled(row, value * weights[0])
+        for buffer in (one, two):
+            buffer[row, 0:8] = pad
+            buffer[row, 40:48] = pad
+
+    old, new = one, two
     for sweep in range(1, 6):
         weight, keep = weights[sweep], keeps[sweep]
         for row in range(sweep, 26 - sweep):
-            middle = old[row]
-            beside = (old[row - 1] + old[row + 1]) + (pltpu.roll(middle, 1, 0) + pltpu.roll(middle, 31, 0))
-            value = keep * middle + weight * (source[row] + beside)
             if sweep == 5:
-                out_ref[row - 5] = value[0:16]
-            elif row < 5:
-                new[row] = jnp.where(open_low, value, 0.0)
-            elif row > 20:
-                new[row] = jnp.where(open_high, value, 0.0)
+                at, weight_here, keep_here, here = 16, weight[8:24], keep[8:24], source[row, 8:24]
             else:
-                new[row] = value
+                at, weight_here, keep_here, here = 8, weight, keep, source[row]
+            end = 32 if sweep == 5 else 40
+            beside = (old[row - 1, at:end] + old[row + 1, at:end]) + (
+                old[row, at - 1 : end - 1] + old[row, at + 1 : end + 1]
+            )
+            value = keep_here * old[row, at:end] + weight_here * (here + beside)
+            if sweep == 5:
+                out_ref[row - 5] = value
+                if row % 8 == 4:
+                    rows = pl.ds(row - 12, 8)
+                    copies.append(
+                        pltpu.make_async_copy(out_ref.at[rows], out_hbm.at[rows], sems.at[len(copies)])
+                    )
+                    copies[-1].start()
+            else:
+                new[row, 8:40] = walled(row, value)
         old, new = new, old
-    copy.wait()
+    for copy in copies:
+        copy.wait()
 
 
 def relaxation(place, rows, low, high, whole):
@@ -523,8 +541,14 @@
             shape((6, BLOCK, BLOCK, LANES), jnp.float32),
         ),
         in_specs=[VMEM] * 6,
-        out_specs=(VMEM, HBM),
-        scratch_shapes=[pltpu.VMEM((26, 32, LANES), jnp.float32)] * 3 + [pltpu.SemaphoreType.DMA],
+        out_specs=(HBM, HBM),
+        scratch_shapes=[
+            pltpu.VMEM((BLOCK, BLOCK, LANES), jnp.float32),
+            pltpu.VMEM((26, 32, LANES), jnp.float32),
+            pltpu.VMEM((26, 48, LANES), jnp.float32),
+            pltpu.VMEM((26, 48, LANES), jnp.float32),
+            pltpu.SemaphoreType.DMA((3,)),
+        ],
         compiler_params=params(),
         cost_estimate=cost(1.8),
         name="relaxation",

time: 47.3 us -> 46.9 us (level)
  no operation moved by 1% of the time
where the time goes in v5:
time: 46.9 us; the launch traced here: 46.6 us
  starting transfers between devices  30.5 us (65%)
  Pallas kernels  14.7 us (31%)
  between operations  0.73 us (2%)
  waiting for transfers between devices  0.58 us (1%)
    ppermute x3, starting transfers between devices, exchange(): lax.ppermute(to_previous, axis, ring(axis, -1))  10.3 us
    pallas_call x3, Pallas kernels, advect(): pl.pallas_call(kernel, out_shape=jax.ShapeDtypeStruct(FULL, jnp.float32),...  7.87 us
    all_to_all x1, starting transfers between devices, shards(): lax.all_to_all(send, 'stream', split_axis=0, concat_axis=0, tiled=True)  5.87 us
    ppermute x2, starting transfers between devices, trade(): second = lax.ppermute(second, axis, outer)  5.63 us
    ppermute x3, starting transfers between devices, exchange(): lax.ppermute(to_next, axis, ring(axis, 1))  3.65 us
    all_to_all x1, starting transfers between devices, shards(): lax.all_to_all(spectrum, 'stream', split_axis=0, concat_axis=0, tiled=True)  3.54 us
    pallas_call x1, Pallas kernels, local_source(): pl.pallas_call(source_kernel, out_shape=shape((PARTS, ROWS, LANES), jnp.f...  3.4 us
    pallas_call x1, Pallas kernels, transform(): pl.pallas_call(transform_kernel, out_shape=jax.ShapeDtypeStruct((PARTS, R...  1.7 us
  transfers between devices with their start and end apart: 12, of which 1 were waited for; matrix products, arithmetic and copies ran while one was open for 0% of the time, Pallas kernels for 22%

profile of v5, /device:TPU:1, one launch (start us, length us, event | category | flops | bytes accessed | tf_op | source)
XLA Modules:
  0.0 46.6 jit_solution(12531940046199334545)
XLA Ops:
  0.6 3.4 %local_source.1 = f32[8,64,128]{2,1,0:T(8,128)} custom-call(f32[6,16,16,128]{3,2,1,0:T(8,128)} %psi_ref.6), custom_call_target="tpu_custom_call" | custom-call | flops 3300000000 | bytes 10800000 | tf_op jit(solution)/shard_map/local_source/pallas_call | solution.py:262
  4.0 5.9 %all-to-all-start = ((f32[8,64,128]{2,1,0:T(8,128)}), f32[8,64,128]{2,1,0:T(8,128)S(1)}, u32[]{:S(2)}, u32[]{:S(2)}) async-start(f32[8,64,128]{2,1,0:T(8,128)} %local_source.1), calls=%async_computation | async-start | bytes 524288 | tf_op jit(solution)/shard_map/all_to_all | solution.py:750
  9.9 0.1 iota.13.place_ref
  10.0 0.5 %messages.1 = (f32[24,256]{1,0:T(8,128)S(1)}, f32[24,256]{1,0:T(8,128)S(1)}, f32[6,3,16,128]{3,2,1,0:T(8,128)S(1)}, f32[6,3,16,128]{3,2,1,0:T(8,128)S(1)}, f32[6...) custom-call(f32[16,128]{1,0:T(8,128)S(1)} %iota.13.place_ref, f32[6,16,16,128]{3,2,1,0:T(8,128)S(1)} %copy-done), custom_call_target="tpu_custom_call" | custom-call | flops 4400000000 | bytes 14400000 | tf_op jit(solution)/shard_map/messages/pallas_call | solution.py:302
  10.5 1.5 %collective-permute-start.2 = (f32[24,256]{1,0:T(8,128)S(1)}, f32[24,256]{1,0:T(8,128)S(1)}, u32[]{:S(2)}, u32[]{:S(2)}) collective-permute-start(f32[24,256]{1,0:T(8,128)S(1)} %get-tuple-element.24), channel_id=1, source_target_pairs={{0,32},{32,64},{64,96},{96,128},{128,160},{160,192},{192,224},{224... | collective-permute-start | bytes 73736 | tf_op jit(solution)/shard_map/ppermute | solution.py:727
  11.9 2.2 %collective-permute-start.3 = (f32[24,256]{1,0:T(8,128)S(1)}, f32[24,256]{1,0:T(8,128)S(1)}, u32[]{:S(2)}, u32[]{:S(2)}) collective-permute-start(f32[24,256]{1,0:T(8,128)S(1)} %get-tuple-element.21.rest_0_), channel_id=1, source_target_pairs={{0,224},{32,0},{64,32},{96,64},{128,96},{160,128},{192,160},{224,1... | collective-permute-start | bytes 73736 | tf_op jit(solution)/shard_map/ppermute | solution.py:728
  14.2 1.5 %collective-permute-start.4 = (f32[6,3,16,128]{3,2,1,0:T(8,128)S(1)}, f32[6,3,16,128]{3,2,1,0:T(8,128)S(1)}, u32[]{:S(2)}, u32[]{:S(2)}) collective-permute-start(f32[6,3,16,128]{3,2,1,0:T(8,128)S(1)} %get-tuple-element.25), channel_id=1, source_target_pairs={{0,1},{1,0},{2,3},{3,2},{4,5},{5,4},{6,7},{7,6},{8,9},{9,8},{10,11... | collective-permute-start | bytes 442376 | tf_op jit(solution)/shard_map/ppermute | solution.py:737
  15.7 2.5 %collective-permute-start.5 = (f32[6,3,16,128]{3,2,1,0:T(8,128)S(1)}, f32[6,3,16,128]{3,2,1,0:T(8,128)S(1)}, u32[]{:S(2)}, u32[]{:S(2)}) collective-permute-start(f32[6,3,16,128]{3,2,1,0:T(8,128)S(1)} %get-tuple-element.26), channel_id=1, source_target_pairs={{0,3},{1,2},{2,1},{3,0},{4,7},{5,6},{6,5},{7,4},{8,11},{9,10},{10,... | collective-permute-start | bytes 442376 | tf_op jit(solution)/shard_map/ppermute | solution.py:736
  18.2 0.0 all-to-all-done.lines_ref
  18.2 1.7 %transform.1.rest_0_ = f32[8,64,128]{2,1,0:T(8,128)} custom-call(f32[8,64,128]{2,1,0:T(8,128)S(1)} %all-to-all-done.lines_ref, bf16[128,1024]{1,0:T(8,128)(2,1)S(1)} %copy-done.3, bf16[128,1024]{1,0:T(8,128)(2,1)S(1)} %copy-done.2, f32[24,256]{1,0:T(8,128)S(1)} %get-tuple-element.21.rest_0_), custom_call_target="tpu_custom_call" | custom-call | flops 1650000000 | bytes 5400000 | tf_op jit(solution)/shard_map/transform/pallas_call | solution.py:356
  19.9 3.5 %all-to-all-start.1 = ((f32[8,64,128]{2,1,0:T(8,128)}), f32[8,64,128]{2,1,0:T(8,128)S(1)}, u32[]{:S(2)}, u32[]{:S(2)}) async-start(f32[8,64,128]{2,1,0:T(8,128)} %transform.1.rest_0_), calls=%async_computation.1 | async-start | bytes 524288 | tf_op jit(solution)/shard_map/all_to_all | solution.py:755
  23.4 1.7 %collective-permute-start.8 = (f32[6,3,16,128]{3,2,1,0:T(8,128)S(1)}, f32[6,3,16,128]{3,2,1,0:T(8,128)S(1)}, u32[]{:S(2)}, u32[]{:S(2)}) collective-permute-start(f32[6,3,16,128]{3,2,1,0:T(8,128)S(1)} %get-tuple-element.32), channel_id=1, source_target_pairs={{0,4},{4,8},{8,12},{12,16},{16,20},{20,24},{24,28},{28,0},{1,5},{5... | collective-permute-start | bytes 442376 | tf_op jit(solution)/shard_map/ppermute | solution.py:727
  25.2 0.0 collective-permute-done.2.left_ref
  25.2 4.0 %collective-permute-start.9 = (f32[6,3,16,128]{3,2,1,0:T(8,128)S(1)}, f32[6,3,16,128]{3,2,1,0:T(8,128)S(1)}, u32[]{:S(2)}, u32[]{:S(2)}) collective-permute-start(f32[6,3,16,128]{3,2,1,0:T(8,128)S(1)} %get-tuple-element.33), channel_id=1, source_target_pairs={{0,28},{4,0},{8,4},{12,8},{16,12},{20,16},{24,20},{28,24},{1,29},{... | collective-permute-start | bytes 442376 | tf_op jit(solution)/shard_map/ppermute | solution.py:728
  29.2 0.0 collective-permute-done.3.right_ref
  29.2 2.8 %advect_stream.1.base_ref = f32[6,16,16,128]{3,2,1,0:T(8,128)S(1)} custom-call(f32[6,16,16,128]{3,2,1,0:T(8,128)S(1)} %copy-done, f32[3,16,16,128]{3,2,1,0:T(8,128)S(1)} %copy-done.1, f32[24,256]{1,0:T(8,128)S(1)} %collective-permute-done.2.left_ref, f32[24,256]{1,0:T(8,128)S(1)} %collective-permute-done.3.right_ref, f32[8,64,128]{2,1,0:T(8,128)} %transform.1.rest_0_), custom_call_target="tpu_custom_call" | custom-call | flops 2750000128 | bytes 9000000 | tf_op jit(solution)/shard_map/advect_stream/pallas_call | solution.py:708
  32.0 0.0 all-to-all-done.1.own_ref.rest_0_
  32.1 0.5 collective-permute-start
  32.5 0.0 collective-permute-done.4.first_ref
  32.5 4.0 %collective-permute-start.1 = (f32[144,128]{1,0:T(8,128)S(1)}, f32[144,128]{1,0:T(8,128)S(1)}, u32[]{:S(2)}, u32[]{:S(2)}) collective-permute-start(f32[144,128]{1,0:T(8,128)S(1)} %get-tuple-element.23), channel_id=1, source_target_pairs={{0,28},{4,0},{8,4},{12,8},{16,12},{20,16},{24,20},{28,24},{1,29},{... | collective-permute-start | bytes 221192 | tf_op jit(solution)/shard_map/ppermute | solution.py:728
  36.6 0.0 collective-permute-done.5.second_ref
  36.6 2.1 %advect_span.1.after_ref.base_ref = f32[6,16,16,128]{3,2,1,0:T(8,128)S(1)} custom-call(f32[16,128]{1,0:T(8,128)S(1)} %iota.13.place_ref, f32[6,16,16,128]{3,2,1,0:T(8,128)S(1)} %copy-done, f32[3,16,16,128]{3,2,1,0:T(8,128)S(1)} %copy-done.1, f32[6,16,16,128]{3,2,1,0:T(8,128)S(1)} %advect_stream.1.base_ref, ...), custom_call_target="tpu_custom_call" | custom-call | flops 2750000128 | bytes 9000000 | tf_op jit(solution)/shard_map/advect_span/pallas_call | solution.py:708
  38.6 0.0 collective-permute-done.1.high_ref
  38.7 0.1 radial_assembly.1
  38.7 3.1 %collective-permute-start.6 = (f32[26,8,128]{2,1,0:T(8,128)S(1)}, f32[26,8,128]{2,1,0:T(8,128)S(1)}, u32[]{:S(2)}, u32[]{:S(2)}) collective-permute-start(f32[26,8,128]{2,1,0:T(8,128)S(1)} %get-tuple-element.28), channel_id=1, source_target_pairs={{0,3},{1,2},{2,1},{3,0},{4,7},{5,6},{6,5},{7,4},{8,11},{9,10},{10,... | collective-permute-start | bytes 319496 | tf_op jit(solution)/shard_map/ppermute | solution.py:736
  41.9 0.0 collective-permute-done.8.low_ref
  41.9 0.0 collective-permute-done.9.high_ref
  41.9 0.0 copy-start.4
  41.9 3.0 %advect_radial.1.rest_0_ = f32[6,16,16,128]{3,2,1,0:T(8,128)S(1)} custom-call(f32[16,128]{1,0:T(8,128)S(1)} %iota.13.place_ref, f32[6,16,16,128]{3,2,1,0:T(8,128)S(1)} %copy-done, f32[3,16,16,128]{3,2,1,0:T(8,128)S(1)} %copy-done.1, f32[6,16,16,128]{3,2,1,0:T(8,128)S(1)} %advect_span.1.after_ref.base_ref, ...), custom_call_target="tpu_custom_call" | custom-call | flops 2750000128 | bytes 9000000 | tf_op jit(solution)/shard_map/advect_radial/pallas_call | solution.py:708
  44.9 0.5 %collective-permute-done.6.second_ref = f32[26,8,128]{2,1,0:T(8,128)S(1)} collective-permute-done((f32[26,8,128]{2,1,0:T(8,128)S(1)}, f32[26,8,128]{2,1,0:T(8,128)S(1)}, u32[]{:S(2)}, u32[]{:S(2)}) %collective-permute-start.6) | collective-permute-done | bytes 106528 | tf_op jit(solution)/shard_map/ppermute | solution.py:736
  45.4 0.0 collective-permute-done.7.first_ref
  45.4 1.2 %relaxation.1 = (f32[16,16,128]{2,1,0:T(8,128)}, f32[6,16,16,128]{3,2,1,0:T(8,128)}) custom-call(f32[16,128]{1,0:T(8,128)S(1)} %iota.13.place_ref, f32[8,16,128]{2,1,0:T(8,128)S(1)} %copy-done.4, f32[26,24,128]{2,1,0:T(8,128)S(1)} %get-tuple-element.27.rest_0_.rows_ref, f32[26,8,128]{2,1,0:T(8,128)S(1)} %collective-permute-done.6.second_ref, ...), custom_call_target="tpu_custom_call" | custom-call | flops 1980000000 | bytes 6480000 | tf_op jit(solution)/shard_map/relaxation/pallas_call | solution.py:537
  (13 shorter events, 0.0 us)
Async XLA Ops:
  0.6 9.4 %copy-start = (f32[6,16,16,128]{3,2,1,0:T(8,128)S(1)}, f32[6,16,16,128]{3,2,1,0:T(8,128)}, u32[]{:S(2)}) copy-start(f32[6,16,16,128]{3,2,1,0:T(8,128)} %psi_ref.6) | copy-start | bytes 2359300
  4.0 14.1 %all-to-all-start = ((f32[8,64,128]{2,1,0:T(8,128)}), f32[8,64,128]{2,1,0:T(8,128)S(1)}, u32[]{:S(2)}, u32[]{:S(2)}) async-start(f32[8,64,128]{2,1,0:T(8,128)} %local_source.1), calls=%async_computation | async-start | bytes 524288 | tf_op jit(solution)/shard_map/all_to_all | solution.py:750
  10.0 8.2 %copy-start.2 = (bf16[128,1024]{1,0:T(8,128)(2,1)S(1)}, bf16[128,1024]{1,0:T(8,128)(2,1)}, u32[]{:S(2)}) copy-start(bf16[128,1024]{1,0:T(8,128)(2,1)} %constant.49.clone.low_ref) | copy-start | bytes 786436
  10.0 8.2 %copy-start.3 = (bf16[128,1024]{1,0:T(8,128)(2,1)S(1)}, bf16[128,1024]{1,0:T(8,128)(2,1)}, u32[]{:S(2)}) copy-start(bf16[128,1024]{1,0:T(8,128)(2,1)} %constant.48.clone.high_ref) | copy-start | bytes 786436
  10.5 14.7 %collective-permute-start.2 = (f32[24,256]{1,0:T(8,128)S(1)}, f32[24,256]{1,0:T(8,128)S(1)}, u32[]{:S(2)}, u32[]{:S(2)}) collective-permute-start(f32[24,256]{1,0:T(8,128)S(1)} %get-tuple-element.24), channel_id=1, source_target_pairs={{0,32},{32,64},{64,96},{96,128},{128,160},{160,192},{192,224},{224... | collective-permute-start | bytes 73736 | tf_op jit(solution)/shard_map/ppermute | solution.py:727
  11.9 17.2 %collective-permute-start.3 = (f32[24,256]{1,0:T(8,128)S(1)}, f32[24,256]{1,0:T(8,128)S(1)}, u32[]{:S(2)}, u32[]{:S(2)}) collective-permute-start(f32[24,256]{1,0:T(8,128)S(1)} %get-tuple-element.21.rest_0_), channel_id=1, source_target_pairs={{0,224},{32,0},{64,32},{96,64},{128,96},{160,128},{192,160},{224,1... | collective-permute-start | bytes 73736 | tf_op jit(solution)/shard_map/ppermute | solution.py:728
  14.2 18.4 %collective-permute-start.4 = (f32[6,3,16,128]{3,2,1,0:T(8,128)S(1)}, f32[6,3,16,128]{3,2,1,0:T(8,128)S(1)}, u32[]{:S(2)}, u32[]{:S(2)}) collective-permute-start(f32[6,3,16,128]{3,2,1,0:T(8,128)S(1)} %get-tuple-element.25), channel_id=1, source_target_pairs={{0,1},{1,0},{2,3},{3,2},{4,5},{5,4},{6,7},{7,6},{8,9},{9,8},{10,11... | collective-permute-start | bytes 442376 | tf_op jit(solution)/shard_map/ppermute | solution.py:737
  15.7 20.9 %collective-permute-start.5 = (f32[6,3,16,128]{3,2,1,0:T(8,128)S(1)}, f32[6,3,16,128]{3,2,1,0:T(8,128)S(1)}, u32[]{:S(2)}, u32[]{:S(2)}) collective-permute-start(f32[6,3,16,128]{3,2,1,0:T(8,128)S(1)} %get-tuple-element.26), channel_id=1, source_target_pairs={{0,3},{1,2},{2,1},{3,0},{4,7},{5,6},{6,5},{7,4},{8,11},{9,10},{10,... | collective-permute-start | bytes 442376 | tf_op jit(solution)/shard_map/ppermute | solution.py:736
  19.9 9.3 %copy-start.1 = (f32[3,16,16,128]{3,2,1,0:T(8,128)S(1)}, f32[3,16,16,128]{3,2,1,0:T(8,128)}, u32[]{:S(2)}) copy-start(f32[3,16,16,128]{3,2,1,0:T(8,128)} %velocity_ref.5) | copy-start | bytes 1179652
  19.9 12.2 %all-to-all-start.1 = ((f32[8,64,128]{2,1,0:T(8,128)}), f32[8,64,128]{2,1,0:T(8,128)S(1)}, u32[]{:S(2)}, u32[]{:S(2)}) async-start(f32[8,64,128]{2,1,0:T(8,128)} %transform.1.rest_0_), calls=%async_computation.1 | async-start | bytes 524288 | tf_op jit(solution)/shard_map/all_to_all | solution.py:755
  23.4 18.4 %collective-permute-start.8 = (f32[6,3,16,128]{3,2,1,0:T(8,128)S(1)}, f32[6,3,16,128]{3,2,1,0:T(8,128)S(1)}, u32[]{:S(2)}, u32[]{:S(2)}) collective-permute-start(f32[6,3,16,128]{3,2,1,0:T(8,128)S(1)} %get-tuple-element.32), channel_id=1, source_target_pairs={{0,4},{4,8},{8,12},{12,16},{16,20},{20,24},{24,28},{28,0},{1,5},{5... | collective-permute-start | bytes 442376 | tf_op jit(solution)/shard_map/ppermute | solution.py:727
  25.2 16.7 %collective-permute-start.9 = (f32[6,3,16,128]{3,2,1,0:T(8,128)S(1)}, f32[6,3,16,128]{3,2,1,0:T(8,128)S(1)}, u32[]{:S(2)}, u32[]{:S(2)}) collective-permute-start(f32[6,3,16,128]{3,2,1,0:T(8,128)S(1)} %get-tuple-element.33), channel_id=1, source_target_pairs={{0,28},{4,0},{8,4},{12,8},{16,12},{20,16},{24,20},{28,24},{1,29},{... | collective-permute-start | bytes 442376 | tf_op jit(solution)/shard_map/ppermute | solution.py:728
  32.1 6.6 %collective-permute-start = (f32[144,128]{1,0:T(8,128)S(1)}, f32[144,128]{1,0:T(8,128)S(1)}, u32[]{:S(2)}, u32[]{:S(2)}) collective-permute-start(f32[144,128]{1,0:T(8,128)S(1)} %get-tuple-element.22), channel_id=1, source_target_pairs={{0,4},{4,8},{8,12},{12,16},{16,20},{20,24},{24,28},{28,0},{1,5},{5... | collective-permute-start | bytes 221192 | tf_op jit(solution)/shard_map/ppermute | solution.py:727
  32.5 6.1 %collective-permute-start.1 = (f32[144,128]{1,0:T(8,128)S(1)}, f32[144,128]{1,0:T(8,128)S(1)}, u32[]{:S(2)}, u32[]{:S(2)}) collective-permute-start(f32[144,128]{1,0:T(8,128)S(1)} %get-tuple-element.23), channel_id=1, source_target_pairs={{0,28},{4,0},{8,4},{12,8},{16,12},{20,16},{24,20},{28,24},{1,29},{... | collective-permute-start | bytes 221192 | tf_op jit(solution)/shard_map/ppermute | solution.py:728
  38.7 6.7 %collective-permute-start.6 = (f32[26,8,128]{2,1,0:T(8,128)S(1)}, f32[26,8,128]{2,1,0:T(8,128)S(1)}, u32[]{:S(2)}, u32[]{:S(2)}) collective-permute-start(f32[26,8,128]{2,1,0:T(8,128)S(1)} %get-tuple-element.28), channel_id=1, source_target_pairs={{0,3},{1,2},{2,1},{3,0},{4,7},{5,6},{6,5},{7,4},{8,11},{9,10},{10,... | collective-permute-start | bytes 319496 | tf_op jit(solution)/shard_map/ppermute | solution.py:736
  41.9 3.5 %collective-permute-start.7 = (f32[26,8,128]{2,1,0:T(8,128)S(1)}, f32[26,8,128]{2,1,0:T(8,128)S(1)}, u32[]{:S(2)}, u32[]{:S(2)}) collective-permute-start(f32[26,8,128]{2,1,0:T(8,128)S(1)} %get-tuple-element.29), channel_id=1, source_target_pairs={{0,1},{1,0},{2,3},{3,2},{4,5},{5,4},{6,7},{7,6},{8,9},{9,8},{10,11... | collective-permute-start | bytes 319496 | tf_op jit(solution)/shard_map/ppermute | solution.py:737
  41.9 3.5 %copy-start.4 = (f32[8,16,128]{2,1,0:T(8,128)S(1)}, f32[8,16,128]{2,1,0:T(8,128)}, u32[]{:S(2)}) copy-start(f32[8,16,128]{2,1,0:T(8,128)} %constant.50.clone.modes_ref) | copy-start | bytes 196612

commit v6 on v5

--- a/solution.py
+++ b/solution.py
@@ -15,8 +15,10 @@
 BLOCK = 16
 PARTS = 8
 FULL = (6, BLOCK, BLOCK, LANES)
-LINES = 60
-ROWS = 64
+COLUMNS = 20
+SIDE_ROWS = 184
+LINES = 50
+ROWS = 56
 
 WEISSENBERG = 20.0
 EXTENSIBILITY = 100.0
@@ -168,7 +170,17 @@
     return (EXTENSIBILITY - 3.0) / (EXTENSIBILITY - (grown[0] + grown[3] + grown[5]))
 
 
-def source_kernel(psi_hbm, send_ref, psi_ref, stress, field, wrapped, sems):
+def segments(first, count):
+    at = 0
+    while at < count:
+        row, column = divmod(first + at, COLUMNS)
+        own = column < 18
+        some = min(count - at, (18 if own else COLUMNS) - column)
+        yield at, row * 24 + column + (0 if own else 4), some
+        at += some
+
+
+def source_kernel(psi_hbm, send_ref, psi_ref, stress, field, wrapped, packed, sems):
     chunk = BLOCK // SOURCE_CHUNKS
     arrivals = []
     for part in range(SOURCE_CHUNKS):
@@ -241,20 +253,22 @@
             emit(row, s11 + along(u12, -1) - along(u12, 1), u01, zero)
         else:
             emit(row, s11, zero, zero)
-    wrapped[480:488] = jnp.zeros((8, LANES), jnp.float32)
     pick = selection((8, 2 * LANES), ((0, 1, 126), (2, 3, -2)))
     pick = pick + selection((8, 2 * LANES), ((0, 1, 126 + LANES), (2, 3, LANES - 2)))
     for part in range(PARTS):
-        send_ref[part, 0:LINES] = field[part * LINES : part * LINES + LINES]
-        lines = jnp.concatenate(pieces(wrapped[part * LINES : part * LINES + ROWS], 2), axis=1)
-        lines = dot_nt(pick, lines)
-        send_ref[part, LINES:ROWS, 0:ROWS] = lines[0:4]
-        send_ref[part, LINES:ROWS, ROWS:LANES] = jnp.zeros((4, LANES - ROWS), jnp.float32)
-
-
-EXP_UNROLL = 2
+        send_ref[part, ROWS - 8 : ROWS] = jnp.zeros((8, LANES), jnp.float32)
+        packed[part, 48:64] = jnp.zeros((16, LANES), jnp.float32)
+        for at, line, count in segments(part * LINES, LINES):
+            send_ref[part, at : at + count] = field[line : line + count]
+            packed[part, at : at + count] = wrapped[line : line + count]
+    for part in range(PARTS):
+        lines = dot_nt(pick, jnp.concatenate(pieces(packed[part], 2), axis=1))
+        send_ref[part, LINES : LINES + 4, 0:64] = lines[0:4]
+
+
+EXP_UNROLL = 4
 SOURCE_CHUNKS = 4
-SOURCE_UNROLL = 8
+SOURCE_UNROLL = 16
 
 
 def local_source(psi):
@@ -268,7 +282,8 @@
             pltpu.VMEM(FULL, jnp.float32),
             pltpu.VMEM((6, 24, 24, LANES), jnp.float32),
             pltpu.VMEM((480, LANES), jnp.float32),
-            pltpu.VMEM((488, LANES), jnp.float32),
+            pltpu.VMEM((480, LANES), jnp.float32),
+            pltpu.VMEM((PARTS, 64, LANES), jnp.float32),
             pltpu.SemaphoreType.DMA((SOURCE_CHUNKS,)),
         ],
         compiler_params=params(SOURCE_VMEM),
@@ -313,15 +328,15 @@
 
 def transform_kernel(lines_ref, high_ref, low_ref, *rest):
     out_ref = rest[-1]
-    edges = jnp.concatenate([lines_ref[part, LINES:ROWS] for part in range(PARTS)], axis=0)
-    edges = jnp.concatenate(pieces(jnp.transpose(edges)[0:ROWS], 2), axis=1)
+    edges = jnp.concatenate([lines_ref[part, LINES : LINES + 4] for part in range(PARTS)], axis=0)
+    edges = jnp.concatenate(pieces(jnp.transpose(edges)[0:64], 2), axis=1)
     row = lax.broadcasted_iota(jnp.int32, (8 * PARTS, NX), 0) & (4 * PARTS - 1)
     lane = lax.broadcasted_iota(jnp.int32, (8 * PARTS, NX), 1)
     offset = jnp.where((row & 3) < 2, (row & 3) - 2, (row & 3) + LANES - 2)
     target = ((row >> 2) * LANES + offset + NX) & (NX - 1)
     target = jnp.where(lane == target, 1.0, 0.0).astype(jnp.bfloat16)
     beyond = jnp.dot(edges, target, preferred_element_type=jnp.float32)
-    f = [lines_ref[part] + beyond[:, part * LANES : (part + 1) * LANES] for part in range(PARTS)]
+    f = [lines_ref[part] + beyond[0:ROWS, part * LANES : (part + 1) * LANES] for part in range(PARTS)]
     s = [f[k] + f[k + 4] for k in range(4)]
     o = [f[k] - f[k + 4] for k in range(4)]
     half = math.sqrt(0.5)
@@ -365,17 +380,13 @@
 
 
 def radial_message_kernel(own_ref, up_ref, down_ref):
-    def copy(to, at, line, count):
-        while count:
-            part, row = divmod(line, LINES)
-            some = min(count, LINES - row)
+    for to, line in ((down_ref, 0), (up_ref, 13 * COLUMNS)):
+        at = 0
+        while at < 140:
+            part, row = divmod(line + at, LINES)
+            some = min(140 - at, LINES - row)
             to[at : at + some] = own_ref[part, row : row + some]
-            at, line, count = at + some, line + some, count - some
-
-    for k in range(7):
-        for to, row in ((down_ref, k), (up_ref, k + 13)):
-            copy(to, k * 20, row * 24, 18)
-            copy(to, k * 20 + 18, row * 24 + 22, 2)
+            at += some
     for to in (down_ref, up_ref):
         to[140:144] = jnp.zeros((4, LANES), jnp.float32)
 
@@ -393,8 +404,10 @@
 
 
 def radial_kernel(place_ref, own_ref, low_ref, high_ref, after_ref, out_ref, first_ref, second_ref, flat, flat_low, flat_high):
+    flat[...] = jnp.zeros_like(flat)
     for part in range(PARTS):
-        flat[part * LINES : part * LINES + LINES] = own_ref[part, 0:LINES]
+        for at, line, count in segments(part * LINES, LINES):
+            flat[line : line + count] = own_ref[part, at : at + count]
     flat_low[...] = jnp.zeros_like(flat_low)
     flat_high[...] = jnp.zeros_like(flat_high)
     for k in range(7):
@@ -414,6 +427,8 @@
     def high(row):
         return jnp.where(has_high, flat_high[row * 24 : row * 24 + 24], 0.0)
 
+    for to in (first_ref, second_ref):
+        to[SIDE_ROWS - 8 : SIDE_ROWS] = jnp.zeros((8, LANES), jnp.float32)
     for row in range(26):
         if row < 3:
             value = low(row + 13)
@@ -432,8 +447,9 @@
         out_ref[row] = value
         up = pltpu.roll(value, 24 - 11, 0)[0:8]
         down = pltpu.roll(value, 2, 0)[0:8]
-        first_ref[row] = jnp.where(even, up, down)
-        second_ref[row] = jnp.where(even, down, up)
+        at = slice(row * 7, row * 7 + 7)
+        first_ref[at] = jnp.where(even, up, down)[0:7]
+        second_ref[at] = jnp.where(even, down, up)[0:7]
 
 
 def radial_assembly(place, own, low, high, after):
@@ -442,8 +458,8 @@
         radial_kernel,
         out_shape=(
             shape((26, 24, LANES), jnp.float32),
-            shape((26, 8, LANES), jnp.float32),
-            shape((26, 8, LANES), jnp.float32),
+            shape((SIDE_ROWS, LANES), jnp.float32),
+            shape((SIDE_ROWS, LANES), jnp.float32),
         ),
         in_specs=[VMEM] * 4 + [ANY],
         out_specs=[VMEM] * 3,
@@ -484,7 +500,7 @@
     for row in range(26):
         own = rows_ref[row]
         tail = own[16:24]
-        first, other = first_ref[row], second_ref[row]
+        first, other = (ref[row * 7 : row * 7 + 8] for ref in (first_ref, second_ref))
         low = jnp.where(has_low, jnp.where(even_span, other, first), 0.0)
         high = jnp.where(has_high, jnp.where(even_span, first, other), 0.0)
         low = pltpu.roll(low, 3, 0)
@@ -492,7 +508,7 @@
         value = jnp.concatenate(
             [
                 jnp.where(sublane >= 6, tail, 0.0) + jnp.where(sublane >= 3, low, 0.0),
-                own[0:8] + jnp.where(sublane < 3, low, 0.0),
+                own[0:8] + jnp.where(sublane < 2, low, 0.0),
                 own[8:16] + jnp.where(sublane >= 6, high, 0.0),
                 jnp.where(sublane < 2, tail, 0.0) + jnp.where(sublane < 6, high, 0.0),
             ],
@@ -598,16 +614,16 @@
     spread = []
     for comp in range(6):
         ends = jnp.concatenate([right_ref[comp * 4 : comp * 4 + 4], left_ref[comp * 4 : comp * 4 + 4]], axis=0)
-        spread += pieces(ends, 3)
+        spread += pieces(ends, 2)
     spread = jnp.concatenate([v.astype(jnp.float32) for v in spread], axis=0)
     spread = jnp.transpose(spread).astype(jnp.bfloat16)
     place = selection((8, LANES), ((0, 2, 0), (4, 6, 121))).astype(jnp.float32)
     for comp in range(6):
-        rows = [place] * 3
+        rows = [place] * 2
         if comp > 0:
-            rows = [jnp.zeros((comp * 24, LANES), jnp.float32)] + rows
+            rows = [jnp.zeros((comp * 16, LANES), jnp.float32)] + rows
         if comp < 5:
-            rows = rows + [jnp.zeros((120 - comp * 24, LANES), jnp.float32)]
+            rows = rows + [jnp.zeros((80 - comp * 16, LANES), jnp.float32)]
         rows = jnp.concatenate(rows, axis=0).astype(jnp.bfloat16)
         found = jnp.dot(spread, rows, preferred_element_type=jnp.float32)
         ahead[comp] = found.reshape(BLOCK, BLOCK, LANES)

time: 46.9 us -> 45.6 us (0.972)
  waiting for transfers between devices: 0.58 us -> 0.03 us
  starting transfers between devices: 30.5 us -> 30 us
    ppermute x3, starting transfers between devices: 10.3 us -> 9.7 us  [exchange(): lax.ppermute(to_previous, axis, ring(axis, -1))]
    ppermute x2, waiting for transfers between devices: 0.55 us -> 0.01 us  [trade(): second = lax.ppermute(second, axis, outer)]
    ppermute x2, starting transfers between devices: 5.63 us -> 6.13 us  [trade(): second = lax.ppermute(second, axis, outer)]
  transfers between devices with their start and end apart: 12 -> 12, of which waited for: 1 -> 0; matrix products, arithmetic and copies ran while one was open for 0% -> 0% of each run, Pallas kernels for 22% -> 22%
where the time goes in v6:
time: 45.6 us; the launch traced here: 45.3 us
  starting transfers between devices  30 us (66%)
  Pallas kernels  14.3 us (31%)
  between operations  0.77 us (2%)
    ppermute x3, starting transfers between devices, exchange(): lax.ppermute(to_previous, axis, ring(axis, -1))  9.7 us
    pallas_call x3, Pallas kernels, advect(): pl.pallas_call(kernel, out_shape=jax.ShapeDtypeStruct(FULL, jnp.float32),...  7.76 us
    ppermute x2, starting transfers between devices, trade(): second = lax.ppermute(second, axis, outer)  6.13 us
    all_to_all x1, starting transfers between devices, shards(): lax.all_to_all(send, 'stream', split_axis=0, concat_axis=0, tiled=True)  5.87 us
    all_to_all x1, starting transfers between devices, shards(): lax.all_to_all(spectrum, 'stream', split_axis=0, concat_axis=0, tiled=True)  3.53 us
    ppermute x3, starting transfers between devices, exchange(): lax.ppermute(to_next, axis, ring(axis, 1))  3.27 us
    pallas_call x1, Pallas kernels, local_source(): pl.pallas_call(source_kernel, out_shape=shape((PARTS, ROWS, LANES), jnp.f...  3.23 us
    pallas_call x1, Pallas kernels, transform(): pl.pallas_call(transform_kernel, out_shape=jax.ShapeDtypeStruct((PARTS, R...  1.62 us
  transfers between devices with their start and end apart: 12, of which 0 were waited for; matrix products, arithmetic and copies ran while one was open for 0% of the time, Pallas kernels for 22%

profile of v6, /device:TPU:1, one launch (start us, length us, event | category | flops | bytes accessed | tf_op | source)
XLA Modules:
  0.0 45.3 jit_solution(1345811819353681347)
XLA Ops:
  0.6 3.2 %local_source.1 = f32[8,56,128]{2,1,0:T(8,128)} custom-call(f32[6,16,16,128]{3,2,1,0:T(8,128)} %psi_ref.6), custom_call_target="tpu_custom_call" | custom-call | flops 3300000000 | bytes 10800000 | tf_op jit(solution)/shard_map/local_source/pallas_call | solution.py:276
  3.9 5.9 %all-to-all-start = ((f32[8,56,128]{2,1,0:T(8,128)}), f32[8,56,128]{2,1,0:T(8,128)S(1)}, u32[]{:S(2)}, u32[]{:S(2)}) async-start(f32[8,56,128]{2,1,0:T(8,128)} %local_source.1), calls=%async_computation | async-start | bytes 458752 | tf_op jit(solution)/shard_map/all_to_all | solution.py:766
  9.8 0.1 iota.13.place_ref
  9.8 0.5 %messages.1 = (f32[24,256]{1,0:T(8,128)S(1)}, f32[24,256]{1,0:T(8,128)S(1)}, f32[6,3,16,128]{3,2,1,0:T(8,128)S(1)}, f32[6,3,16,128]{3,2,1,0:T(8,128)S(1)}, f32[6...) custom-call(f32[16,128]{1,0:T(8,128)S(1)} %iota.13.place_ref, f32[6,16,16,128]{3,2,1,0:T(8,128)S(1)} %copy-done), custom_call_target="tpu_custom_call" | custom-call | flops 4400000000 | bytes 14400000 | tf_op jit(solution)/shard_map/messages/pallas_call | solution.py:317
  10.3 1.5 %collective-permute-start.2 = (f32[24,256]{1,0:T(8,128)S(1)}, f32[24,256]{1,0:T(8,128)S(1)}, u32[]{:S(2)}, u32[]{:S(2)}) collective-permute-start(f32[24,256]{1,0:T(8,128)S(1)} %get-tuple-element.24), channel_id=1, source_target_pairs={{0,32},{32,64},{64,96},{96,128},{128,160},{160,192},{192,224},{224... | collective-permute-start | bytes 73736 | tf_op jit(solution)/shard_map/ppermute | solution.py:743
  11.8 2.2 %collective-permute-start.3 = (f32[24,256]{1,0:T(8,128)S(1)}, f32[24,256]{1,0:T(8,128)S(1)}, u32[]{:S(2)}, u32[]{:S(2)}) collective-permute-start(f32[24,256]{1,0:T(8,128)S(1)} %get-tuple-element.21.rest_0_), channel_id=1, source_target_pairs={{0,224},{32,0},{64,32},{96,64},{128,96},{160,128},{192,160},{224,1... | collective-permute-start | bytes 73736 | tf_op jit(solution)/shard_map/ppermute | solution.py:744
  14.0 1.5 %collective-permute-start.4 = (f32[6,3,16,128]{3,2,1,0:T(8,128)S(1)}, f32[6,3,16,128]{3,2,1,0:T(8,128)S(1)}, u32[]{:S(2)}, u32[]{:S(2)}) collective-permute-start(f32[6,3,16,128]{3,2,1,0:T(8,128)S(1)} %get-tuple-element.25), channel_id=1, source_target_pairs={{0,1},{1,0},{2,3},{3,2},{4,5},{5,4},{6,7},{7,6},{8,9},{9,8},{10,11... | collective-permute-start | bytes 442376 | tf_op jit(solution)/shard_map/ppermute | solution.py:753
  15.5 2.5 %collective-permute-start.5 = (f32[6,3,16,128]{3,2,1,0:T(8,128)S(1)}, f32[6,3,16,128]{3,2,1,0:T(8,128)S(1)}, u32[]{:S(2)}, u32[]{:S(2)}) collective-permute-start(f32[6,3,16,128]{3,2,1,0:T(8,128)S(1)} %get-tuple-element.26), channel_id=1, source_target_pairs={{0,3},{1,2},{2,1},{3,0},{4,7},{5,6},{6,5},{7,4},{8,11},{9,10},{10,... | collective-permute-start | bytes 442376 | tf_op jit(solution)/shard_map/ppermute | solution.py:752
  18.0 0.0 all-to-all-done.lines_ref
  18.0 1.6 %transform.1.rest_0_ = f32[8,56,128]{2,1,0:T(8,128)} custom-call(f32[8,56,128]{2,1,0:T(8,128)S(1)} %all-to-all-done.lines_ref, bf16[128,1024]{1,0:T(8,128)(2,1)S(1)} %copy-done.3, bf16[128,1024]{1,0:T(8,128)(2,1)S(1)} %copy-done.2, f32[24,256]{1,0:T(8,128)S(1)} %get-tuple-element.21.rest_0_), custom_call_target="tpu_custom_call" | custom-call | flops 1650000000 | bytes 5400000 | tf_op jit(solution)/shard_map/transform/pallas_call | solution.py:371
  19.6 3.5 %all-to-all-start.1 = ((f32[8,56,128]{2,1,0:T(8,128)}), f32[8,56,128]{2,1,0:T(8,128)S(1)}, u32[]{:S(2)}, u32[]{:S(2)}) async-start(f32[8,56,128]{2,1,0:T(8,128)} %transform.1.rest_0_), calls=%async_computation.1 | async-start | bytes 458752 | tf_op jit(solution)/shard_map/all_to_all | solution.py:771
  23.2 1.7 %collective-permute-start.8 = (f32[6,3,16,128]{3,2,1,0:T(8,128)S(1)}, f32[6,3,16,128]{3,2,1,0:T(8,128)S(1)}, u32[]{:S(2)}, u32[]{:S(2)}) collective-permute-start(f32[6,3,16,128]{3,2,1,0:T(8,128)S(1)} %get-tuple-element.32), channel_id=1, source_target_pairs={{0,4},{4,8},{8,12},{12,16},{16,20},{20,24},{24,28},{28,0},{1,5},{5... | collective-permute-start | bytes 442376 | tf_op jit(solution)/shard_map/ppermute | solution.py:743
  24.9 0.0 collective-permute-done.2.left_ref
  24.9 4.0 %collective-permute-start.9 = (f32[6,3,16,128]{3,2,1,0:T(8,128)S(1)}, f32[6,3,16,128]{3,2,1,0:T(8,128)S(1)}, u32[]{:S(2)}, u32[]{:S(2)}) collective-permute-start(f32[6,3,16,128]{3,2,1,0:T(8,128)S(1)} %get-tuple-element.33), channel_id=1, source_target_pairs={{0,28},{4,0},{8,4},{12,8},{16,12},{20,16},{24,20},{28,24},{1,29},{... | collective-permute-start | bytes 442376 | tf_op jit(solution)/shard_map/ppermute | solution.py:744
  28.9 0.0 collective-permute-done.3.right_ref
  28.9 2.7 %advect_stream.1.base_ref = f32[6,16,16,128]{3,2,1,0:T(8,128)S(1)} custom-call(f32[6,16,16,128]{3,2,1,0:T(8,128)S(1)} %copy-done, f32[3,16,16,128]{3,2,1,0:T(8,128)S(1)} %copy-done.1, f32[24,256]{1,0:T(8,128)S(1)} %collective-permute-done.2.left_ref, f32[24,256]{1,0:T(8,128)S(1)} %collective-permute-done.3.right_ref, f32[8,56,128]{2,1,0:T(8,128)} %transform.1.rest_0_), custom_call_target="tpu_custom_call" | custom-call | flops 2750000128 | bytes 9000000 | tf_op jit(solution)/shard_map/advect_stream/pallas_call | solution.py:724
  31.7 0.0 all-to-all-done.1.own_ref.rest_0_
  31.7 0.1 collective-permute-start
  31.8 0.0 collective-permute-done.4.first_ref
  31.8 3.5 %collective-permute-start.1 = (f32[144,128]{1,0:T(8,128)S(1)}, f32[144,128]{1,0:T(8,128)S(1)}, u32[]{:S(2)}, u32[]{:S(2)}) collective-permute-start(f32[144,128]{1,0:T(8,128)S(1)} %get-tuple-element.23), channel_id=1, source_target_pairs={{0,28},{4,0},{8,4},{12,8},{16,12},{20,16},{24,20},{28,24},{1,29},{... | collective-permute-start | bytes 221192 | tf_op jit(solution)/shard_map/ppermute | solution.py:744
  35.3 0.0 collective-permute-done.5.second_ref
  35.3 2.1 %advect_span.1.after_ref.base_ref = f32[6,16,16,128]{3,2,1,0:T(8,128)S(1)} custom-call(f32[16,128]{1,0:T(8,128)S(1)} %iota.13.place_ref, f32[6,16,16,128]{3,2,1,0:T(8,128)S(1)} %copy-done, f32[3,16,16,128]{3,2,1,0:T(8,128)S(1)} %copy-done.1, f32[6,16,16,128]{3,2,1,0:T(8,128)S(1)} %advect_stream.1.base_ref, ...), custom_call_target="tpu_custom_call" | custom-call | flops 2750000128 | bytes 9000000 | tf_op jit(solution)/shard_map/advect_span/pallas_call | solution.py:724
  37.3 0.0 collective-permute-done.low_ref
  37.4 0.0 collective-permute-done.1.high_ref
  37.4 0.1 radial_assembly.1
  37.5 3.6 %collective-permute-start.6 = (f32[184,128]{1,0:T(8,128)S(1)}, f32[184,128]{1,0:T(8,128)S(1)}, u32[]{:S(2)}, u32[]{:S(2)}) collective-permute-start(f32[184,128]{1,0:T(8,128)S(1)} %get-tuple-element.28), channel_id=1, source_target_pairs={{0,3},{1,2},{2,1},{3,0},{4,7},{5,6},{6,5},{7,4},{8,11},{9,10},{10,... | collective-permute-start | bytes 282632 | tf_op jit(solution)/shard_map/ppermute | solution.py:752
  41.1 0.0 collective-permute-start.7
  41.1 0.0 collective-permute-done.8.low_ref
  41.1 0.0 collective-permute-done.9.high_ref
  41.1 0.0 copy-start.4
  41.1 3.0 %advect_radial.1.rest_0_ = f32[6,16,16,128]{3,2,1,0:T(8,128)S(1)} custom-call(f32[16,128]{1,0:T(8,128)S(1)} %iota.13.place_ref, f32[6,16,16,128]{3,2,1,0:T(8,128)S(1)} %copy-done, f32[3,16,16,128]{3,2,1,0:T(8,128)S(1)} %copy-done.1, f32[6,16,16,128]{3,2,1,0:T(8,128)S(1)} %advect_span.1.after_ref.base_ref, ...), custom_call_target="tpu_custom_call" | custom-call | flops 2750000128 | bytes 9000000 | tf_op jit(solution)/shard_map/advect_radial/pallas_call | solution.py:724
  44.1 1.2 %relaxation.1 = (f32[16,16,128]{2,1,0:T(8,128)}, f32[6,16,16,128]{3,2,1,0:T(8,128)}) custom-call(f32[16,128]{1,0:T(8,128)S(1)} %iota.13.place_ref, f32[8,16,128]{2,1,0:T(8,128)S(1)} %copy-done.4, f32[26,24,128]{2,1,0:T(8,128)S(1)} %get-tuple-element.27.rest_0_.rows_ref, f32[184,128]{1,0:T(8,128)S(1)} %collective-permute-done.6.second_ref, ...), custom_call_target="tpu_custom_call" | custom-call | flops 1980000000 | bytes 6480000 | tf_op jit(solution)/shard_map/relaxation/pallas_call | solution.py:553
  (13 shorter events, 0.0 us)
Async XLA Ops:
  0.6 9.2 %copy-start = (f32[6,16,16,128]{3,2,1,0:T(8,128)S(1)}, f32[6,16,16,128]{3,2,1,0:T(8,128)}, u32[]{:S(2)}) copy-start(f32[6,16,16,128]{3,2,1,0:T(8,128)} %psi_ref.6) | copy-start | bytes 2359300
  3.9 14.1 %all-to-all-start = ((f32[8,56,128]{2,1,0:T(8,128)}), f32[8,56,128]{2,1,0:T(8,128)S(1)}, u32[]{:S(2)}, u32[]{:S(2)}) async-start(f32[8,56,128]{2,1,0:T(8,128)} %local_source.1), calls=%async_computation | async-start | bytes 458752 | tf_op jit(solution)/shard_map/all_to_all | solution.py:766
  9.8 8.2 %copy-start.2 = (bf16[128,1024]{1,0:T(8,128)(2,1)S(1)}, bf16[128,1024]{1,0:T(8,128)(2,1)}, u32[]{:S(2)}) copy-start(bf16[128,1024]{1,0:T(8,128)(2,1)} %constant.49.clone.low_ref) | copy-start | bytes 786436
  9.8 8.2 %copy-start.3 = (bf16[128,1024]{1,0:T(8,128)(2,1)S(1)}, bf16[128,1024]{1,0:T(8,128)(2,1)}, u32[]{:S(2)}) copy-start(bf16[128,1024]{1,0:T(8,128)(2,1)} %constant.48.clone.high_ref) | copy-start | bytes 786436
  10.3 14.6 %collective-permute-start.2 = (f32[24,256]{1,0:T(8,128)S(1)}, f32[24,256]{1,0:T(8,128)S(1)}, u32[]{:S(2)}, u32[]{:S(2)}) collective-permute-start(f32[24,256]{1,0:T(8,128)S(1)} %get-tuple-element.24), channel_id=1, source_target_pairs={{0,32},{32,64},{64,96},{96,128},{128,160},{160,192},{192,224},{224... | collective-permute-start | bytes 73736 | tf_op jit(solution)/shard_map/ppermute | solution.py:743
  11.8 17.2 %collective-permute-start.3 = (f32[24,256]{1,0:T(8,128)S(1)}, f32[24,256]{1,0:T(8,128)S(1)}, u32[]{:S(2)}, u32[]{:S(2)}) collective-permute-start(f32[24,256]{1,0:T(8,128)S(1)} %get-tuple-element.21.rest_0_), channel_id=1, source_target_pairs={{0,224},{32,0},{64,32},{96,64},{128,96},{160,128},{192,160},{224,1... | collective-permute-start | bytes 73736 | tf_op jit(solution)/shard_map/ppermute | solution.py:744
  14.0 17.8 %collective-permute-start.4 = (f32[6,3,16,128]{3,2,1,0:T(8,128)S(1)}, f32[6,3,16,128]{3,2,1,0:T(8,128)S(1)}, u32[]{:S(2)}, u32[]{:S(2)}) collective-permute-start(f32[6,3,16,128]{3,2,1,0:T(8,128)S(1)} %get-tuple-element.25), channel_id=1, source_target_pairs={{0,1},{1,0},{2,3},{3,2},{4,5},{5,4},{6,7},{7,6},{8,9},{9,8},{10,11... | collective-permute-start | bytes 442376 | tf_op jit(solution)/shard_map/ppermute | solution.py:753
  15.5 19.8 %collective-permute-start.5 = (f32[6,3,16,128]{3,2,1,0:T(8,128)S(1)}, f32[6,3,16,128]{3,2,1,0:T(8,128)S(1)}, u32[]{:S(2)}, u32[]{:S(2)}) collective-permute-start(f32[6,3,16,128]{3,2,1,0:T(8,128)S(1)} %get-tuple-element.26), channel_id=1, source_target_pairs={{0,3},{1,2},{2,1},{3,0},{4,7},{5,6},{6,5},{7,4},{8,11},{9,10},{10,... | collective-permute-start | bytes 442376 | tf_op jit(solution)/shard_map/ppermute | solution.py:752
  19.6 9.3 %copy-start.1 = (f32[3,16,16,128]{3,2,1,0:T(8,128)S(1)}, f32[3,16,16,128]{3,2,1,0:T(8,128)}, u32[]{:S(2)}) copy-start(f32[3,16,16,128]{3,2,1,0:T(8,128)} %velocity_ref.5) | copy-start | bytes 1179652
  19.6 12.0 %all-to-all-start.1 = ((f32[8,56,128]{2,1,0:T(8,128)}), f32[8,56,128]{2,1,0:T(8,128)S(1)}, u32[]{:S(2)}, u32[]{:S(2)}) async-start(f32[8,56,128]{2,1,0:T(8,128)} %transform.1.rest_0_), calls=%async_computation.1 | async-start | bytes 458752 | tf_op jit(solution)/shard_map/all_to_all | solution.py:771
  23.2 17.9 %collective-permute-start.8 = (f32[6,3,16,128]{3,2,1,0:T(8,128)S(1)}, f32[6,3,16,128]{3,2,1,0:T(8,128)S(1)}, u32[]{:S(2)}, u32[]{:S(2)}) collective-permute-start(f32[6,3,16,128]{3,2,1,0:T(8,128)S(1)} %get-tuple-element.32), channel_id=1, source_target_pairs={{0,4},{4,8},{8,12},{12,16},{16,20},{20,24},{24,28},{28,0},{1,5},{5... | collective-permute-start | bytes 442376 | tf_op jit(solution)/shard_map/ppermute | solution.py:743
  24.9 16.2 %collective-permute-start.9 = (f32[6,3,16,128]{3,2,1,0:T(8,128)S(1)}, f32[6,3,16,128]{3,2,1,0:T(8,128)S(1)}, u32[]{:S(2)}, u32[]{:S(2)}) collective-permute-start(f32[6,3,16,128]{3,2,1,0:T(8,128)S(1)} %get-tuple-element.33), channel_id=1, source_target_pairs={{0,28},{4,0},{8,4},{12,8},{16,12},{20,16},{24,20},{28,24},{1,29},{... | collective-permute-start | bytes 442376 | tf_op jit(solution)/shard_map/ppermute | solution.py:744
  31.7 5.6 %collective-permute-start = (f32[144,128]{1,0:T(8,128)S(1)}, f32[144,128]{1,0:T(8,128)S(1)}, u32[]{:S(2)}, u32[]{:S(2)}) collective-permute-start(f32[144,128]{1,0:T(8,128)S(1)} %get-tuple-element.22), channel_id=1, source_target_pairs={{0,4},{4,8},{8,12},{12,16},{16,20},{20,24},{24,28},{28,0},{1,5},{5... | collective-permute-start | bytes 221192 | tf_op jit(solution)/shard_map/ppermute | solution.py:743
  31.8 5.5 %collective-permute-start.1 = (f32[144,128]{1,0:T(8,128)S(1)}, f32[144,128]{1,0:T(8,128)S(1)}, u32[]{:S(2)}, u32[]{:S(2)}) collective-permute-start(f32[144,128]{1,0:T(8,128)S(1)} %get-tuple-element.23), channel_id=1, source_target_pairs={{0,28},{4,0},{8,4},{12,8},{16,12},{20,16},{24,20},{28,24},{1,29},{... | collective-permute-start | bytes 221192 | tf_op jit(solution)/shard_map/ppermute | solution.py:744
  37.5 6.6 %collective-permute-start.6 = (f32[184,128]{1,0:T(8,128)S(1)}, f32[184,128]{1,0:T(8,128)S(1)}, u32[]{:S(2)}, u32[]{:S(2)}) collective-permute-start(f32[184,128]{1,0:T(8,128)S(1)} %get-tuple-element.28), channel_id=1, source_target_pairs={{0,3},{1,2},{2,1},{3,0},{4,7},{5,6},{6,5},{7,4},{8,11},{9,10},{10,... | collective-permute-start | bytes 282632 | tf_op jit(solution)/shard_map/ppermute | solution.py:752
  41.1 3.0 %collective-permute-start.7 = (f32[184,128]{1,0:T(8,128)S(1)}, f32[184,128]{1,0:T(8,128)S(1)}, u32[]{:S(2)}, u32[]{:S(2)}) collective-permute-start(f32[184,128]{1,0:T(8,128)S(1)} %get-tuple-element.29), channel_id=1, source_target_pairs={{0,1},{1,0},{2,3},{3,2},{4,5},{5,4},{6,7},{7,6},{8,9},{9,8},{10,11... | collective-permute-start | bytes 282632 | tf_op jit(solution)/shard_map/ppermute | solution.py:753
  41.1 3.0 %copy-start.4 = (f32[8,16,128]{2,1,0:T(8,128)S(1)}, f32[8,16,128]{2,1,0:T(8,128)}, u32[]{:S(2)}) copy-start(f32[8,16,128]{2,1,0:T(8,128)} %constant.50.clone.modes_ref) | copy-start | bytes 196612

commit v7 on v6

--- a/solution.py
+++ b/solution.py
@@ -295,11 +295,11 @@
 def message_kernel(place_ref, psi_ref, left_ref, right_ref, first_ref, second_ref, high_ref, low_ref):
     even = flag(place_ref, 4, BLOCK)
     ends = sum(
-        (selection((8, 3 * LANES), ((0, 2, k * LANES), (4, 6, k * LANES + 121))) for k in range(1, 3)),
-        selection((8, 3 * LANES), ((0, 2, 0), (4, 6, 121))),
+        (selection((8, 2 * LANES), ((0, 2, k * LANES), (4, 6, k * LANES + 121))) for k in range(1, 2)),
+        selection((8, 2 * LANES), ((0, 2, 0), (4, 6, 121))),
     )
     for comp in range(6):
-        lines = jnp.concatenate(pieces(psi_ref[comp].reshape(BLOCK * BLOCK, LANES), 3), axis=1)
+        lines = jnp.concatenate(pieces(psi_ref[comp].reshape(BLOCK * BLOCK, LANES), 2), axis=1)
         found = dot_nt(ends, lines)
         left_ref[comp * 4 : comp * 4 + 4] = found[0:4]
         right_ref[comp * 4 : comp * 4 + 4] = found[4:8]
@@ -646,7 +646,7 @@
             out_ref[comp, row] = psi - change
         return carry
 
-    lax.fori_loop(0, BLOCK, step, 0, unroll=STEP_UNROLL)
+    lax.fori_loop(0, BLOCK, step, 0, unroll=STREAM_UNROLL)
 
 
 def span_kernel(place_ref, psi_ref, velocity_ref, base_ref, first_ref, second_ref, *rest):
@@ -718,6 +718,7 @@
 
 
 STEP_UNROLL = 2
+STREAM_UNROLL = 8
 
 
 def advect(kernel, name, scratch, arrays, after):

time: 45.6 us -> 45.6 us (level)
  starting transfers between devices: 30 us -> 30.6 us
  Pallas kernels: 14.3 us -> 13.8 us
    pallas_call x3, Pallas kernels: 7.76 us -> 7.3 us  [advect(): pl.pallas_call(kernel, out_shape=jax.ShapeDtypeStruct(FULL, jnp.float32),...]
  transfers between devices with their start and end apart: 12 -> 12, of which waited for: 0 -> 0; matrix products, arithmetic and copies ran while one was open for 0% -> 0% of each run, Pallas kernels for 22% -> 21%
where the time goes in v7:
time: 45.6 us; the launch traced here: 45.3 us
  starting transfers between devices  30.6 us (67%)
  Pallas kernels  13.8 us (30%)
  between operations  0.77 us (2%)
    ppermute x3, starting transfers between devices, exchange(): lax.ppermute(to_previous, axis, ring(axis, -1))  10.2 us
    pallas_call x3, Pallas kernels, advect(): pl.pallas_call(kernel, out_shape=jax.ShapeDtypeStruct(FULL, jnp.float32),...  7.3 us
    ppermute x2, starting transfers between devices, trade(): second = lax.ppermute(second, axis, outer)  6.2 us
    all_to_all x1, starting transfers between devices, shards(): lax.all_to_all(send, 'stream', split_axis=0, concat_axis=0, tiled=True)  5.87 us
    all_to_all x1, starting transfers between devices, shards(): lax.all_to_all(spectrum, 'stream', split_axis=0, concat_axis=0, tiled=True)  3.53 us
    ppermute x3, starting transfers between devices, exchange(): lax.ppermute(to_next, axis, ring(axis, 1))  3.29 us
    pallas_call x1, Pallas kernels, local_source(): pl.pallas_call(source_kernel, out_shape=shape((PARTS, ROWS, LANES), jnp.f...  3.23 us
    pallas_call x1, Pallas kernels, transform(): pl.pallas_call(transform_kernel, out_shape=jax.ShapeDtypeStruct((PARTS, R...  1.62 us
  transfers between devices with their start and end apart: 12, of which 0 were waited for; matrix products, arithmetic and copies ran while one was open for 0% of the time, Pallas kernels for 21%

profile of v7, /device:TPU:1, one launch (start us, length us, event | category | flops | bytes accessed | tf_op | source)
XLA Modules:
  0.0 45.3 jit_solution(8486644182863618905)
XLA Ops:
  0.6 3.2 %local_source.1 = f32[8,56,128]{2,1,0:T(8,128)} custom-call(f32[6,16,16,128]{3,2,1,0:T(8,128)} %psi_ref.6), custom_call_target="tpu_custom_call" | custom-call | flops 3300000000 | bytes 10800000 | tf_op jit(solution)/shard_map/local_source/pallas_call | solution.py:276
  3.9 5.9 %all-to-all-start = ((f32[8,56,128]{2,1,0:T(8,128)}), f32[8,56,128]{2,1,0:T(8,128)S(1)}, u32[]{:S(2)}, u32[]{:S(2)}) async-start(f32[8,56,128]{2,1,0:T(8,128)} %local_source.1), calls=%async_computation | async-start | bytes 458752 | tf_op jit(solution)/shard_map/all_to_all | solution.py:767
  9.8 0.1 iota.13.place_ref
  9.8 0.4 messages.1
  10.2 1.5 %collective-permute-start.2 = (f32[24,256]{1,0:T(8,128)S(1)}, f32[24,256]{1,0:T(8,128)S(1)}, u32[]{:S(2)}, u32[]{:S(2)}) collective-permute-start(f32[24,256]{1,0:T(8,128)S(1)} %get-tuple-element.24), channel_id=1, source_target_pairs={{0,32},{32,64},{64,96},{96,128},{128,160},{160,192},{192,224},{224... | collective-permute-start | bytes 73736 | tf_op jit(solution)/shard_map/ppermute | solution.py:744
  11.7 2.2 %collective-permute-start.3 = (f32[24,256]{1,0:T(8,128)S(1)}, f32[24,256]{1,0:T(8,128)S(1)}, u32[]{:S(2)}, u32[]{:S(2)}) collective-permute-start(f32[24,256]{1,0:T(8,128)S(1)} %get-tuple-element.21.rest_0_), channel_id=1, source_target_pairs={{0,224},{32,0},{64,32},{96,64},{128,96},{160,128},{192,160},{224,1... | collective-permute-start | bytes 73736 | tf_op jit(solution)/shard_map/ppermute | solution.py:745
  13.9 1.5 %collective-permute-start.4 = (f32[6,3,16,128]{3,2,1,0:T(8,128)S(1)}, f32[6,3,16,128]{3,2,1,0:T(8,128)S(1)}, u32[]{:S(2)}, u32[]{:S(2)}) collective-permute-start(f32[6,3,16,128]{3,2,1,0:T(8,128)S(1)} %get-tuple-element.25), channel_id=1, source_target_pairs={{0,1},{1,0},{2,3},{3,2},{4,5},{5,4},{6,7},{7,6},{8,9},{9,8},{10,11... | collective-permute-start | bytes 442376 | tf_op jit(solution)/shard_map/ppermute | solution.py:754
  15.4 2.5 %collective-permute-start.5 = (f32[6,3,16,128]{3,2,1,0:T(8,128)S(1)}, f32[6,3,16,128]{3,2,1,0:T(8,128)S(1)}, u32[]{:S(2)}, u32[]{:S(2)}) collective-permute-start(f32[6,3,16,128]{3,2,1,0:T(8,128)S(1)} %get-tuple-element.26), channel_id=1, source_target_pairs={{0,3},{1,2},{2,1},{3,0},{4,7},{5,6},{6,5},{7,4},{8,11},{9,10},{10,... | collective-permute-start | bytes 442376 | tf_op jit(solution)/shard_map/ppermute | solution.py:753
  17.9 0.0 all-to-all-done.lines_ref
  18.0 1.6 %transform.1.rest_0_ = f32[8,56,128]{2,1,0:T(8,128)} custom-call(f32[8,56,128]{2,1,0:T(8,128)S(1)} %all-to-all-done.lines_ref, bf16[128,1024]{1,0:T(8,128)(2,1)S(1)} %copy-done.3, bf16[128,1024]{1,0:T(8,128)(2,1)S(1)} %copy-done.2, f32[24,256]{1,0:T(8,128)S(1)} %get-tuple-element.21.rest_0_), custom_call_target="tpu_custom_call" | custom-call | flops 1650000000 | bytes 5400000 | tf_op jit(solution)/shard_map/transform/pallas_call | solution.py:371
  19.6 3.5 %all-to-all-start.1 = ((f32[8,56,128]{2,1,0:T(8,128)}), f32[8,56,128]{2,1,0:T(8,128)S(1)}, u32[]{:S(2)}, u32[]{:S(2)}) async-start(f32[8,56,128]{2,1,0:T(8,128)} %transform.1.rest_0_), calls=%async_computation.1 | async-start | bytes 458752 | tf_op jit(solution)/shard_map/all_to_all | solution.py:772
  23.1 1.7 %collective-permute-start.8 = (f32[6,3,16,128]{3,2,1,0:T(8,128)S(1)}, f32[6,3,16,128]{3,2,1,0:T(8,128)S(1)}, u32[]{:S(2)}, u32[]{:S(2)}) collective-permute-start(f32[6,3,16,128]{3,2,1,0:T(8,128)S(1)} %get-tuple-element.32), channel_id=1, source_target_pairs={{0,4},{4,8},{8,12},{12,16},{16,20},{20,24},{24,28},{28,0},{1,5},{5... | collective-permute-start | bytes 442376 | tf_op jit(solution)/shard_map/ppermute | solution.py:744
  24.8 0.0 collective-permute-done.2.left_ref
  24.8 4.0 %collective-permute-start.9 = (f32[6,3,16,128]{3,2,1,0:T(8,128)S(1)}, f32[6,3,16,128]{3,2,1,0:T(8,128)S(1)}, u32[]{:S(2)}, u32[]{:S(2)}) collective-permute-start(f32[6,3,16,128]{3,2,1,0:T(8,128)S(1)} %get-tuple-element.33), channel_id=1, source_target_pairs={{0,28},{4,0},{8,4},{12,8},{16,12},{20,16},{24,20},{28,24},{1,29},{... | collective-permute-start | bytes 442376 | tf_op jit(solution)/shard_map/ppermute | solution.py:745
  28.9 0.0 collective-permute-done.3.right_ref
  28.9 2.3 %advect_stream.1.base_ref = f32[6,16,16,128]{3,2,1,0:T(8,128)S(1)} custom-call(f32[6,16,16,128]{3,2,1,0:T(8,128)S(1)} %copy-done, f32[3,16,16,128]{3,2,1,0:T(8,128)S(1)} %copy-done.1, f32[24,256]{1,0:T(8,128)S(1)} %collective-permute-done.2.left_ref, f32[24,256]{1,0:T(8,128)S(1)} %collective-permute-done.3.right_ref, f32[8,56,128]{2,1,0:T(8,128)} %transform.1.rest_0_), custom_call_target="tpu_custom_call" | custom-call | flops 2750000128 | bytes 9000000 | tf_op jit(solution)/shard_map/advect_stream/pallas_call | solution.py:725
  31.2 0.0 all-to-all-done.1.own_ref.rest_0_
  31.2 0.1 collective-permute-start
  31.3 3.9 %collective-permute-start.1 = (f32[144,128]{1,0:T(8,128)S(1)}, f32[144,128]{1,0:T(8,128)S(1)}, u32[]{:S(2)}, u32[]{:S(2)}) collective-permute-start(f32[144,128]{1,0:T(8,128)S(1)} %get-tuple-element.23), channel_id=1, source_target_pairs={{0,28},{4,0},{8,4},{12,8},{16,12},{20,16},{24,20},{28,24},{1,29},{... | collective-permute-start | bytes 221192 | tf_op jit(solution)/shard_map/ppermute | solution.py:745
  35.2 0.0 collective-permute-done.5.second_ref
  35.2 2.1 %advect_span.1.after_ref.base_ref = f32[6,16,16,128]{3,2,1,0:T(8,128)S(1)} custom-call(f32[16,128]{1,0:T(8,128)S(1)} %iota.13.place_ref, f32[6,16,16,128]{3,2,1,0:T(8,128)S(1)} %copy-done, f32[3,16,16,128]{3,2,1,0:T(8,128)S(1)} %copy-done.1, f32[6,16,16,128]{3,2,1,0:T(8,128)S(1)} %advect_stream.1.base_ref, ...), custom_call_target="tpu_custom_call" | custom-call | flops 2750000128 | bytes 9000000 | tf_op jit(solution)/shard_map/advect_span/pallas_call | solution.py:725
  37.3 0.0 collective-permute-done.low_ref
  37.3 0.0 collective-permute-done.1.high_ref
  37.3 0.1 radial_assembly.1
  37.4 3.7 %collective-permute-start.6 = (f32[184,128]{1,0:T(8,128)S(1)}, f32[184,128]{1,0:T(8,128)S(1)}, u32[]{:S(2)}, u32[]{:S(2)}) collective-permute-start(f32[184,128]{1,0:T(8,128)S(1)} %get-tuple-element.28), channel_id=1, source_target_pairs={{0,3},{1,2},{2,1},{3,0},{4,7},{5,6},{6,5},{7,4},{8,11},{9,10},{10,... | collective-permute-start | bytes 282632 | tf_op jit(solution)/shard_map/ppermute | solution.py:753
  41.1 0.0 collective-permute-start.7
  41.1 0.0 collective-permute-done.8.low_ref
  41.1 0.0 collective-permute-done.9.high_ref
  41.1 0.0 copy-start.4
  41.1 3.0 %advect_radial.1.rest_0_ = f32[6,16,16,128]{3,2,1,0:T(8,128)S(1)} custom-call(f32[16,128]{1,0:T(8,128)S(1)} %iota.13.place_ref, f32[6,16,16,128]{3,2,1,0:T(8,128)S(1)} %copy-done, f32[3,16,16,128]{3,2,1,0:T(8,128)S(1)} %copy-done.1, f32[6,16,16,128]{3,2,1,0:T(8,128)S(1)} %advect_span.1.after_ref.base_ref, ...), custom_call_target="tpu_custom_call" | custom-call | flops 2750000128 | bytes 9000000 | tf_op jit(solution)/shard_map/advect_radial/pallas_call | solution.py:725
  44.1 0.0 collective-permute-done.7.first_ref
  44.1 1.2 %relaxation.1 = (f32[16,16,128]{2,1,0:T(8,128)}, f32[6,16,16,128]{3,2,1,0:T(8,128)}) custom-call(f32[16,128]{1,0:T(8,128)S(1)} %iota.13.place_ref, f32[8,16,128]{2,1,0:T(8,128)S(1)} %copy-done.4, f32[26,24,128]{2,1,0:T(8,128)S(1)} %get-tuple-element.27.rest_0_.rows_ref, f32[184,128]{1,0:T(8,128)S(1)} %collective-permute-done.6.second_ref, ...), custom_call_target="tpu_custom_call" | custom-call | flops 1980000000 | bytes 6480000 | tf_op jit(solution)/shard_map/relaxation/pallas_call | solution.py:553
  (13 shorter events, 0.0 us)
Async XLA Ops:
  0.6 9.2 %copy-start = (f32[6,16,16,128]{3,2,1,0:T(8,128)S(1)}, f32[6,16,16,128]{3,2,1,0:T(8,128)}, u32[]{:S(2)}) copy-start(f32[6,16,16,128]{3,2,1,0:T(8,128)} %psi_ref.6) | copy-start | bytes 2359300
  3.9 14.1 %all-to-all-start = ((f32[8,56,128]{2,1,0:T(8,128)}), f32[8,56,128]{2,1,0:T(8,128)S(1)}, u32[]{:S(2)}, u32[]{:S(2)}) async-start(f32[8,56,128]{2,1,0:T(8,128)} %local_source.1), calls=%async_computation | async-start | bytes 458752 | tf_op jit(solution)/shard_map/all_to_all | solution.py:767
  9.8 8.1 %copy-start.2 = (bf16[128,1024]{1,0:T(8,128)(2,1)S(1)}, bf16[128,1024]{1,0:T(8,128)(2,1)}, u32[]{:S(2)}) copy-start(bf16[128,1024]{1,0:T(8,128)(2,1)} %constant.49.clone.low_ref) | copy-start | bytes 786436
  9.8 8.1 %copy-start.3 = (bf16[128,1024]{1,0:T(8,128)(2,1)S(1)}, bf16[128,1024]{1,0:T(8,128)(2,1)}, u32[]{:S(2)}) copy-start(bf16[128,1024]{1,0:T(8,128)(2,1)} %constant.48.clone.high_ref) | copy-start | bytes 786436
  10.2 14.6 %collective-permute-start.2 = (f32[24,256]{1,0:T(8,128)S(1)}, f32[24,256]{1,0:T(8,128)S(1)}, u32[]{:S(2)}, u32[]{:S(2)}) collective-permute-start(f32[24,256]{1,0:T(8,128)S(1)} %get-tuple-element.24), channel_id=1, source_target_pairs={{0,32},{32,64},{64,96},{96,128},{128,160},{160,192},{192,224},{224... | collective-permute-start | bytes 73736 | tf_op jit(solution)/shard_map/ppermute | solution.py:744
  11.7 17.2 %collective-permute-start.3 = (f32[24,256]{1,0:T(8,128)S(1)}, f32[24,256]{1,0:T(8,128)S(1)}, u32[]{:S(2)}, u32[]{:S(2)}) collective-permute-start(f32[24,256]{1,0:T(8,128)S(1)} %get-tuple-element.21.rest_0_), channel_id=1, source_target_pairs={{0,224},{32,0},{64,32},{96,64},{128,96},{160,128},{192,160},{224,1... | collective-permute-start | bytes 73736 | tf_op jit(solution)/shard_map/ppermute | solution.py:745
  13.9 17.4 %collective-permute-start.4 = (f32[6,3,16,128]{3,2,1,0:T(8,128)S(1)}, f32[6,3,16,128]{3,2,1,0:T(8,128)S(1)}, u32[]{:S(2)}, u32[]{:S(2)}) collective-permute-start(f32[6,3,16,128]{3,2,1,0:T(8,128)S(1)} %get-tuple-element.25), channel_id=1, source_target_pairs={{0,1},{1,0},{2,3},{3,2},{4,5},{5,4},{6,7},{7,6},{8,9},{9,8},{10,11... | collective-permute-start | bytes 442376 | tf_op jit(solution)/shard_map/ppermute | solution.py:754
  15.4 19.8 %collective-permute-start.5 = (f32[6,3,16,128]{3,2,1,0:T(8,128)S(1)}, f32[6,3,16,128]{3,2,1,0:T(8,128)S(1)}, u32[]{:S(2)}, u32[]{:S(2)}) collective-permute-start(f32[6,3,16,128]{3,2,1,0:T(8,128)S(1)} %get-tuple-element.26), channel_id=1, source_target_pairs={{0,3},{1,2},{2,1},{3,0},{4,7},{5,6},{6,5},{7,4},{8,11},{9,10},{10,... | collective-permute-start | bytes 442376 | tf_op jit(solution)/shard_map/ppermute | solution.py:753
  19.6 9.3 %copy-start.1 = (f32[3,16,16,128]{3,2,1,0:T(8,128)S(1)}, f32[3,16,16,128]{3,2,1,0:T(8,128)}, u32[]{:S(2)}) copy-start(f32[3,16,16,128]{3,2,1,0:T(8,128)} %velocity_ref.5) | copy-start | bytes 1179652
  19.6 11.6 %all-to-all-start.1 = ((f32[8,56,128]{2,1,0:T(8,128)}), f32[8,56,128]{2,1,0:T(8,128)S(1)}, u32[]{:S(2)}, u32[]{:S(2)}) async-start(f32[8,56,128]{2,1,0:T(8,128)} %transform.1.rest_0_), calls=%async_computation.1 | async-start | bytes 458752 | tf_op jit(solution)/shard_map/all_to_all | solution.py:772
  23.1 18.0 %collective-permute-start.8 = (f32[6,3,16,128]{3,2,1,0:T(8,128)S(1)}, f32[6,3,16,128]{3,2,1,0:T(8,128)S(1)}, u32[]{:S(2)}, u32[]{:S(2)}) collective-permute-start(f32[6,3,16,128]{3,2,1,0:T(8,128)S(1)} %get-tuple-element.32), channel_id=1, source_target_pairs={{0,4},{4,8},{8,12},{12,16},{16,20},{20,24},{24,28},{28,0},{1,5},{5... | collective-permute-start | bytes 442376 | tf_op jit(solution)/shard_map/ppermute | solution.py:744
  24.8 16.3 %collective-permute-start.9 = (f32[6,3,16,128]{3,2,1,0:T(8,128)S(1)}, f32[6,3,16,128]{3,2,1,0:T(8,128)S(1)}, u32[]{:S(2)}, u32[]{:S(2)}) collective-permute-start(f32[6,3,16,128]{3,2,1,0:T(8,128)S(1)} %get-tuple-element.33), channel_id=1, source_target_pairs={{0,28},{4,0},{8,4},{12,8},{16,12},{20,16},{24,20},{28,24},{1,29},{... | collective-permute-start | bytes 442376 | tf_op jit(solution)/shard_map/ppermute | solution.py:745
  31.2 6.1 %collective-permute-start = (f32[144,128]{1,0:T(8,128)S(1)}, f32[144,128]{1,0:T(8,128)S(1)}, u32[]{:S(2)}, u32[]{:S(2)}) collective-permute-start(f32[144,128]{1,0:T(8,128)S(1)} %get-tuple-element.22), channel_id=1, source_target_pairs={{0,4},{4,8},{8,12},{12,16},{16,20},{20,24},{24,28},{28,0},{1,5},{5... | collective-permute-start | bytes 221192 | tf_op jit(solution)/shard_map/ppermute | solution.py:744
  31.3 6.0 %collective-permute-start.1 = (f32[144,128]{1,0:T(8,128)S(1)}, f32[144,128]{1,0:T(8,128)S(1)}, u32[]{:S(2)}, u32[]{:S(2)}) collective-permute-start(f32[144,128]{1,0:T(8,128)S(1)} %get-tuple-element.23), channel_id=1, source_target_pairs={{0,28},{4,0},{8,4},{12,8},{16,12},{20,16},{24,20},{28,24},{1,29},{... | collective-permute-start | bytes 221192 | tf_op jit(solution)/shard_map/ppermute | solution.py:745
  37.4 6.7 %collective-permute-start.6 = (f32[184,128]{1,0:T(8,128)S(1)}, f32[184,128]{1,0:T(8,128)S(1)}, u32[]{:S(2)}, u32[]{:S(2)}) collective-permute-start(f32[184,128]{1,0:T(8,128)S(1)} %get-tuple-element.28), channel_id=1, source_target_pairs={{0,3},{1,2},{2,1},{3,0},{4,7},{5,6},{6,5},{7,4},{8,11},{9,10},{10,... | collective-permute-start | bytes 282632 | tf_op jit(solution)/shard_map/ppermute | solution.py:753
  41.1 3.0 %collective-permute-start.7 = (f32[184,128]{1,0:T(8,128)S(1)}, f32[184,128]{1,0:T(8,128)S(1)}, u32[]{:S(2)}, u32[]{:S(2)}) collective-permute-start(f32[184,128]{1,0:T(8,128)S(1)} %get-tuple-element.29), channel_id=1, source_target_pairs={{0,1},{1,0},{2,3},{3,2},{4,5},{5,4},{6,7},{7,6},{8,9},{9,8},{10,11... | collective-permute-start | bytes 282632 | tf_op jit(solution)/shard_map/ppermute | solution.py:754
  41.1 3.0 %copy-start.4 = (f32[8,16,128]{2,1,0:T(8,128)S(1)}, f32[8,16,128]{2,1,0:T(8,128)}, u32[]{:S(2)}) copy-start(f32[8,16,128]{2,1,0:T(8,128)} %constant.50.clone.modes_ref) | copy-start | bytes 196612
